TPU v7x, 32 devices: a whole 2x2x4 slice. The times are simulated.
32 devices in a mesh: tensor: 4 (over y, core), dp: 8 (over z, x).
Axes of the slice: x: 2, y: 2, z: 4, core: 2. Of those that a mesh axis runs over, the one named last changes fastest.
Arguments:
- hidden: bfloat16 [8192, 1536], P('dp'), may hold values from -6 to 6
- segments: int32 [8192], P('dp'), may hold values from 0 to 31, never falling along the last dimension, each value on 1 to 512 neighbouring positions
- norm_gain: float32 [2, 1536], replicated, may hold values from 0.5 to 1.5
- w_z: bfloat16 [2, 1536, 3072], P(None, 'dp', 'tensor'), may hold values from -0.15625 to 0.15625
- w_x: bfloat16 [2, 1536, 3072], P(None, 'dp', 'tensor'), may hold values from -0.15625 to 0.15625
- w_bc: bfloat16 [2, 1536, 256], P(None, 'dp'), may hold values from -0.15625 to 0.15625
- w_dt: bfloat16 [2, 1536, 48], P(None, 'dp', 'tensor'), may hold values from -0.15625 to 0.15625
- conv_x_w: float32 [2, 4, 3072], P(None, None, 'tensor'), may hold values from -3 to 3
- conv_x_b: float32 [2, 3072], P(None, 'tensor'), may hold values from -3 to 3
- conv_bc_w: float32 [2, 4, 256], replicated, may hold values from -3 to 3
- conv_bc_b: float32 [2, 256], replicated, may hold values from -3 to 3
- dt_bias: float32 [2, 48], P(None, 'tensor'), may hold values from -6 to -2
- a_log: float32 [2, 48], P(None, 'tensor'), may hold values from 0 to 2.77
- d_skip: float32 [2, 48], P(None, 'tensor'), may hold values from 0.5 to 1.5
- gated_gain: float32 [2, 3072], P(None, 'tensor'), may hold values from 0.5 to 1.5
- w_out: bfloat16 [2, 1536, 3072], P(None, 'dp', 'tensor'), may hold values from -0.109375 to 0.109375
- cotangent: bfloat16 [8192, 1536], P('dp'), may hold values from -6 to 6
Outputs:
- mixed: bfloat16 [8192, 1536], P('dp')
- d_hidden: float32 [8192, 1536], P('dp')
- d_norm_gain: float32 [2, 1536], replicated
- d_w_z: float32 [2, 1536, 3072], P(None, 'dp', 'tensor')
- d_w_x: float32 [2, 1536, 3072], P(None, 'dp', 'tensor')
- d_w_bc: float32 [2, 1536, 256], P(None, 'dp', 'tensor')
- d_w_dt: float32 [2, 1536, 48], P(None, 'dp', 'tensor')
- d_conv_x_w: float32 [2, 4, 3072], P(None, None, 'tensor')
- d_conv_x_b: float32 [2, 3072], P(None, 'tensor')
- d_conv_bc_w: float32 [2, 4, 256], replicated
- d_conv_bc_b: float32 [2, 256], replicated
- d_dt_bias: float32 [2, 48], P(None, 'tensor')
- d_a_log: float32 [2, 48], P(None, 'tensor')
- d_d_skip: float32 [2, 48], P(None, 'tensor')
- d_gated_gain: float32 [2, 3072], P(None, 'tensor')
- d_w_out: float32 [2, 1536, 3072], P(None, 'dp', 'tensor')
Inputs may be any that keep to these rules, and one draw needn't show every extreme that they name: `segments`: segment numbers never fall along the tokens; a segment holds 1 to 512 tokens.
All inputs are finite; a program needn't handle non-finite values.
Results may differ from a plain program's by a relative error of at most 0.02.
Values may be sent and summed in bfloat16 or wider, within the bound.
No kernel may reach another device: no remote copies, remote signals or barrier semaphores. Data moves between devices by JAX's collectives and lax.ppermute only.
A program may use at most 256 MiB of HBM per device.

v0:
```python
from functools import partial

import jax
import jax.numpy as jnp
from jax import lax
from jax.sharding import PartitionSpec as P

HEAD_DIM = 64
STATE = 128
SCAN_BLOCK = 256
PACK = 1024
LAYERS = 2
INNER = 3072


EPSILON = 1e-05
PRECISE = lax.Precision.HIGHEST


def rms_scale(values, gain):
    return values * lax.rsqrt(jnp.mean(values * values, -1, keepdims=True) + EPSILON) * gain


def causal_conv(values, weight, bias_row, doc_ids):
    length = values.shape[0]
    summed = bias_row + weight[0] * values
    for offset in range(1, weight.shape[0]):
        moved_rows = jnp.concatenate(
            [jnp.zeros((offset, values.shape[1]), values.dtype), values[: length - offset]], 0
        )
        moved_doc = jnp.concatenate(
            [jnp.full((offset,), -1, jnp.int32), doc_ids[: length - offset]], 0
        )
        kept_mask = (moved_doc == doc_ids).astype(values.dtype)
        summed = summed + weight[offset] * moved_rows * kept_mask[:, None]
    return summed


def block_scan(heads_x, dt_vals, decay_rates, b_matrix, c_matrix, doc_ids):
    length, head_count, head_size = heads_x.shape
    blocks = length // SCAN_BLOCK
    state_size = b_matrix.shape[1]
    x_blocks = heads_x.reshape(blocks, SCAN_BLOCK, head_count, head_size)
    dt_blocks = dt_vals.reshape(blocks, SCAN_BLOCK, head_count)
    b_blocks = b_matrix.reshape(blocks, SCAN_BLOCK, state_size)
    c_blocks = c_matrix.reshape(blocks, SCAN_BLOCK, state_size)
    doc_blocks = doc_ids.reshape(blocks, SCAN_BLOCK)
    log_decay = jnp.cumsum(dt_blocks * decay_rates, 1)
    order_idx = jnp.arange(SCAN_BLOCK)
    visible = (doc_blocks[:, :, None] == doc_blocks[:, None, :]) & (
        order_idx[:, None] >= order_idx[None, :]
    )
    log_gap = log_decay[:, :, None, :] - log_decay[:, None, :, :]
    weights = jnp.exp(jnp.where(visible[..., None], log_gap, -10000.0))
    intersection = jnp.einsum("ctn,csn->cts", c_blocks, b_blocks, precision=PRECISE)
    inputs = x_blocks * dt_blocks[..., None]
    local_out = jnp.einsum(
        "ctsh,cshp->cthp", weights * intersection[..., None], inputs, precision=PRECISE
    )
    tail_log = log_decay[:, -1:, :]
    to_end = (
        jnp.exp(tail_log - log_decay)
        * (doc_blocks == doc_blocks[:, -1:]).astype(jnp.float32)[..., None]
    )
    block_states = jnp.einsum("cth,ctn,cthp->chpn", to_end, b_blocks, inputs, precision=PRECISE)
    through = jnp.exp(tail_log[:, 0, :])

    def advance(carried_in, pieces):
        state_now, last_doc = carried_in
        own_state, own_through, own_c, own_log, own_doc = pieces
        reach_mask = jnp.exp(own_log) * (own_doc == last_doc).astype(jnp.float32)[:, None]
        carried = (
            jnp.einsum("tn,hpn->thp", own_c, state_now, precision=PRECISE) * reach_mask[:, :, None]
        )
        kept_on = (own_doc[-1] == last_doc).astype(jnp.float32)
        new_state = state_now * (own_through * kept_on)[:, None, None] + own_state
        return ((new_state, own_doc[-1]), carried)

    scan_init = (
        jnp.zeros((head_count, head_size, state_size), jnp.float32),
        jnp.array(-1, jnp.int32),
    )
    _, carried_out = lax.scan(
        advance, scan_init, (block_states, through, c_blocks, log_decay, doc_blocks)
    )
    return (local_out + carried_out).reshape(length, head_count, head_size)


def mixer_core(
    doc_ids,
    x_pre,
    bc_pre,
    dt_pre,
    conv_xw,
    conv_xb,
    conv_bcw,
    conv_bcb,
    bias_dt,
    log_rate,
    skip_now,
):
    length = x_pre.shape[0]
    x_conv = jax.nn.silu(causal_conv(x_pre, conv_xw, conv_xb, doc_ids))
    bc_conv = jax.nn.silu(causal_conv(bc_pre, conv_bcw, conv_bcb, doc_ids))
    dt_vals = jax.nn.softplus(dt_pre + bias_dt)
    decay_rates = -jnp.exp(log_rate)
    heads_x = x_conv.reshape(length, bias_dt.shape[0], HEAD_DIM)
    scanned = block_scan(
        heads_x, dt_vals, decay_rates, bc_conv[:, :STATE], bc_conv[:, STATE:], doc_ids
    )
    return (scanned + skip_now[None, :, None] * heads_x).reshape(length, -1)


def add_rows(source, pieces):
    return tuple(
        (
            jnp.dot(source, weight_piece, preferred_element_type=jnp.float32)
            for weight_piece in pieces
        )
    )


def add_single(source, weight_piece):
    return jnp.dot(source, weight_piece, preferred_element_type=jnp.float32)


def project_rows(scaled, weight_piece):
    return lax.dot_general(
        scaled, weight_piece, (((1,), (1,)), ((), ())), preferred_element_type=jnp.float32
    )


def input_rows(grad_gate, grad_x, own_bc, grad_dt, offset, pieces):
    contract_dims = (((1,), (1,)), ((), ()))
    bc_piece = lax.dynamic_slice_in_dim(pieces[2], offset, own_bc.shape[1], 1)
    summed = lax.dot_general(
        grad_gate, pieces[0], contract_dims, preferred_element_type=jnp.float32
    )
    summed = summed + lax.dot_general(
        grad_x, pieces[1], contract_dims, preferred_element_type=jnp.float32
    )
    summed = summed + lax.dot_general(
        own_bc, bc_piece, contract_dims, preferred_element_type=jnp.float32
    )
    summed = summed + lax.dot_general(
        grad_dt, pieces[3], contract_dims, preferred_element_type=jnp.float32
    )
    return summed


def head_reduce(partial_rows):
    return lax.psum(partial_rows, "tensor")


def on_device(
    hidden,
    segments,
    norm_gain,
    w_z,
    w_x,
    w_bc,
    w_dt,
    conv_x_w,
    conv_x_b,
    conv_bc_w,
    conv_bc_b,
    dt_bias,
    a_log,
    d_skip,
    gated_gain,
    w_out,
    cotangent,
):
    length = hidden.shape[0]
    tensor_count = lax.axis_size("tensor")
    tensor_idx = lax.axis_index("tensor")
    position = jnp.arange(length, dtype=jnp.int32)
    previous = jnp.concatenate([jnp.full((1,), -1, jnp.int32), segments[:-1]], 0)
    starts = (position % PACK == 0) | (segments != previous)
    doc_ids = jnp.cumsum(starts.astype(jnp.int32))
    core_fn = partial(mixer_core, doc_ids)
    contract_rows = (((0,), (0,)), ((), ()))
    stream = hidden.astype(jnp.float32)
    kept_state = []
    for layer_idx in range(LAYERS):
        normed, norm_pull = jax.vjp(rms_scale, stream, norm_gain[layer_idx])
        normed_low = normed.astype(jnp.bfloat16)
        norm_keep = norm_pull
        projected = add_rows(
            normed_low,
            (
                lax.all_gather(w_z[layer_idx], "dp", axis=0, tiled=True),
                lax.all_gather(w_x[layer_idx], "dp", axis=0, tiled=True),
                lax.all_gather(w_bc[layer_idx], "dp", axis=0, tiled=True),
                lax.all_gather(w_dt[layer_idx], "dp", axis=0, tiled=True),
            ),
        )
        gate_pre, x_pre, bc_pre, dt_pre = projected
        mixer_out, core_pull = jax.vjp(
            core_fn,
            x_pre,
            bc_pre,
            dt_pre,
            conv_x_w[layer_idx],
            conv_x_b[layer_idx],
            conv_bc_w[layer_idx],
            conv_bc_b[layer_idx],
            dt_bias[layer_idx],
            a_log[layer_idx],
            d_skip[layer_idx],
        )
        gate_act = jax.nn.silu(gate_pre)
        gated = mixer_out * gate_act
        square_sum = lax.psum(jnp.sum(gated * gated, -1), "tensor")
        inv_rms = lax.rsqrt(square_sum / INNER + EPSILON)[:, None]
        normal = gated * inv_rms
        scaled = (normal * gated_gain[layer_idx]).astype(jnp.bfloat16)
        partial_out = project_rows(
            scaled, lax.all_gather(w_out[layer_idx], "dp", axis=0, tiled=True)
        )
        stream = stream + head_reduce(partial_out)
        kept_state.append(
            (
                normed_low,
                norm_keep,
                gate_pre,
                gate_act,
                mixer_out,
                core_pull,
                gated,
                inv_rms,
                normal,
                scaled,
            )
        )
    grad_stream = cotangent.astype(jnp.float32)
    weight_parts = [None] * LAYERS
    small_parts = [None] * LAYERS
    for layer_idx in reversed(range(LAYERS)):
        (
            normed_low,
            norm_keep,
            gate_pre,
            gate_act,
            mixer_out,
            core_pull,
            gated,
            inv_rms,
            normal,
            scaled,
        ) = kept_state[layer_idx]
        grad_low = grad_stream.astype(jnp.bfloat16)
        grad_scaled = add_single(
            grad_low, lax.all_gather(w_out[layer_idx], "dp", axis=0, tiled=True)
        )
        grad_out_w = lax.dot_general(
            grad_low, scaled, contract_rows, preferred_element_type=jnp.float32
        )
        grad_gated_gain = jnp.sum(grad_scaled * normal, 0)
        grad_normal = grad_scaled * gated_gain[layer_idx]
        cross_sum = lax.psum(jnp.sum(grad_normal * gated, -1), "tensor")
        grad_gated = (
            inv_rms * grad_normal
            - gated * (inv_rms * inv_rms * inv_rms) * (cross_sum / INNER)[:, None]
        )
        grad_mixer = grad_gated * gate_act
        sigmoid_gate = jax.nn.sigmoid(gate_pre)
        grad_gate = grad_gated * mixer_out * sigmoid_gate * (1.0 + gate_pre * (1.0 - sigmoid_gate))
        core_grads = core_pull(grad_mixer)
        grad_bc, grad_conv_bcw, grad_conv_bcb = (
            lax.psum(core_grads[1].astype(jnp.bfloat16), "tensor").astype(jnp.float32),
            lax.psum(core_grads[5].astype(jnp.bfloat16), "tensor").astype(jnp.float32),
            lax.psum(core_grads[6].astype(jnp.bfloat16), "tensor").astype(jnp.float32),
        )
        low_gate = grad_gate.astype(jnp.bfloat16)
        low_x = core_grads[0].astype(jnp.bfloat16)
        low_bc = grad_bc.astype(jnp.bfloat16)
        low_dt = core_grads[2].astype(jnp.bfloat16)
        shared_width = low_bc.shape[1] // tensor_count
        bc_offset = tensor_idx * shared_width
        own_bc = lax.dynamic_slice_in_dim(low_bc, bc_offset, shared_width, 1)
        grad_wz = lax.dot_general(
            normed_low, low_gate, contract_rows, preferred_element_type=jnp.float32
        )
        grad_wx = lax.dot_general(
            normed_low, low_x, contract_rows, preferred_element_type=jnp.float32
        )
        grad_wbc = lax.dot_general(
            normed_low, own_bc, contract_rows, preferred_element_type=jnp.float32
        )
        grad_wdt = lax.dot_general(
            normed_low, low_dt, contract_rows, preferred_element_type=jnp.float32
        )
        grad_input_part = input_rows(
            low_gate,
            low_x,
            own_bc,
            low_dt,
            bc_offset,
            lax.all_gather(
                (w_z[layer_idx], w_x[layer_idx], w_bc[layer_idx], w_dt[layer_idx]),
                "dp",
                axis=0,
                tiled=True,
            ),
        )
        grad_input = head_reduce(grad_input_part)
        grad_prev, grad_norm_gain = norm_keep(grad_input)
        grad_stream = grad_stream + grad_prev
        weight_parts[layer_idx] = (
            lax.psum_scatter(
                grad_wz.astype(jnp.bfloat16), "dp", scatter_dimension=0, tiled=True
            ).astype(jnp.float32),
            lax.psum_scatter(
                grad_wx.astype(jnp.bfloat16), "dp", scatter_dimension=0, tiled=True
            ).astype(jnp.float32),
            lax.psum_scatter(
                grad_wbc.astype(jnp.bfloat16), "dp", scatter_dimension=0, tiled=True
            ).astype(jnp.float32),
            lax.psum_scatter(
                grad_wdt.astype(jnp.bfloat16), "dp", scatter_dimension=0, tiled=True
            ).astype(jnp.float32),
            lax.psum_scatter(
                grad_out_w.astype(jnp.bfloat16), "dp", scatter_dimension=0, tiled=True
            ).astype(jnp.float32),
        )
        small_parts[layer_idx] = (
            grad_norm_gain,
            core_grads[3],
            core_grads[4],
            grad_conv_bcw,
            grad_conv_bcb,
            core_grads[7],
            core_grads[8],
            core_grads[9],
            grad_gated_gain,
        )
    stacked = [
        jnp.stack([small_parts[layer_idx][member] for layer_idx in range(LAYERS)])
        for member in range(9)
    ]
    mixed = stream.astype(jnp.bfloat16)
    summed_small = (
        lax.psum(stacked[0].astype(jnp.bfloat16), "dp").astype(jnp.float32),
        lax.psum(stacked[1].astype(jnp.bfloat16), "dp").astype(jnp.float32),
        lax.psum(stacked[2].astype(jnp.bfloat16), "dp").astype(jnp.float32),
        lax.psum(stacked[3].astype(jnp.bfloat16), "dp").astype(jnp.float32),
        lax.psum(stacked[4].astype(jnp.bfloat16), "dp").astype(jnp.float32),
        lax.psum(stacked[5].astype(jnp.bfloat16), "dp").astype(jnp.float32),
        lax.psum(stacked[6].astype(jnp.bfloat16), "dp").astype(jnp.float32),
        lax.psum(stacked[7].astype(jnp.bfloat16), "dp").astype(jnp.float32),
        lax.psum(stacked[8].astype(jnp.bfloat16), "dp").astype(jnp.float32),
    )
    weight_stacks = [
        jnp.stack([weight_parts[layer_idx][member] for layer_idx in range(LAYERS)])
        for member in range(5)
    ]
    return (
        mixed,
        grad_stream,
        summed_small[0],
        weight_stacks[0],
        weight_stacks[1],
        weight_stacks[2],
        weight_stacks[3],
        summed_small[1],
        summed_small[2],
        summed_small[3],
        summed_small[4],
        summed_small[5],
        summed_small[6],
        summed_small[7],
        summed_small[8],
        weight_stacks[4],
    )


def solution(mesh):
    in_specs = (
        P("dp", None),
        P("dp"),
        P(),
        P(None, "dp", "tensor"),
        P(None, "dp", "tensor"),
        P(None, "dp", None),
        P(None, "dp", "tensor"),
        P(None, None, "tensor"),
        P(None, "tensor"),
        P(),
        P(),
        P(None, "tensor"),
        P(None, "tensor"),
        P(None, "tensor"),
        P(None, "tensor"),
        P(None, "dp", "tensor"),
        P("dp", None),
    )
    out_specs = (
        P("dp", None),
        P("dp", None),
        P(),
        P(None, "dp", "tensor"),
        P(None, "dp", "tensor"),
        P(None, "dp", "tensor"),
        P(None, "dp", "tensor"),
        P(None, None, "tensor"),
        P(None, "tensor"),
        P(),
        P(),
        P(None, "tensor"),
        P(None, "tensor"),
        P(None, "tensor"),
        P(None, "tensor"),
        P(None, "dp", "tensor"),
    )
    return jax.shard_map(
        on_device, mesh=mesh, in_specs=in_specs, out_specs=out_specs, check_vma=False
    )
```

profile of v0, /device:TPU:0, one launch (start us, length us, event | category | flops | bytes accessed | tf_op | source)
XLA Modules:
  0.0 2063.1 jit_solution(9069154089228637264)
XLA Ops:
  22.0 35.9 %all-gather.2 = bf16[1,1536,256]{2,1,0:T(8,128)(2,1)S(1)} all-gather(bf16[1,192,256]{2,1,0:T(8,128)(2,1)S(1)} %get-tuple-element.1670), channel_id=4, replica_groups=mesh['tensor'=4,'dp'=8] {'dp'}, dimensions={1}, use_global_device_ids=true | all-gather | bytes 884736 | tf_op jit(solution)/shard_map/all_gather | solution.py:194
  67.4 35.2 %all-gather.1 = bf16[1,1536,12]{2,0,1:T(2,128)(2,1)} all-gather(bf16[1,192,12]{2,0,1:T(2,128)(2,1)} %copy.405), channel_id=3, replica_groups=mesh['tensor'=4,'dp'=8] {'dp'}, dimensions={1}, use_global_device_ids=true | all-gather | bytes 41472 | tf_op jit(solution)/shard_map/all_gather | solution.py:195
  181.6 62.1 %while.104 = (s32[]{:T(128)}, f32[12,64,128]{2,1,0:T(8,128)S(1)}, s32[]{:T(128)}, f32[4,256,12,64]{1,3,2,0:T(8,128)}, f32[4,256,12]{1,2,0:T(8,128)}, /*index=5*/...) while((s32[]{:T(128)}, f32[12,64,128]{2,1,0:T(8,128)S(1)}, ...), condition=%wide.region_6.8_spmd.clone, body=%wide.region_5.7_spmd.clone.sunk | while | flops 302684704 | bytes 4180403 | solution.py:83
  243.7 16.9 bitcast_add_fusion.5
  293.0 34.1 %all-gather.7 = bf16[1,1536,256]{2,1,0:T(8,128)(2,1)} all-gather(bf16[1,192,256]{2,1,0:T(8,128)(2,1)} %get-tuple-element.1669), channel_id=9, replica_groups=mesh['tensor'=4,'dp'=8] {'dp'}, dimensions={1}, use_global_device_ids=true | all-gather | bytes 884736 | tf_op jit(solution)/shard_map/all_gather | solution.py:194
  327.9 34.4 %all-gather.6 = bf16[1,1536,12]{2,0,1:T(2,128)(2,1)} all-gather(bf16[1,192,12]{2,0,1:T(2,128)(2,1)} %copy.406), channel_id=8, replica_groups=mesh['tensor'=4,'dp'=8] {'dp'}, dimensions={1}, use_global_device_ids=true | all-gather | bytes 41472 | tf_op jit(solution)/shard_map/all_gather | solution.py:195
  366.0 46.2 %all-reduce.57.cloned.1.call-done = f32[1024,1536]{1,0:T(8,128)} async-done(((f32[1024,1536]{1,0:T(8,128)}), f32[1024,1536]{1,0:T(8,128)}) %all-reduce.57.cloned.1.call-update) | async-done | bytes 6291472 | tf_op jit(solution)/shard_map/psum | solution.py:152
  445.5 21.1 %all-gather.23.cloned.1.call-done = bf16[1,1536,768]{2,1,0:T(8,128)(2,1)} async-done(((bf16[1,192,768]{2,1,0:T(8,128)(2,1)}), bf16[1,1536,768]{2,1,0:T(8,128)(2,1)}) %all-gather.23.cloned.1.call-update) | async-done | bytes 2359312 | tf_op jit(solution)/shard_map/all_gather | solution.py:193
  500.3 63.2 %while.105 = (s32[]{:T(128)}, f32[12,64,128]{2,1,0:T(8,128)S(1)}, s32[]{:T(128)}, f32[4,256,12,64]{1,3,2,0:T(8,128)}, f32[4,256,12]{1,2,0:T(8,128)}, /*index=5*/...) while((s32[]{:T(128)}, f32[12,64,128]{2,1,0:T(8,128)S(1)}, ...), condition=%wide.region_14.16_spmd.clone, body=%wide.region_13.15_spmd.clone.sunk | while | flops 302684704 | bytes 4180403 | solution.py:83
  566.7 16.5 bitcast_add_fusion.4
  638.7 49.7 %while.106 = (s32[]{:T(128)}, f32[12,64,128]{2,1,0:T(8,128)S(1)}, f32[4,12,64,128]{3,2,1,0:T(8,128)}, f32[4,12]{1,0:T(4,128)S(1)}, f32[4,256,128]{2,1,0:T(8,128)...) while((s32[]{:T(128)}, f32[12,64,128]{2,1,0:T(8,128)S(1)}, ...), condition=%wide.region_23.25_spmd.clone, body=%wide.region_20.24_spmd.clone.sunk | while | flops 605457408 | bytes 7848565 | solution.py:83
  701.5 18.2 fusion.71
  727.6 14.0 multiply_reduce_fusion.6
  765.4 9.9 reduce-window.45
  797.4 10.3 add_add_fusion.3
  807.8 117.8 %all-reduce.61.cloned.1.call-done = f32[1024,1536]{1,0:T(8,128)} async-done(((f32[1024,1536]{1,0:T(8,128)}), f32[1024,1536]{1,0:T(8,128)}) %all-reduce.61.cloned.1.call-update) | async-done | bytes 6291472 | tf_op jit(solution)/shard_map/psum | solution.py:152
  968.5 48.2 %while.107 = (s32[]{:T(128)}, f32[12,64,128]{2,1,0:T(8,128)S(1)}, f32[4,12,64,128]{3,2,1,0:T(8,128)}, f32[4,12]{1,0:T(4,128)S(1)}, f32[4,256,128]{2,1,0:T(8,128)...) while((s32[]{:T(128)}, f32[12,64,128]{2,1,0:T(8,128)S(1)}, ...), condition=%wide.region_39.41_spmd.clone, body=%wide.region_36.40_spmd.clone.sunk | while | flops 605457408 | bytes 7853125 | solution.py:83
  1016.7 21.6 %fusion.73 = (f32[4,256,12]{1,2,0:T(8,128)}, f32[4,256,12]{1,2,0:T(8,128)}, f32[4,256,256]{2,1,0:T(8,128)S(1)}) fusion(f32[4,256,256]{2,1,0:T(8,128)} %fusion.288, f32[4,256,12]{1,2,0:T(8,128)S(1)} %copy-done.36, pred[4,256,256]{2,1,0:T(8,128)(4,1)} %compare_and_fusion, f32[4,256,12,64]{1,0,3,2:T(4,128)} %reshape.929, f32[4,256,12]{1,2,0:T(8,128)S(1)} %copy-done.60, ...), kind=kOutput, calls=%fused_computation.130 | convolution fusion | flops 2444730368 | bytes 8847360 | tf_op jit(solution)/shard_map/transpose(jvp(ctsh,cshp->cthp))/dot_general | solution.py:57
  1061.2 14.2 multiply_reduce_fusion.5
  1077.8 9.9 reduce-window.49
  1175.1 38.9 %reduce-scatter.33.cloned.1.call-done = bf16[192,64]{1,0:T(8,128)(2,1)} async-done(((bf16[1536,64]{1,0:T(8,128)(2,1)}), bf16[192,64]{1,0:T(8,128)(2,1)}) %reduce-scatter.33.cloned.1.call-update) | async-done | bytes 24592
  1221.2 56.9 %reduce-scatter.35.cloned.1.call-done = bf16[192,12]{1,0:T(8,128)(2,1)} async-done(((bf16[1536,12]{1,0:T(8,128)(2,1)}), bf16[192,12]{1,0:T(8,128)(2,1)}) %reduce-scatter.35.cloned.1.call-update) | async-done | bytes 4624
  1279.7 62.5 %reduce-scatter.31.cloned.1.call-done = bf16[192,64]{1,0:T(8,128)(2,1)} async-done(((bf16[1536,64]{1,0:T(8,128)(2,1)}), bf16[192,64]{1,0:T(8,128)(2,1)}) %reduce-scatter.31.cloned.1.call-update) | async-done | bytes 24592
  1343.8 69.8 %reduce-scatter.29.cloned.1.call-done = bf16[192,768]{1,0:T(8,128)(2,1)} async-done(((bf16[1536,768]{1,0:T(8,128)(2,1)}), bf16[192,768]{1,0:T(8,128)(2,1)}) %reduce-scatter.29.cloned.1.call-update) | async-done | bytes 294928 | tf_op jit(solution)/shard_map/reduce_scatter | solution.py:323
  1413.5 71.3 %reduce-scatter.27.cloned.1.call-done = bf16[192,768]{1,0:T(8,128)(2,1)} async-done(((bf16[1536,768]{1,0:T(8,128)(2,1)}), bf16[192,768]{1,0:T(8,128)(2,1)}) %reduce-scatter.27.cloned.1.call-update) | async-done | bytes 294928 | tf_op jit(solution)/shard_map/reduce_scatter | solution.py:323
  1487.0 69.3 %reduce-scatter.25.cloned.1.call-done = bf16[192,768]{1,0:T(8,128)(2,1)} async-done(((bf16[1536,768]{1,0:T(8,128)(2,1)}), bf16[192,768]{1,0:T(8,128)(2,1)}) %reduce-scatter.25.cloned.1.call-update) | async-done | bytes 294928 | tf_op jit(solution)/shard_map/reduce_scatter | solution.py:314
  1556.3 71.3 %reduce-scatter.23.cloned.1.call-done = bf16[192,768]{1,0:T(8,128)(2,1)} async-done(((bf16[1536,768]{1,0:T(8,128)(2,1)}), bf16[192,768]{1,0:T(8,128)(2,1)}) %reduce-scatter.23.cloned.1.call-update) | async-done | bytes 294928 | tf_op jit(solution)/shard_map/reduce_scatter | solution.py:314
  1629.7 69.8 %reduce-scatter.21.cloned.1.call-done = bf16[192,768]{1,0:T(8,128)(2,1)} async-done(((bf16[1536,768]{1,0:T(8,128)(2,1)}), bf16[192,768]{1,0:T(8,128)(2,1)}) %reduce-scatter.21.cloned.1.call-update) | async-done | bytes 294928 | tf_op jit(solution)/shard_map/reduce_scatter | solution.py:311
  1699.6 71.3 %reduce-scatter.19.cloned.1.call-done = bf16[192,768]{1,0:T(8,128)(2,1)} async-done(((bf16[1536,768]{1,0:T(8,128)(2,1)}), bf16[192,768]{1,0:T(8,128)(2,1)}) %reduce-scatter.19.cloned.1.call-update) | async-done | bytes 294928 | tf_op jit(solution)/shard_map/reduce_scatter | solution.py:311
  1773.0 221.2 %all-reduce.65.cloned.1.call-done = (f32[1024,1536]{1,0:T(8,128)}, f32[1024,1536]{1,0:T(8,128)}) async-done(((f32[1024,1536]{1,0:T(8,128)}, f32[1024,1536]{1,0:T(8,128)}), (f32[1024,1536]{1,0:T(8,128)}, f32[1024,1536]{1,0:T(8,128)})) %all-reduce.65.cloned.1.call-update) | async-done | bytes 12582928 | tf_op jit(solution)/shard_map/psum | solution.py:152
  1999.2 37.6 %all-reduce.49 = (bf16[2,1536]{1,0:T(2,128)(2,1)S(1)}, bf16[2,4,768]{2,1,0:T(4,128)(2,1)S(1)}, bf16[2,768]{1,0:T(2,128)(2,1)S(1)}, bf16[2,4,256]{2,1,0:T(4,128)(...) all-reduce(bf16[2,1536]{1,0:T(2,128)(2,1)S(1)} %pad_maximum_fusion., ...), channel_id=1, replica_groups=mesh['tensor'=4,'dp'=8] {'dp'}, use_global_device_ids=true, to_apply=%region_52.54 | all-reduce | flops 14920 | bytes 59680 | tf_op jit(solution)/shard_map/psum | solution.py:344
  2042.2 9.2 fusion.79
  (967 shorter events, 729.8 us)
Async XLA Ops:
  7.2 141.7 %all-gather.17.cloned.1.call-start = ((), (), s32[]{:S(2)}) async-start(), calls=%async_computation.20 | async-start | bytes 2654208 | tf_op jit(solution)/shard_map/all_gather | solution.py:193
  9.3 259.3 %all-gather.19.cloned.1.call-start = ((), (), s32[]{:S(2)}) async-start(), calls=%async_computation.21 | async-start | bytes 2654208 | tf_op jit(solution)/shard_map/all_gather | solution.py:192
  11.3 271.7 %all-gather.21.cloned.1.call-start = ((), (), s32[]{:S(2)}) async-start(), calls=%async_computation.22 | async-start | bytes 2654208 | tf_op jit(solution)/shard_map/all_gather | solution.py:219
  13.3 398.9 %all-reduce.57.cloned.1.call-start = ((), (), s32[]{:S(2)}) async-start(), calls=%async_computation.10 | async-start | bytes 12582912 | tf_op jit(solution)/shard_map/psum | solution.py:152
  61.0 207.7 %copy-start.8 = (bf16[1024,1536]{1,0:T(8,128)(2,1)}, bf16[1024,1536]{1,0:T(8,128)(2,1)S(1)}, u32[]{:S(2)}) copy-start(bf16[1024,1536]{1,0:T(8,128)(2,1)S(1)} %fusion.76) | copy-start | bytes 9437188
  62.1 91.1 %copy-start.71 = (f32[1024]{0:T(1024)}, f32[1024]{0:T(1024)S(1)}, u32[]{:S(2)}) copy-start(f32[1024]{0:T(1024)S(1)} %get-tuple-element.1693) | copy-start | bytes 12292
  62.1 91.1 %copy-start.74 = (f32[1024]{0:T(1024)}, f32[1024]{0:T(1024)S(1)}, u32[]{:S(2)}) copy-start(f32[1024]{0:T(1024)S(1)} %get-tuple-element.1695) | copy-start | bytes 12292
  62.1 91.1 %copy-start.77 = (f32[1024]{0:T(1024)}, f32[1024]{0:T(1024)S(1)}, u32[]{:S(2)}) copy-start(f32[1024]{0:T(1024)S(1)} %get-tuple-element.1694) | copy-start | bytes 12292
  291.0 74.3 %copy-start.190 = (f32[12]{0:T(128)S(1)}, f32[12]{0:T(128)}, u32[]{:S(2)}) copy-start(f32[12]{0:T(128)} %get-tuple-element.1700) | copy-start | bytes 148
  291.0 121.2 %copy-start.13 = (bf16[1024,1536]{1,0:T(8,128)(2,1)S(1)}, bf16[1024,1536]{1,0:T(8,128)(2,1)}, u32[]{:S(2)}) copy-start(bf16[1024,1536]{1,0:T(8,128)(2,1)} %param.26) | copy-start | bytes 9437188
  291.0 175.5 %all-gather.23.cloned.1.call-start = ((), (), s32[]{:S(2)}) async-start(), calls=%async_computation.23 | async-start | bytes 2654208 | tf_op jit(solution)/shard_map/all_gather | solution.py:193
  291.6 299.5 %all-gather.25.cloned.1.call-start = ((), (), s32[]{:S(2)}) async-start(), calls=%async_computation.24 | async-start | bytes 2654208 | tf_op jit(solution)/shard_map/all_gather | solution.py:192
  292.2 312.8 %all-gather.27.cloned.1.call-start = ((), (), s32[]{:S(2)}) async-start(), calls=%async_computation.25 | async-start | bytes 2654208 | tf_op jit(solution)/shard_map/all_gather | solution.py:219
  292.9 504.5 %all-reduce.59.cloned.1.call-start = ((), (), s32[]{:S(2)}) async-start(), calls=%async_computation.11 | async-start | bytes 1048576 | tf_op jit(solution)/shard_map/psum | solution.py:271
  418.6 172.6 %copy-start.5 = (bf16[1024,1536]{1,0:T(8,128)(2,1)}, bf16[1024,1536]{1,0:T(8,128)(2,1)S(1)}, u32[]{:S(2)}) copy-start(bf16[1024,1536]{1,0:T(8,128)(2,1)S(1)} %multiply_convert_fusion) | copy-start | bytes 9437188
  727.5 198.2 %all-reduce.61.cloned.1.call-start = ((), (), s32[]{:S(2)}) async-start(), calls=%async_computation.12 | async-start | bytes 12582912 | tf_op jit(solution)/shard_map/psum | solution.py:152
  807.8 285.1 %all-reduce.63.cloned.1.call-start = ((), (), s32[]{:S(2)}) async-start(), calls=%async_computation.13 | async-start | bytes 1048576 | tf_op jit(solution)/shard_map/psum | solution.py:271
  807.8 124.1 %copy-start.40 = (bf16[1024,1536]{1,0:T(8,128)(2,1)S(1)}, bf16[1024,1536]{1,0:T(8,128)(2,1)}, u32[]{:S(2)}) copy-start(bf16[1024,1536]{1,0:T(8,128)(2,1)} %param.42) | copy-start | bytes 9437188
  1051.4 122.7 %reduce-scatter.37.cloned.1.call-start = ((), (), s32[]{:S(2)}) async-start(), calls=%async_computation.29 | async-start | bytes 442368
  1053.3 160.7 %reduce-scatter.33.cloned.1.call-start = ((), (), s32[]{:S(2)}) async-start(), calls=%async_computation.27 | async-start | bytes 442368
  1056.0 222.1 %reduce-scatter.35.cloned.1.call-start = ((), (), s32[]{:S(2)}) async-start(), calls=%async_computation.28 | async-start | bytes 442368
  1092.8 249.4 %reduce-scatter.31.cloned.1.call-start = ((), (), s32[]{:S(2)}) async-start(), calls=%async_computation.26 | async-start | bytes 442368
  1096.5 317.0 %reduce-scatter.29.cloned.1.call-start = ((), (), s32[]{:S(2)}) async-start(), calls=%async_computation.19 | async-start | bytes 2654208 | tf_op jit(solution)/shard_map/reduce_scatter | solution.py:323
  1103.9 381.0 %reduce-scatter.27.cloned.1.call-start = ((), (), s32[]{:S(2)}) async-start(), calls=%async_computation.18 | async-start | bytes 2654208 | tf_op jit(solution)/shard_map/reduce_scatter | solution.py:323
  1112.0 444.3 %reduce-scatter.25.cloned.1.call-start = ((), (), s32[]{:S(2)}) async-start(), calls=%async_computation.17 | async-start | bytes 2654208 | tf_op jit(solution)/shard_map/reduce_scatter | solution.py:314
  1117.4 510.2 %reduce-scatter.23.cloned.1.call-start = ((), (), s32[]{:S(2)}) async-start(), calls=%async_computation.16 | async-start | bytes 2654208 | tf_op jit(solution)/shard_map/reduce_scatter | solution.py:314
  1142.9 556.6 %reduce-scatter.21.cloned.1.call-start = ((), (), s32[]{:S(2)}) async-start(), calls=%async_computation.15 | async-start | bytes 2654208 | tf_op jit(solution)/shard_map/reduce_scatter | solution.py:311
  1148.4 622.5 %reduce-scatter.19.cloned.1.call-start = ((), (), s32[]{:S(2)}) async-start(), calls=%async_computation.14 | async-start | bytes 2654208 | tf_op jit(solution)/shard_map/reduce_scatter | solution.py:311
  1155.3 838.9 %all-reduce.65.cloned.1.call-start = ((), (), s32[]{:S(2)}) async-start(), calls=%async_computation.30 | async-start | bytes 25165824 | tf_op jit(solution)/shard_map/psum | solution.py:152
  1173.4 820.8 %copy-start.93 = (f32[1536]{0:T(1024)S(1)}, f32[1536]{0:T(1024)}, u32[]{:S(2)}) copy-start(f32[1536]{0:T(1024)} %copy-done.92) | copy-start | bytes 18436
  1173.4 820.8 %copy-start.102 = (f32[1024]{0:T(1024)S(1)}, f32[1024]{0:T(1024)}, u32[]{:S(2)}) copy-start(f32[1024]{0:T(1024)} %copy-done.101) | copy-start | bytes 12292
  1994.2 57.2 %slice-start = ((s8[6291456]{0:T(1024)(128)(4,1)}), s8[2097152]{0:T(1024)(128)(4,1)S(1)}, s32[]{:S(2)}) async-start(s8[6291456]{0:T(1024)(128)(4,1)} %bitcast.606), calls=%async_computation.31 | async-start | bytes 4194304
  (197 other events, 2177.1 us)
Sparse Core Ops, SparseCore 0:
  10.8 61.1 all-gather.16
  74.2 55.5 all-gather.18
  132.5 50.5 all-gather.20
  291.1 121.0 all-reduce.56
  414.2 52.2 all-gather.22
  468.6 50.6 all-gather.24
  521.4 50.5 all-gather.26
  727.6 31.2 all-reduce.58
  807.9 117.7 all-reduce.60
  1051.6 33.6 all-reduce.62
  1088.5 61.2 reduce-scatter.36
  1153.5 60.3 reduce-scatter.32
  1217.8 60.2 reduce-scatter.34
  1281.8 60.3 reduce-scatter.30
  1345.5 67.9 reduce-scatter.28
  1416.9 67.8 reduce-scatter.26
  1488.2 68.0 reduce-scatter.24
  1559.6 67.9 reduce-scatter.22
  1631.7 67.8 reduce-scatter.20
  1702.9 67.9 reduce-scatter.18
  1774.1 220.0 all-reduce.64
where the time goes:
time: 2080 us; the launch traced here: 2060 us
  waiting for transfers between devices  990 us (48%)
  matrix products  332 us (16%)
  local copies, waits for them, and re-layouts  253 us (12%)
  other arithmetic  251 us (12%)
  blocking collectives  208 us (10%)
    psum x3, waiting for transfers between devices, head_reduce(): return lax.psum(partial_rows, 'tensor')  385 us
    unnamed x25, waiting for transfers between devices  160 us
    reduce_scatter x2, waiting for transfers between devices, on_device(): lax.psum_scatter(grad_wz.astype(jnp.bfloat16), 'dp', scatter_dimension=0,...  141 us
    reduce_scatter x2, waiting for transfers between devices, on_device(): lax.psum_scatter(grad_out_w.astype(jnp.bfloat16), 'dp', scatter_dimension...  141 us
    reduce_scatter x2, waiting for transfers between devices, on_device(): lax.psum_scatter(grad_wx.astype(jnp.bfloat16), 'dp', scatter_dimension=0,...  141 us
    dot_general x6, matrix products, block_scan(): jnp.einsum('ctsh,cshp->cthp', weights * intersection[..., None], inputs,...  101 us
    all_gather x2, blocking collectives, on_device(): lax.all_gather(w_bc[layer_idx], 'dp', axis=0, tiled=True)  69.9 us
    all_gather x2, blocking collectives, on_device(): lax.all_gather(w_dt[layer_idx], 'dp', axis=0, tiled=True)  69.6 us
  transfers between devices with their start and end apart: 21, of which 13 were waited for; matrix products, arithmetic and copies ran while one was open for 26% of the time, Pallas kernels for 0%

commit v1 on v0

v1 whole, which is shorter than its diff:
```python
import jax
import jax.numpy as jnp
from jax import lax
from jax.sharding import PartitionSpec as P
from jax.experimental import pallas as pl
from jax.experimental.pallas import tpu as pltpu

HEAD_DIM = 64
STATE = 128
PACK = 1024
LAYERS = 2
INNER = 3072
EPSILON = 1e-05
CHUNK = 128
LANES = 128
GROUP = 16
TAIL = 8
FAR = -10000.0
PRECISE = lax.Precision.HIGHEST
BF16 = jnp.bfloat16
F32 = jnp.float32
VMEM_BYTES = 48 * 1024 * 1024


def mm(lhs, rhs, precision=None):
    return lax.dot_general(
        lhs, rhs, (((1,), (0,)), ((), ())), precision=precision, preferred_element_type=F32
    )


def mm_t(lhs, rhs):
    return lax.dot_general(lhs, rhs, (((1,), (1,)), ((), ())), preferred_element_type=F32)


def t_mm(lhs, rhs):
    return lax.dot_general(lhs, rhs, (((0,), (0,)), ((), ())), preferred_element_type=F32)


def iota(shape, dim):
    return lax.broadcasted_iota(jnp.int32, shape, dim)


def expand(values, spread):
    lane = iota(values.shape, 1)
    high = values.astype(BF16).astype(F32)
    parts = jnp.where(lane < GROUP, high, jnp.where(lane < 2 * GROUP, values - high, 0.0))
    return mm(parts.astype(BF16), spread)


def shifted_back(joined, offset):
    return joined[TAIL - offset : TAIL - offset + CHUNK]


def conv_pre(joined, taps, bias_row, aux):
    summed = bias_row + taps[0:1] * joined[TAIL:]
    for offset in range(1, 4):
        summed = summed + taps[offset : offset + 1] * (
            shifted_back(joined, offset) * aux[:, offset : offset + 1]
        )
    return summed


def halves_rows(tile, low_lanes):
    zero = jnp.zeros_like(tile)
    return jnp.concatenate(
        [jnp.where(low_lanes, tile, zero), jnp.where(low_lanes, zero, tile)], 0
    )


def step_values(dt_ref, head_ref):
    raw = dt_ref + head_ref[0:1]
    dt = jnp.maximum(raw, 0.0) + jnp.log1p(jnp.exp(-jnp.abs(raw)))
    row = iota((CHUNK, CHUNK), 0)
    col = iota((CHUNK, CHUNK), 1)
    lower = (row >= col).astype(F32)
    log_decay = mm(lower, dt * head_ref[1:2], PRECISE)
    return raw, dt, log_decay, row, col


def scan_fwd_kernel(
    with_cross,
    x_ref,
    bcdt_ref,
    gate_ref,
    aux_ref,
    seg_ref,
    taps_ref,
    bias_ref,
    bc_taps_ref,
    bc_bias_ref,
    head_ref,
    skip_ref,
    gain_ref,
    spread_ref,
    *rest,
):
    if with_cross:
        gs_ref, u_ref, y_ref, sq_ref, kept_ref, state, tail_x, tail_bc = rest
    else:
        u_ref, y_ref, sq_ref, kept_ref, state, tail_x, tail_bc = rest
    width = x_ref.shape[1]

    @pl.when(pl.program_id(0) == 0)
    def _():
        state[...] = jnp.zeros_like(state)
        tail_x[...] = jnp.zeros_like(tail_x)
        tail_bc[...] = jnp.zeros_like(tail_bc)

    aux = aux_ref[...]
    bc_now = bcdt_ref[:, : 2 * STATE]
    joined_bc = jnp.concatenate([tail_bc[...], bc_now], 0)
    tail_bc[...] = bc_now[CHUNK - TAIL :]
    bc_pre = conv_pre(joined_bc, bc_taps_ref[...], bc_bias_ref[...], aux)
    bc = bc_pre * jax.nn.sigmoid(bc_pre)
    b_low = bc[:, :STATE].astype(BF16)
    c_low = bc[:, STATE:].astype(BF16)
    b_turned = bc[:, :STATE].T.astype(BF16)
    _, dt, log_decay, row, col = step_values(bcdt_ref[:, 2 * STATE :], head_ref)
    log_turned = log_decay.T
    meet = mm_t(c_low, b_low)
    visible = (aux[:, 0:1] == seg_ref[0]) & (row >= col)
    spread = spread_ref[...]
    dt_wide = expand(dt, spread)
    reach = expand(jnp.exp(log_decay) * aux[:, 4:5], spread)
    to_end = expand(jnp.exp(log_decay[CHUNK - 1 :] - log_decay) * aux[:, 5:6], spread)
    state_low = state[...].astype(BF16)
    kept_ref[0] = state_low
    carried = mm(c_low, state_low)
    low_lanes = iota((CHUNK, LANES), 1) < HEAD_DIM
    squares = jnp.zeros((CHUNK, LANES), F32)
    crosses = jnp.zeros((CHUNK, LANES), F32)
    for pair in range(width // LANES):
        at = slice(pair * LANES, (pair + 1) * LANES)
        now = x_ref[:, at]
        joined = jnp.concatenate([tail_x[:, at], now], 0)
        tail_x[:, at] = now[CHUNK - TAIL :]
        pre = conv_pre(joined, taps_ref[:, at], bias_ref[:, at], aux)
        x_conv = pre * jax.nn.sigmoid(pre)
        inputs = x_conv * dt_wide[:, at]
        mats = []
        for head in (2 * pair, 2 * pair + 1):
            gap = log_decay[:, head : head + 1] - log_turned[head : head + 1, :]
            mats.append((jnp.exp(jnp.where(visible, gap, FAR)) * meet).astype(BF16))
        local = mm(jnp.concatenate(mats, 1), halves_rows(inputs.astype(BF16), low_lanes))
        y = local + carried[:, at] * reach[:, at] + skip_ref[:, at] * x_conv
        y_ref[:, at] = y.astype(y_ref.dtype)
        ending = (inputs * to_end[:, at]).astype(BF16)
        state[:, at] = state[:, at] * reach[CHUNK - 1 :, at] + mm(b_turned, ending)
        gate = gate_ref[:, at].astype(F32)
        gated = y * (gate * jax.nn.sigmoid(gate))
        grown = gated * gain_ref[:, at]
        u_ref[:, at] = grown.astype(BF16)
        squares = squares + gated * gated
        if with_cross:
            crosses = crosses + grown * gs_ref[:, at].astype(F32)
    ones = jnp.ones((8, LANES), F32)
    sums = lax.dot_general(
        ones, squares, (((1,), (1,)), ((), ())), precision=PRECISE, preferred_element_type=F32
    )
    if with_cross:
        more = lax.dot_general(
            ones, crosses, (((1,), (1,)), ((), ())), precision=PRECISE, preferred_element_type=F32
        )
        sums = jnp.where(iota((8, CHUNK), 0) == 0, sums, more)
    sq_ref[...] = sums


def whole(shape):
    return pl.BlockSpec(shape, lambda c: (0,) * len(shape))


def scan_fwd(x_pre, bcdt_pre, gate_pre, side, weights, gs=None, y_dtype=F32):
    length, width = x_pre.shape
    chunks = length // CHUNK
    aux, seg_rows = side
    taps, bias, bc_taps, bc_bias, head, skip, gain, spread = weights
    tile = lambda columns: pl.BlockSpec((CHUNK, columns), lambda c: (c, 0))
    in_specs = [
        tile(width),
        tile(bcdt_pre.shape[1]),
        tile(width),
        tile(LANES),
        pl.BlockSpec((1, 1, CHUNK), lambda c: (c, 0, 0)),
    ] + [whole(w.shape) for w in weights]
    args = [x_pre, bcdt_pre, gate_pre, aux, seg_rows, *weights]
    if gs is not None:
        in_specs.append(tile(width))
        args.append(gs)

    def kernel(*refs):
        scan_fwd_kernel(gs is not None, *refs)

    return pl.pallas_call(
        kernel,
        grid=(chunks,),
        in_specs=in_specs,
        out_specs=[
            tile(width),
            tile(width),
            pl.BlockSpec((8, CHUNK), lambda c: (0, c)),
            pl.BlockSpec((1, STATE, width), lambda c: (c, 0, 0)),
        ],
        out_shape=[
            jax.ShapeDtypeStruct((length, width), BF16),
            jax.ShapeDtypeStruct((length, width), y_dtype),
            jax.ShapeDtypeStruct((8, length), F32),
            jax.ShapeDtypeStruct((chunks, STATE, width), BF16),
        ],
        scratch_shapes=[
            pltpu.VMEM((STATE, width), F32),
            pltpu.VMEM((TAIL, width), F32),
            pltpu.VMEM((TAIL, 2 * STATE), F32),
        ],
        compiler_params=pltpu.CompilerParams(vmem_limit_bytes=VMEM_BYTES),
        cost_estimate=pl.CostEstimate(
            flops=16 * length * width * LANES, bytes_accessed=16 * length * width, transcendentals=0
        ),
        name="scan_fwd",
    )(*args)


def gate_bwd_kernel(
    gs_ref, y_ref, gate_ref, col_ref, gain_ref, g_gate_ref, g_y_ref, scaled_ref, d_gain_ref
):
    @pl.when(pl.program_id(0) == 0)
    def _():
        d_gain_ref[...] = jnp.zeros_like(d_gain_ref)

    inv = col_ref[:, 0:1]
    pull = col_ref[:, 1:2]
    for pair in range(gs_ref.shape[1] // LANES):
        at = slice(pair * LANES, (pair + 1) * LANES)
        gs = gs_ref[:, at].astype(F32)
        y = y_ref[:, at].astype(F32)
        gate = gate_ref[:, at].astype(F32)
        sig = jax.nn.sigmoid(gate)
        act = gate * sig
        gated = y * act
        normal = gated * inv
        gain = gain_ref[:, at]
        d_gain_ref[:, at] += jnp.sum(gs * normal, 0, keepdims=True)
        g_gated = inv * (gs * gain) - gated * pull
        scaled_ref[:, at] = (normal * gain).astype(BF16)
        g_y_ref[:, at] = (g_gated * act).astype(BF16)
        g_gate_ref[:, at] = (g_gated * y * sig * (1.0 + gate * (1.0 - sig))).astype(BF16)


def gate_bwd(gs, y, gate_pre, columns, gain, rows=256):
    length, width = gs.shape
    tile = pl.BlockSpec((rows, width), lambda c: (c, 0))
    return pl.pallas_call(
        gate_bwd_kernel,
        grid=(length // rows,),
        in_specs=[
            tile,
            tile,
            tile,
            pl.BlockSpec((rows, columns.shape[1]), lambda c: (c, 0)),
            whole(gain.shape),
        ],
        out_specs=[tile, tile, tile, whole((1, width))],
        out_shape=[jax.ShapeDtypeStruct((length, width), BF16)] * 3
        + [jax.ShapeDtypeStruct((1, width), F32)],
        compiler_params=pltpu.CompilerParams(vmem_limit_bytes=VMEM_BYTES),
        cost_estimate=pl.CostEstimate(
            flops=20 * length * width, bytes_accessed=18 * length * width, transcendentals=0
        ),
        name="gate_bwd",
    )(gs, y, gate_pre, columns, gain)


def conv_bwd(joined, joined_grad, grad, taps, aux, acc_ref, at):
    acc_ref[4:5, at] += jnp.sum(grad, 0, keepdims=True)
    acc_ref[0:1, at] += jnp.sum(grad * joined[TAIL:], 0, keepdims=True)
    result = taps[0:1] * grad
    for offset in range(1, 4):
        moved = shifted_back(joined, offset) * aux[:, offset : offset + 1]
        acc_ref[offset : offset + 1, at] += jnp.sum(grad * moved, 0, keepdims=True)
        later = joined_grad[offset : offset + CHUNK] * aux[:, 5 + offset : 6 + offset]
        result = result + taps[offset : offset + 1] * later
    return result


def scan_bwd_kernel(
    g_ref,
    x_ref,
    x_tail_ref,
    bcdt_ref,
    bc_tail_ref,
    kept_ref,
    aux_ref,
    seg_ref,
    taps_ref,
    bias_ref,
    bc_taps_ref,
    bc_bias_ref,
    head_ref,
    skip_ref,
    gain_ref,
    spread_ref,
    gx_ref,
    gbc_ref,
    gdt_ref,
    accx_ref,
    accbc_ref,
    acch_ref,
    grad_state,
    next_x,
    next_bc,
):
    width = x_ref.shape[1]

    @pl.when(pl.program_id(0) == 0)
    def _():
        grad_state[...] = jnp.zeros_like(grad_state)
        next_x[...] = jnp.zeros_like(next_x)
        next_bc[...] = jnp.zeros_like(next_bc)
        accx_ref[...] = jnp.zeros_like(accx_ref)
        accbc_ref[...] = jnp.zeros_like(accbc_ref)
        acch_ref[...] = jnp.zeros_like(acch_ref)

    aux = aux_ref[...]
    joined_bc = jnp.concatenate([bc_tail_ref[:, : 2 * STATE], bcdt_ref[:, : 2 * STATE]], 0)
    bc_pre = conv_pre(joined_bc, bc_taps_ref[...], bc_bias_ref[...], aux)
    bc_sig = jax.nn.sigmoid(bc_pre)
    bc = bc_pre * bc_sig
    b_low = bc[:, :STATE].astype(BF16)
    c_low = bc[:, STATE:].astype(BF16)
    c_turned = bc[:, STATE:].T.astype(BF16)
    raw, dt, log_decay, row, col = step_values(bcdt_ref[:, 2 * STATE :], head_ref)
    log_turned = log_decay.T
    meet = mm_t(b_low, c_low)
    visible = (aux[:, 0:1] == seg_ref[0]) & (row <= col)
    spread = spread_ref[...]
    dt_wide = expand(dt, spread)
    reach = expand(jnp.exp(log_decay) * aux[:, 4:5], spread)
    to_end = expand(jnp.exp(log_decay[CHUNK - 1 :] - log_decay) * aux[:, 5:6], spread)
    low_lanes = iota((CHUNK, LANES), 1) < HEAD_DIM
    lane = iota((CHUNK, LANES), 1)
    grad_meet = jnp.zeros((CHUNK, CHUNK), F32)
    grad_b = jnp.zeros((CHUNK, STATE), F32)
    grad_c = jnp.zeros((CHUNK, STATE), F32)
    col_sums = jnp.zeros((CHUNK, LANES), F32)
    row_sums = jnp.zeros((LANES, CHUNK), F32)
    head_sums = jnp.zeros((3 * CHUNK, LANES), F32)
    through = jnp.zeros((8, LANES), F32)
    head_row = iota((LANES, CHUNK), 0)
    for pair in range(width // LANES):
        at = slice(pair * LANES, (pair + 1) * LANES)
        joined = jnp.concatenate([x_tail_ref[:, at], x_ref[:, at]], 0)
        pre = conv_pre(joined, taps_ref[:, at], bias_ref[:, at], aux)
        sig = jax.nn.sigmoid(pre)
        x_conv = pre * sig
        inputs = x_conv * dt_wide[:, at]
        g_low = g_ref[:, at]
        g = g_low.astype(F32)
        grad_mats = mm_t(halves_rows(inputs.astype(BF16), low_lanes), g_low)
        mats = []
        for member in range(2):
            head = 2 * pair + member
            gap = log_turned[head : head + 1, :] - log_decay[:, head : head + 1]
            weight = jnp.exp(jnp.where(visible, gap, FAR))
            mats.append((weight * meet).astype(BF16))
            part = weight * grad_mats[member * CHUNK : (member + 1) * CHUNK]
            grad_meet = grad_meet + part
            product = part * meet
            col_sums = jnp.where(lane == head, jnp.sum(product, 1, keepdims=True), col_sums)
            row_sums = jnp.where(head_row == head, jnp.sum(product, 0, keepdims=True), row_sums)
        local = mm(jnp.concatenate(mats, 1), halves_rows(g_low, low_lanes))
        reach_now = reach[:, at]
        to_end_now = to_end[:, at]
        state_low = kept_ref[0, :, at]
        coming = g * reach_now
        coming_low = coming.astype(BF16)
        carried = mm(c_low, state_low)
        grad_c = grad_c + mm_t(coming_low, state_low)
        grad_state_now = grad_state[:, at]
        grad_state_low = grad_state_now.astype(BF16)
        leaving = mm(b_low, grad_state_low)
        ending = inputs * to_end_now
        grad_b = grad_b + mm_t(ending.astype(BF16), grad_state_low)
        last = reach_now[CHUNK - 1 :]
        passed = jnp.sum(grad_state_now * state_low.astype(F32), 0, keepdims=True) * last
        through = through + mm_t(
            jnp.broadcast_to(passed, (8, LANES)).astype(BF16), spread[:, at]
        )
        grad_state[:, at] = grad_state_now * last + mm(c_turned, coming_low)
        grad_inputs = local + leaving * to_end_now
        stacked = jnp.concatenate([coming * carried, ending * leaving, grad_inputs * x_conv], 0)
        head_sums = head_sums + mm_t(stacked.astype(BF16), spread[:, at])
        acch_ref[0:1, at] += jnp.sum(g * x_conv, 0, keepdims=True)
        grad_conv = (grad_inputs * dt_wide[:, at] + g * skip_ref[:, at]) * (
            sig * (1.0 + pre * (1.0 - sig))
        )
        joined_grad = jnp.concatenate([grad_conv, next_x[:, at]], 0)
        next_x[:, at] = grad_conv[:TAIL]
        gx_ref[:, at] = conv_bwd(
            joined, joined_grad, grad_conv, taps_ref[:, at], aux, accx_ref, at
        ).astype(BF16)
    upper = (row <= col).astype(F32)
    strict = (row > col).astype(F32)
    straddle = (
        mm(upper, row_sums.T - col_sums + head_sums[:CHUNK], PRECISE)
        + mm(strict, head_sums[CHUNK : 2 * CHUNK], PRECISE)
        + through[0:1]
    )
    grad_dt = head_sums[2 * CHUNK :] + head_ref[1:2] * straddle
    grad_raw = jnp.where(lane < GROUP, grad_dt * jax.nn.sigmoid(raw), 0.0)
    gdt_ref[...] = grad_raw.astype(BF16)
    acch_ref[1:2, :LANES] += jnp.sum(grad_raw, 0, keepdims=True)
    acch_ref[2:3, :LANES] += jnp.sum(dt * straddle, 0, keepdims=True)
    grad_meet_low = grad_meet.astype(BF16)
    grad_b = grad_b + mm(grad_meet_low, c_low)
    grad_c = grad_c + t_mm(grad_meet_low, b_low)
    grad_bc = jnp.concatenate([grad_b, grad_c], 1) * (bc_sig * (1.0 + bc_pre * (1.0 - bc_sig)))
    joined_grad = jnp.concatenate([grad_bc, next_bc[...]], 0)
    next_bc[...] = grad_bc[:TAIL]
    gbc_ref[...] = conv_bwd(
        joined_bc, joined_grad, grad_bc, bc_taps_ref[...], aux, accbc_ref, slice(None)
    ).astype(BF16)


def scan_bwd(g_y, x_pre, bcdt_pre, kept, side, weights):
    length, width = x_pre.shape
    chunks = length // CHUNK
    aux, seg_rows = side
    back = lambda c: chunks - 1 - c
    tile = lambda columns: pl.BlockSpec((CHUNK, columns), lambda c: (back(c), 0))
    tail = lambda columns: pl.BlockSpec(
        (TAIL, columns), lambda c: (jnp.maximum(back(c) * (CHUNK // TAIL) - 1, 0), 0)
    )
    wide = bcdt_pre.shape[1]
    in_specs = [
        tile(width),
        tile(width),
        tail(width),
        tile(wide),
        tail(wide),
        pl.BlockSpec((1, STATE, width), lambda c: (back(c), 0, 0)),
        tile(LANES),
        pl.BlockSpec((1, 1, CHUNK), lambda c: (back(c), 0, 0)),
    ] + [whole(w.shape) for w in weights]
    return pl.pallas_call(
        scan_bwd_kernel,
        grid=(chunks,),
        in_specs=in_specs,
        out_specs=[
            tile(width),
            tile(2 * STATE),
            tile(LANES),
            whole((8, width)),
            whole((8, 2 * STATE)),
            whole((8, width)),
        ],
        out_shape=[
            jax.ShapeDtypeStruct((length, width), BF16),
            jax.ShapeDtypeStruct((length, 2 * STATE), BF16),
            jax.ShapeDtypeStruct((length, LANES), BF16),
            jax.ShapeDtypeStruct((8, width), F32),
            jax.ShapeDtypeStruct((8, 2 * STATE), F32),
            jax.ShapeDtypeStruct((8, width), F32),
        ],
        scratch_shapes=[
            pltpu.VMEM((STATE, width), F32),
            pltpu.VMEM((TAIL, width), F32),
            pltpu.VMEM((TAIL, 2 * STATE), F32),
        ],
        compiler_params=pltpu.CompilerParams(vmem_limit_bytes=VMEM_BYTES),
        cost_estimate=pl.CostEstimate(
            flops=40 * length * width * LANES, bytes_accessed=16 * length * width, transcendentals=0
        ),
        name="scan_bwd",
    )(g_y, x_pre, x_pre, bcdt_pre, bcdt_pre, kept, aux, seg_rows, *weights)


def side_arrays(segments):
    length = segments.shape[0]
    seg = segments.astype(F32)
    columns = [seg]
    nothing = lambda count: jnp.full((count,), -1.0, F32)
    for offset in range(1, 4):
        moved = jnp.concatenate([nothing(offset), seg[: length - offset]], 0)
        columns.append((moved == seg).astype(F32))
    blocks = seg.reshape(-1, CHUNK)
    ends = blocks[:, -1]
    before = jnp.concatenate([nothing(1), ends[:-1]], 0)
    columns.append((blocks == before[:, None]).astype(F32).reshape(-1))
    columns.append((blocks == ends[:, None]).astype(F32).reshape(-1))
    for offset in range(1, 4):
        moved = jnp.concatenate([seg[offset:], nothing(offset)], 0)
        columns.append((moved == seg).astype(F32))
    stacked = jnp.stack(columns, 1)
    aux = jnp.pad(stacked, ((0, 0), (0, LANES - stacked.shape[1])))
    return aux, blocks.reshape(-1, 1, CHUNK)


def in_groups(values):
    padded = jnp.pad(values, [(0, 0)] * (values.ndim - 1) + [(0, GROUP - values.shape[-1])])
    return jnp.tile(padded, (1,) * (values.ndim - 1) + (LANES // GROUP,))


def spread_matrix(width):
    head = lax.broadcasted_iota(jnp.int32, (LANES, width), 0) % GROUP
    owner = lax.broadcasted_iota(jnp.int32, (LANES, width), 1) // HEAD_DIM
    return (head == owner).astype(BF16)


def scan_weights(taps, bias, bc_taps, bc_bias, dt_bias, a_log, d_skip, gain, spread):
    rates = -jnp.exp(a_log)
    rows = jnp.stack([in_groups(dt_bias), in_groups(rates)])
    head = jnp.pad(rows, ((0, 6), (0, 0)))
    return (
        taps,
        bias[None],
        bc_taps,
        bc_bias[None],
        head,
        jnp.repeat(d_skip, HEAD_DIM)[None],
        gain[None],
        spread,
    )


def partners(count, step):
    return [(index, index ^ step) for index in range(count)]


def swap(values, axis, step):
    return lax.ppermute(values, axis, partners(lax.axis_size(axis), step))


def turn(values, blocks, ahead):
    perm = [
        (2 * block + side, 2 * ((block + ahead) % blocks) + side)
        for block in range(blocks)
        for side in range(2)
    ]
    return lax.ppermute(values, "dp", perm)


def after(values, *earlier):
    return lax.optimization_barrier((values, *earlier))[0]


def gather_rows(own, blocks):
    slots = [own] + [turn(own, blocks, ahead) for ahead in range(1, blocks)]
    across = [swap(slot, "dp", 1) for slot in slots]
    return jnp.concatenate(slots + across, 0), slots[-1]


def scatter_rows(left_part, right_part, blocks):
    height = left_part.shape[0] // blocks
    mine = right_part.astype(F32) + swap(left_part, "dp", 1).astype(F32)
    total = mine[:height]
    low = mine.astype(BF16)
    for ahead in range(1, blocks):
        piece = low[ahead * height : (ahead + 1) * height]
        total = total + turn(piece, blocks, blocks - ahead).astype(F32)
    return total


def weight_grad(rows, grads, blocks):
    width = rows.shape[1] // 2
    dims = (((0,), (0,)), ((), ()))
    sent = lax.dot_general(rows[:, width:], grads, dims, preferred_element_type=F32).astype(BF16)
    kept = lax.dot_general(rows[:, :width], grads, dims, preferred_element_type=F32)
    return scatter_rows(sent, kept, blocks)


class Quarters:
    def __init__(self, length):
        place = lax.axis_index("tensor")
        self.core = place % 2
        self.far = place // 2
        self.half = length // 2
        self.size = length // 4

    def own(self, values):
        start = self.core * self.half + self.far * self.size
        return lax.dynamic_slice_in_dim(values, start, self.size, 0)

    def reduce(self, make):
        sent = make((1 - self.core) * self.half).astype(BF16)
        got = swap(sent, "tensor", 1)
        mine = make(self.core * self.half) + got.astype(F32)
        away = lax.dynamic_slice_in_dim(mine, (1 - self.far) * self.size, self.size, 0)
        got = swap(away.astype(BF16), "tensor", 2)
        near = lax.dynamic_slice_in_dim(mine, self.far * self.size, self.size, 0)
        return near + got.astype(F32)

    def join(self, values):
        got = swap(values, "tensor", 2)
        first = self.far == 0
        half = jnp.concatenate([jnp.where(first, values, got), jnp.where(first, got, values)], 0)
        got = swap(half, "tensor", 1)
        first = self.core == 0
        return jnp.concatenate([jnp.where(first, half, got), jnp.where(first, got, half)], 0)


def tensor_sum(values):
    values = values + swap(values, "tensor", 1)
    return values + swap(values, "tensor", 2)


def dp_sum(values):
    step = 1
    while step < lax.axis_size("dp"):
        values = values + swap(values, "dp", step)
        step = 2 * step
    return values


def dot(lhs, rhs):
    return lax.dot_general(lhs, rhs, (((1,), (0,)), ((), ())), preferred_element_type=F32)


def dot_t(lhs, rhs):
    return lax.dot_general(lhs, rhs, (((1,), (1,)), ((), ())), preferred_element_type=F32)


def turned_order(features, blocks):
    place = lax.axis_index("dp")
    block, side = place // 2, place % 2
    height = features // (2 * blocks)
    index = lax.broadcasted_iota(jnp.int32, (features, features), 1)
    part, within = index // height, index % height
    source_side = lax.rem(side + part // blocks, 2)
    source_block = lax.rem(block + blocks - part % blocks, blocks)
    source = (2 * source_block + source_side) * height + within
    return (lax.broadcasted_iota(jnp.int32, (features, features), 0) == source).astype(BF16)


def on_device(
    hidden,
    segments,
    norm_gain,
    w_z,
    w_x,
    w_bc,
    w_dt,
    conv_x_w,
    conv_x_b,
    conv_bc_w,
    conv_bc_b,
    dt_bias,
    a_log,
    d_skip,
    gated_gain,
    w_out,
    cotangent,
):
    length, features = hidden.shape
    width = w_x.shape[2]
    heads = dt_bias.shape[1]
    blocks = lax.axis_size("dp") // 2
    quarters = Quarters(length)
    order = turned_order(features, blocks)

    w_bcdt = jnp.concatenate([w_bc, in_groups(w_dt)], 2)
    gathered = []
    earlier = None
    for layer in range(LAYERS):
        row = []
        for group in (w_bcdt[layer], w_x[layer], w_z[layer], w_out[layer]):
            if earlier is not None:
                group = after(group, earlier)
            full, earlier = gather_rows(group, blocks)
            row.append(full)
        gathered.append(row)

    side = side_arrays(segments)
    spread = spread_matrix(width)
    weights = [
        scan_weights(
            conv_x_w[layer],
            conv_x_b[layer],
            conv_bc_w[layer],
            conv_bc_b[layer],
            dt_bias[layer],
            a_log[layer],
            d_skip[layer],
            gated_gain[layer],
            spread,
        )
        for layer in range(LAYERS)
    ]
    gains = mm(norm_gain, order.astype(F32), PRECISE)
    hidden_low = dot(hidden, order).astype(BF16)
    cotangent_low = dot(cotangent, order).astype(BF16)

    def rms_of(stream):
        return lax.rsqrt(jnp.mean(stream * stream, -1, keepdims=True) + EPSILON)

    def half_of(values, start):
        return lax.dynamic_slice_in_dim(values, start, quarters.half, 0)

    streams, totals, saved = [], [], []
    stream_full = hidden_low.astype(F32)
    normed = (stream_full * rms_of(stream_full) * gains[0]).astype(BF16)
    stream = quarters.own(hidden_low).astype(F32)
    for layer in range(LAYERS):
        wf_bcdt, wf_x, wf_z, wf_out = gathered[layer]
        bcdt_pre = dot(normed, wf_bcdt)
        x_pre = dot(normed, wf_x)
        gate_pre = dot(normed, wf_z)
        u, y, sq, kept = scan_fwd(x_pre, bcdt_pre, gate_pre, side, weights[layer])
        inv = lax.rsqrt(tensor_sum(sq[0:1]) / INNER + EPSILON)[0]
        total = quarters.reduce(lambda start: dot_t(half_of(u, start), wf_out))
        streams.append(stream)
        totals.append(total)
        saved.append((normed, x_pre, bcdt_pre, gate_pre, u, y, kept, inv))
        stream = stream + quarters.own(inv)[:, None] * total
        if layer + 1 < LAYERS:
            normed_own = (stream * rms_of(stream) * gains[layer + 1]).astype(BF16)
            normed = quarters.join(normed_own)
    mixed = quarters.join(dot_t(stream.astype(BF16), order).astype(BF16))

    grad_low = cotangent_low
    grad_stream = quarters.own(cotangent_low).astype(F32)
    weight_parts = [None] * LAYERS
    small_parts = [None] * LAYERS
    for layer in reversed(range(LAYERS)):
        wf_bcdt, wf_x, wf_z, wf_out = gathered[layer]
        normed, x_pre, bcdt_pre, gate_pre, u, y, kept, inv = saved[layer]
        grad_scaled = dot(grad_low, wf_out)
        if layer + 1 == LAYERS:
            cross = jnp.sum(grad_scaled * u.astype(F32), -1)
            cross = tensor_sum(cross[None])[0]
        else:
            cross = quarters.join(jnp.sum(grad_low_own.astype(F32) * totals[layer], -1))
        columns = jnp.stack([inv, inv * inv * inv * cross / INNER], 1)
        g_gate, g_y, scaled, d_gain = gate_bwd(
            grad_scaled, y, gate_pre, columns, gated_gain[layer][None]
        )
        d_out = weight_grad(grad_low, scaled, blocks)
        d_z = weight_grad(normed, g_gate, blocks)
        g_x, g_bc, g_dt, acc_x, acc_bc, acc_head = scan_bwd(
            g_y, x_pre, bcdt_pre, kept, side, weights[layer]
        )
        d_x = weight_grad(normed, g_x, blocks)
        g_bcdt = jnp.concatenate([g_bc, g_dt], 1)

        def partial_rows(start):
            return (
                dot_t(half_of(g_gate, start), wf_z)
                + dot_t(half_of(g_x, start), wf_x)
                + dot_t(half_of(g_bcdt, start), wf_bcdt)
            )

        grad_normed = quarters.reduce(partial_rows)
        stream = streams[layer]
        rms = rms_of(stream)
        normal = stream * rms
        d_norm = jnp.sum(grad_normed * normal, 0)
        grown = grad_normed * gains[layer]
        grad_stream = grad_stream + rms * (
            grown - normal * jnp.mean(grown * normal, -1, keepdims=True)
        )
        if layer > 0:
            grad_low_own = grad_stream.astype(BF16)
            grad_low = quarters.join(grad_low_own)
        far_cols = lax.dynamic_slice_in_dim(g_bc, (1 - quarters.far) * STATE, STATE, 1)
        near_cols = lax.dynamic_slice_in_dim(g_bc, quarters.far * STATE, STATE, 1)
        bc_sum = near_cols.astype(F32) + swap(far_cols, "tensor", 2).astype(F32)
        bc_sum = bc_sum + swap(bc_sum.astype(BF16), "tensor", 1).astype(F32)
        rolled = jnp.roll(bc_sum, STATE // 2, 1)
        own_bc = jnp.where(quarters.core == 0, bc_sum, rolled)[:, : STATE // 2].astype(BF16)
        own_bcdt = jnp.concatenate([own_bc, g_dt[:, : STATE // 2]], 1)
        d_bcdt = weight_grad(normed, own_bcdt, blocks)
        weight_parts[layer] = (d_z, d_x, d_bcdt, d_out)
        small_parts[layer] = (d_norm, acc_x, acc_bc, acc_head, d_gain)

    d_hidden = quarters.join(dot_t(grad_stream.astype(BF16), order).astype(BF16)).astype(F32)

    norm_part = mm(
        jnp.stack([part[0] for part in small_parts]), order.astype(F32).T, PRECISE
    )
    pieces = []
    for layer in range(LAYERS):
        _, acc_x, acc_bc, acc_head, d_gain = small_parts[layer]
        skips = acc_head[0].reshape(heads, HEAD_DIM).sum(1)
        rates = -jnp.exp(a_log[layer])
        pieces.append(
            (
                acc_x[:5].reshape(-1),
                d_gain.reshape(-1),
                jnp.concatenate([acc_head[1, :heads], acc_head[2, :heads] * rates, skips]),
            )
        )
    shared = jnp.concatenate(
        [norm_part.reshape(-1)] + [small_parts[layer][2][:5].reshape(-1) for layer in range(LAYERS)]
    )
    flat = jnp.concatenate([tensor_sum(shared[None])[0]] + [v for piece in pieces for v in piece])
    flat = dp_sum(flat[None])[0]

    at = 0

    def take(*shape):
        nonlocal at
        size = 1
        for extent in shape:
            size *= extent
        values = flat[at : at + size].reshape(shape)
        at += size
        return values

    d_norm_gain = take(LAYERS, features)
    bc_acc = take(LAYERS, 5, 2 * STATE)
    x_acc, gain_acc, head_acc = [], [], []
    for layer in range(LAYERS):
        x_acc.append(take(5, width))
        gain_acc.append(take(width))
        head_acc.append(take(3, heads))
    x_acc = jnp.stack(x_acc)
    head_acc = jnp.stack(head_acc)
    stacked = [jnp.stack([weight_parts[layer][m] for layer in range(LAYERS)]) for m in range(4)]
    own_width = STATE // 2
    return (
        mixed,
        d_hidden,
        d_norm_gain,
        stacked[0],
        stacked[1],
        stacked[2][:, :, :own_width],
        stacked[2][:, :, own_width : own_width + heads],
        x_acc[:, :4],
        x_acc[:, 4],
        bc_acc[:, :4],
        bc_acc[:, 4],
        head_acc[:, 0],
        head_acc[:, 1],
        head_acc[:, 2],
        jnp.stack(gain_acc),
        stacked[3],
    )


def solution(mesh):
    in_specs = (
        P("dp", None),
        P("dp"),
        P(),
        P(None, "dp", "tensor"),
        P(None, "dp", "tensor"),
        P(None, "dp", None),
        P(None, "dp", "tensor"),
        P(None, None, "tensor"),
        P(None, "tensor"),
        P(),
        P(),
        P(None, "tensor"),
        P(None, "tensor"),
        P(None, "tensor"),
        P(None, "tensor"),
        P(None, "dp", "tensor"),
        P("dp", None),
    )
    out_specs = (
        P("dp", None),
        P("dp", None),
        P(),
        P(None, "dp", "tensor"),
        P(None, "dp", "tensor"),
        P(None, "dp", "tensor"),
        P(None, "dp", "tensor"),
        P(None, None, "tensor"),
        P(None, "tensor"),
        P(),
        P(),
        P(None, "tensor"),
        P(None, "tensor"),
        P(None, "tensor"),
        P(None, "tensor"),
        P(None, "dp", "tensor"),
    )
    return jax.shard_map(
        on_device, mesh=mesh, in_specs=in_specs, out_specs=out_specs, check_vma=False
    )
```

time: 2080 us -> 845 us (0.41)
  waiting for transfers between devices: 990 us -> 362 us
  blocking collectives: 208 us -> 0 us
  local copies, waits for them, and re-layouts: 253 us -> 45.2 us
  other arithmetic: 251 us -> 49.7 us
  matrix products: 332 us -> 138 us
  starting transfers between devices: 1.96 us -> 148 us
  Pallas kernels: 0 us -> 90.3 us
    reduce_scatter x6 -> x0, waiting for transfers between devices: 423 us -> none  [the longest x2 141 us: on_device(): lax.psum_scatter(grad_wz.astype(jnp.bfloat16), 'dp', scatter_dimension=0,...]
    psum x5 -> x0, waiting for transfers between devices: 385 us -> none  [the longest x3 385 us: head_reduce(): return lax.psum(partial_rows, 'tensor')]
    ppermute x0 -> x121, waiting for transfers between devices: none -> 362 us  [the longest x73 263 us: swap(): return lax.ppermute(values, axis, partners(lax.axis_size(axis), step))]
    dot_general x72 -> x46, matrix products: 332 us -> 138 us  [the longest x10 49.6 us: dot(): lax.dot_general(lhs, rhs, (((1,), (0,)), ((), ())), preferred_element_typ...]
    unnamed x25 -> x0, waiting for transfers between devices: 160 us -> none
    ppermute x0 -> x121, starting transfers between devices: none -> 148 us  [the longest x48 89.6 us: turn(): return lax.ppermute(values, 'dp', perm)]
    all_gather x4 -> x0, blocking collectives: 140 us -> none  [the longest x2 69.9 us: on_device(): lax.all_gather(w_bc[layer_idx], 'dp', axis=0, tiled=True)]
    pallas_call x0 -> x6, Pallas kernels: none -> 90.3 us  [the longest x2 53.2 us: scan_bwd(): pl.pallas_call(scan_bwd_kernel, grid=(chunks,), in_specs=in_specs, out_sp...]
  transfers between devices with their start and end apart: 21 -> 121, of which waited for: 13 -> 51; matrix products, arithmetic and copies ran while one was open for 26% -> 19% of each run, Pallas kernels for 0% -> 2%
where the time goes in v1:
time: 845 us; the launch traced here: 836 us
  waiting for transfers between devices  362 us (43%)
  starting transfers between devices  148 us (18%)
  matrix products  138 us (16%)
  Pallas kernels  90.3 us (11%)
  other arithmetic  49.7 us (6%)
  local copies, waits for them, and re-layouts  45.2 us (5%)
    ppermute x73, waiting for transfers between devices, swap(): return lax.ppermute(values, axis, partners(lax.axis_size(axis), step))  263 us
    ppermute x48, waiting for transfers between devices, turn(): return lax.ppermute(values, 'dp', perm)  98.7 us
    ppermute x48, starting transfers between devices, turn(): return lax.ppermute(values, 'dp', perm)  89.6 us
    ppermute x73, starting transfers between devices, swap(): return lax.ppermute(values, axis, partners(lax.axis_size(axis), step))  58.1 us
    pallas_call x2, Pallas kernels, scan_bwd(): pl.pallas_call(scan_bwd_kernel, grid=(chunks,), in_specs=in_specs, out_sp...  53.2 us
    dot_general x10, matrix products, dot(): lax.dot_general(lhs, rhs, (((1,), (0,)), ((), ())), preferred_element_typ...  49.6 us
    dot_general x18, matrix products, dot_t(): lax.dot_general(lhs, rhs, (((1,), (1,)), ((), ())), preferred_element_typ...  45.1 us
    unnamed x342, local copies, waits for them, and re-layouts  29.3 us
  transfers between devices with their start and end apart: 121, of which 51 were waited for; matrix products, arithmetic and copies ran while one was open for 19% of the time, Pallas kernels for 2%

profile of v1, /device:TPU:0, one launch (start us, length us, event | category | flops | bytes accessed | tf_op | source)
XLA Modules:
  0.0 836.5 jit_solution(1917435866408962421)
XLA Ops:
  23.0 7.7 fusion.13
  35.2 8.6 %fusion.23 = bf16[1536,1024]{1,0:T(8,128)(2,1)} fusion(bf16[1024,1536]{1,0:T(8,128)(2,1)} %param.33, s32[1536]{0:T(1024)S(1)} %copy-done.107, s32[1536]{0:T(1024)S(1)} %copy-done.110, s32[]{:T(128)S(6)} %select_n.222, s32[1536]{0:T(1024)S(1)} %copy-done.104, s32[1536]{0:T(1024)S(1)} %copy-done.113, s32[]{:T(128)S(6)} %add.365, ...), kind=kOutput, calls=%fused_computation.45 | convolution fusion | flops 4930142208 | bytes 6319112 | tf_op jit(solution)/shard_map/dot_general | solution.py:614
  74.4 8.8 %collective-permute-done.2 = bf16[192,768]{1,0:T(8,128)(2,1)S(1)} collective-permute-done((bf16[192,768]{1,0:T(8,128)(2,1)}, bf16[192,768]{1,0:T(8,128)(2,1)S(1)}, u32[]{:S(2)}, u32[]{:S(2)}) %collective-permute-start.2) | collective-permute-done | bytes 294944 | tf_op jit(solution)/shard_map/ppermute | solution.py:538
  101.1 12.7 %collective-permute-done.15 = bf16[192,768]{1,0:T(8,128)(2,1)S(1)} collective-permute-done((bf16[192,768]{1,0:T(8,128)(2,1)S(1)}, bf16[192,768]{1,0:T(8,128)(2,1)S(1)}, u32[]{:S(2)}, u32[]{:S(2)}) %collective-permute-start.15) | collective-permute-done | bytes 294944 | tf_op jit(solution)/shard_map/ppermute | solution.py:538
  116.1 7.6 collective-permute-done.19
  135.0 12.9 %scan_fwd.2 = (bf16[1024,768]{1,0:T(8,128)(2,1)S(1)}, f32[1024,768]{1,0:T(8,128)}, f32[8,1024]{1,0:T(8,128)S(1)}, bf16[8,128,768]{2,1,0:T(8,128)(2,1)S(1)}) custom-call(f32[1024,768]{1,0:T(8,128)} %fusion.214.refs_0_.x_ref.x_tail_ref, f32[1024,384]{1,0:T(8,128)S(1)} %fusion.212.refs_1_.bcdt_ref.bc_tail_ref, f32[1024,768]{1,0:T(8,128)} %fusion.210.refs_2_.gate_ref, ...), custom_call_target="tpu_custom_call" | custom-call | flops 1610612736 | bytes 12582912 | tf_op jit(solution)/shard_map/scan_fwd/pallas_call | solution.py:193
  150.8 7.1 collective-permute-done.27
  157.9 6.3 collective-permute-done.28
  201.9 8.2 collective-permute-start.50
  210.3 6.6 collective-permute-done.36
  221.2 7.1 collective-permute-done.48
  229.1 11.1 %collective-permute-done.49 = bf16[192,768]{1,0:T(8,128)(2,1)S(1)} collective-permute-done((bf16[192,768]{1,0:T(8,128)(2,1)S(1)}, bf16[192,768]{1,0:T(8,128)(2,1)S(1)}, u32[]{:S(2)}, u32[]{:S(2)}) %collective-permute-start.49) | collective-permute-done | bytes 294944 | tf_op jit(solution)/shard_map/ppermute | solution.py:538
  256.3 7.0 collective-permute-done.58
  283.0 6.3 collective-permute-done.61
  289.3 6.3 collective-permute-done.62
  313.5 13.3 %scan_fwd.3 = (bf16[1024,768]{1,0:T(8,128)(2,1)S(1)}, f32[1024,768]{1,0:T(8,128)}, f32[8,1024]{1,0:T(8,128)S(1)}, bf16[8,128,768]{2,1,0:T(8,128)(2,1)S(1)}) custom-call(f32[1024,768]{1,0:T(8,128)} %fusion.86.refs_0_.x_ref.x_tail_ref, f32[1024,384]{1,0:T(8,128)S(1)} %fusion.85.refs_1_.bcdt_ref.bc_tail_ref, f32[1024,768]{1,0:T(8,128)} %fusion.84.refs_2_.gate_ref, ...), custom_call_target="tpu_custom_call" | custom-call | flops 1610612736 | bytes 12582912 | tf_op jit(solution)/shard_map/scan_fwd/pallas_call | solution.py:193
  345.1 26.6 %scan_bwd.2 = (bf16[1024,768]{1,0:T(8,128)(2,1)S(1)}, bf16[1024,256]{1,0:T(8,128)(2,1)S(1)}, bf16[1024,128]{1,0:T(8,128)(2,1)S(1)}, f32[8,768]{1,0:T(8,128)S(1)}...) custom-call(bf16[1024,768]{1,0:T(8,128)(2,1)S(1)} %get-tuple-element.64.g_ref, f32[1024,768]{1,0:T(8,128)} %fusion.86.refs_0_.x_ref.x_tail_ref, ...), custom_call_target="tpu_custom_call" | custom-call | flops 4026531840 | bytes 12582912 | tf_op jit(solution)/shard_map/scan_bwd/pallas_call | solution.py:443
  398.9 39.2 %collective-permute-done.109 = bf16[768,128]{1,0:T(8,128)(2,1)S(1)} collective-permute-done((bf16[768,128]{1,0:T(8,128)(2,1)S(1)}, bf16[768,128]{1,0:T(8,128)(2,1)S(1)}, u32[]{:S(2)}, u32[]{:S(2)}) %collective-permute-start.109) | collective-permute-done | bytes 196640 | tf_op jit(solution)/shard_map/ppermute | solution.py:529
  458.1 17.0 %collective-permute-done.97 = bf16[768,768]{1,0:T(8,128)(2,1)S(1)} collective-permute-done((bf16[768,768]{1,0:T(8,128)(2,1)}, bf16[768,768]{1,0:T(8,128)(2,1)S(1)}, u32[]{:S(2)}, u32[]{:S(2)}) %collective-permute-start.97) | collective-permute-done | bytes 1179680 | tf_op jit(solution)/shard_map/ppermute | solution.py:529
  480.7 9.1 %collective-permute-done.90 = bf16[192,768]{1,0:T(8,128)(2,1)S(1)} collective-permute-done((bf16[192,768]{1,0:T(8,128)(2,1)S(1)}, bf16[192,768]{1,0:T(8,128)(2,1)S(1)}, u32[]{:S(2)}, u32[]{:S(2)}) %collective-permute-start.90) | collective-permute-done | bytes 294944 | tf_op jit(solution)/shard_map/ppermute | solution.py:538
  490.8 6.9 collective-permute-start.120
  503.1 14.1 %collective-permute-done.65 = bf16[256,1536]{0,1:T(8,128)(2,1)S(1)} collective-permute-done((bf16[256,1536]{0,1:T(8,128)(2,1)S(1)}, bf16[256,1536]{0,1:T(8,128)(2,1)S(1)}, u32[]{:S(2)}, u32[]{:S(2)}) %collective-permute-start.65) | collective-permute-done | bytes 786464 | tf_op jit(solution)/shard_map/ppermute | solution.py:529
  519.9 15.0 %collective-permute-done.71 = bf16[256,1536]{0,1:T(8,128)(2,1)S(1)} collective-permute-done((bf16[256,1536]{0,1:T(8,128)(2,1)S(1)}, bf16[256,1536]{0,1:T(8,128)(2,1)S(1)}, u32[]{:S(2)}, u32[]{:S(2)}) %collective-permute-start.71) | collective-permute-done | bytes 786464 | tf_op jit(solution)/shard_map/ppermute | solution.py:529
  552.5 9.8 %collective-permute-done.72 = bf16[256,1536]{0,1:T(8,128)(2,1)S(1)} collective-permute-done((bf16[256,1536]{0,1:T(8,128)(2,1)S(1)}, bf16[256,1536]{0,1:T(8,128)(2,1)S(1)}, u32[]{:S(2)}, u32[]{:S(2)}) %collective-permute-start.72) | collective-permute-done | bytes 786464 | tf_op jit(solution)/shard_map/ppermute | solution.py:529
  587.4 26.5 %scan_bwd.3 = (bf16[1024,768]{1,0:T(8,128)(2,1)S(1)}, bf16[1024,256]{1,0:T(8,128)(2,1)S(1)}, bf16[1024,128]{1,0:T(8,128)(2,1)S(1)}, f32[8,768]{1,0:T(8,128)S(1)}...) custom-call(bf16[1024,768]{1,0:T(8,128)(2,1)S(1)} %get-tuple-element.71.g_ref, ...), custom_call_target="tpu_custom_call" | custom-call | flops 4026531840 | bytes 12582912 | tf_op jit(solution)/shard_map/scan_bwd/pallas_call | solution.py:443
  640.9 43.4 %collective-permute-done.103 = bf16[768,128]{1,0:T(8,128)(2,1)S(1)} collective-permute-done((bf16[768,128]{1,0:T(8,128)(2,1)S(1)}, bf16[768,128]{1,0:T(8,128)(2,1)S(1)}, u32[]{:S(2)}, u32[]{:S(2)}) %collective-permute-start.103) | collective-permute-done | bytes 196640 | tf_op jit(solution)/shard_map/ppermute | solution.py:529
  705.2 14.5 %collective-permute-done.113 = bf16[768,768]{1,0:T(8,128)(2,1)} collective-permute-done((bf16[768,768]{1,0:T(8,128)(2,1)}, bf16[768,768]{1,0:T(8,128)(2,1)}, u32[]{:S(2)}, u32[]{:S(2)}) %collective-permute-start.113) | collective-permute-done | bytes 1179680 | tf_op jit(solution)/shard_map/ppermute | solution.py:529
  730.9 8.9 %collective-permute-start.115 = (bf16[192,768]{1,0:T(8,128)(2,1)S(1)}, bf16[192,768]{1,0:T(8,128)(2,1)S(1)}, u32[]{:S(2)}, u32[]{:S(2)}) collective-permute-start(bf16[192,768]{1,0:T(8,128)(2,1)S(1)} %get-tuple-element.188), channel_id=1, source_target_pairs={{0,4},{1,5},{2,6},{3,7},{4,0},{5,1},{6,2},{7,3},{8,12},{9,13},{10,... | collective-permute-start | bytes 884744 | tf_op jit(solution)/shard_map/ppermute | solution.py:538
  743.9 14.7 %collective-permute-done.95 = bf16[192,768]{1,0:T(8,128)(2,1)S(1)} collective-permute-done((bf16[192,768]{1,0:T(8,128)(2,1)S(1)}, bf16[192,768]{1,0:T(8,128)(2,1)S(1)}, u32[]{:S(2)}, u32[]{:S(2)}) %collective-permute-start.95) | collective-permute-done | bytes 294944 | tf_op jit(solution)/shard_map/ppermute | solution.py:538
  761.9 9.3 %collective-permute-done.115 = bf16[192,768]{1,0:T(8,128)(2,1)S(1)} collective-permute-done((bf16[192,768]{1,0:T(8,128)(2,1)S(1)}, bf16[192,768]{1,0:T(8,128)(2,1)S(1)}, u32[]{:S(2)}, u32[]{:S(2)}) %collective-permute-start.115) | collective-permute-done | bytes 294944 | tf_op jit(solution)/shard_map/ppermute | solution.py:538
  807.0 8.9 %collective-permute-done.78 = bf16[256,1536]{0,1:T(8,128)(2,1)S(1)} collective-permute-done((bf16[256,1536]{0,1:T(8,128)(2,1)S(1)}, bf16[256,1536]{0,1:T(8,128)(2,1)S(1)}, u32[]{:S(2)}, u32[]{:S(2)}) %collective-permute-start.78) | collective-permute-done | bytes 786464 | tf_op jit(solution)/shard_map/ppermute | solution.py:529
  829.3 6.7 copy.180
  (792 shorter events, 424.1 us)
Async XLA Ops:
  3.3 41.5 %collective-permute-start = (bf16[192,384]{1,0:T(8,128)(2,1)}, bf16[192,384]{1,0:T(8,128)(2,1)}, u32[]{:S(2)}, u32[]{:S(2)}) collective-permute-start(bf16[192,384]{1,0:T(8,128)(2,1)} %get-tuple-element.168), channel_id=1, source_target_pairs={{0,6},{1,7},{2,0},{3,1},{4,2},{5,3},{6,4},{7,5},{8,14},{9,15},{10,... | collective-permute-start | bytes 442376 | tf_op jit(solution)/shard_map/ppermute | solution.py:538
  8.4 40.0 %collective-permute-start.8 = (bf16[192,384]{1,0:T(8,128)(2,1)}, bf16[192,384]{1,0:T(8,128)(2,1)}, u32[]{:S(2)}, u32[]{:S(2)}) collective-permute-start(bf16[192,384]{1,0:T(8,128)(2,1)} %get-tuple-element.168), channel_id=1, source_target_pairs={{0,2},{1,3},{2,4},{3,5},{4,6},{5,7},{6,0},{7,1},{8,10},{9,11},{10,... | collective-permute-start | bytes 442376 | tf_op jit(solution)/shard_map/ppermute | solution.py:538
  8.4 43.3 %collective-permute-start.9 = (bf16[192,384]{1,0:T(8,128)(2,1)}, bf16[192,384]{1,0:T(8,128)(2,1)}, u32[]{:S(2)}, u32[]{:S(2)}) collective-permute-start(bf16[192,384]{1,0:T(8,128)(2,1)} %get-tuple-element.168), channel_id=1, source_target_pairs={{0,4},{1,5},{2,6},{3,7},{4,0},{5,1},{6,2},{7,3},{8,12},{9,13},{10,... | collective-permute-start | bytes 442376 | tf_op jit(solution)/shard_map/ppermute | solution.py:538
  9.4 44.8 %collective-permute-start.10 = (bf16[192,384]{1,0:T(8,128)(2,1)}, bf16[192,384]{1,0:T(8,128)(2,1)}, u32[]{:S(2)}, u32[]{:S(2)}) collective-permute-start(bf16[192,384]{1,0:T(8,128)(2,1)} %get-tuple-element.168), channel_id=1, source_target_pairs={{0,1},{1,0},{2,3},{3,2},{4,5},{5,4},{6,7},{7,6},{8,9},{9,8},{10,11... | collective-permute-start | bytes 442376 | tf_op jit(solution)/shard_map/ppermute | solution.py:529
  48.3 34.9 %collective-permute-start.2 = (bf16[192,768]{1,0:T(8,128)(2,1)}, bf16[192,768]{1,0:T(8,128)(2,1)S(1)}, u32[]{:S(2)}, u32[]{:S(2)}) collective-permute-start(bf16[192,768]{1,0:T(8,128)(2,1)} %get-tuple-element.51), channel_id=1, source_target_pairs={{0,4},{1,5},{2,6},{3,7},{4,0},{5,1},{6,2},{7,3},{8,12},{9,13},{10,... | collective-permute-start | bytes 884744 | tf_op jit(solution)/shard_map/ppermute | solution.py:538
  91.6 56.3 %collective-permute-start.23 = (bf16[192,768]{1,0:T(8,128)(2,1)S(1)}, bf16[192,768]{1,0:T(8,128)(2,1)S(1)}, u32[]{:S(2)}, u32[]{:S(2)}) collective-permute-start(bf16[192,768]{1,0:T(8,128)(2,1)S(1)} %copy-done.74), channel_id=1, source_target_pairs={{0,2},{1,3},{2,4},{3,5},{4,6},{5,7},{6,0},{7,1},{8,10},{9,11},{10,... | collective-permute-start | bytes 884744 | tf_op jit(solution)/shard_map/ppermute | solution.py:538
  96.2 52.3 %collective-permute-start.24 = (bf16[192,768]{1,0:T(8,128)(2,1)S(1)}, bf16[192,768]{1,0:T(8,128)(2,1)S(1)}, u32[]{:S(2)}, u32[]{:S(2)}) collective-permute-start(bf16[192,768]{1,0:T(8,128)(2,1)S(1)} %copy-done.74), channel_id=1, source_target_pairs={{0,4},{1,5},{2,6},{3,7},{4,0},{5,1},{6,2},{7,3},{8,12},{9,13},{10,... | collective-permute-start | bytes 884744 | tf_op jit(solution)/shard_map/ppermute | solution.py:538
  116.0 34.1 %collective-permute-start.25 = (bf16[192,768]{1,0:T(8,128)(2,1)S(1)}, bf16[192,768]{1,0:T(8,128)(2,1)S(1)}, u32[]{:S(2)}, u32[]{:S(2)}) collective-permute-start(bf16[192,768]{1,0:T(8,128)(2,1)S(1)} %copy-done.74), channel_id=1, source_target_pairs={{0,6},{1,7},{2,0},{3,1},{4,2},{5,3},{6,4},{7,5},{8,14},{9,15},{10,... | collective-permute-start | bytes 884744 | tf_op jit(solution)/shard_map/ppermute | solution.py:538
  216.9 37.2 %collective-permute-start.51 = (bf16[192,768]{1,0:T(8,128)(2,1)S(1)}, bf16[192,768]{1,0:T(8,128)(2,1)S(1)}, u32[]{:S(2)}, u32[]{:S(2)}) collective-permute-start(bf16[192,768]{1,0:T(8,128)(2,1)S(1)} %copy-done.73), channel_id=1, source_target_pairs={{0,1},{1,0},{2,3},{3,2},{4,5},{5,4},{6,7},{7,6},{8,9},{9,8},{10,11... | collective-permute-start | bytes 884744 | tf_op jit(solution)/shard_map/ppermute | solution.py:529
  219.2 29.1 %collective-permute-start.32 = (bf16[256,1536]{0,1:T(8,128)(2,1)S(1)}, bf16[256,1536]{0,1:T(8,128)(2,1)S(1)}, u32[]{:S(2)}, u32[]{:S(2)}) collective-permute-start(bf16[256,1536]{0,1:T(8,128)(2,1)S(1)} %multiply_convert_fusion), channel_id=1, source_target_pairs={{0,16},{8,24},{16,0},{24,8},{1,17},{9,25},{17,1},{25,9},{2,18},{10... | collective-permute-start | bytes 2359304 | tf_op jit(solution)/shard_map/ppermute | solution.py:529
  254.0 48.2 %collective-permute-start.33 = (bf16[512,1536]{0,1:T(8,128)(2,1)S(1)}, bf16[512,1536]{0,1:T(8,128)(2,1)S(1)}, u32[]{:S(2)}, u32[]{:S(2)}) collective-permute-start(bf16[512,1536]{0,1:T(8,128)(2,1)S(1)} %pad_maximum_fusion.4), channel_id=1, source_target_pairs={{0,8},{8,0},{16,24},{24,16},{1,9},{9,1},{17,25},{25,17},{2,10},{10... | collective-permute-start | bytes 4718600 | tf_op jit(solution)/shard_map/ppermute | solution.py:529
  381.5 67.0 %collective-permute-start.89 = (bf16[768,768]{1,0:T(8,128)(2,1)}, bf16[768,768]{1,0:T(8,128)(2,1)}, u32[]{:S(2)}, u32[]{:S(2)}) collective-permute-start(bf16[768,768]{1,0:T(8,128)(2,1)} %convolution_convert_fusion.6), channel_id=1, source_target_pairs={{0,1},{1,0},{2,3},{3,2},{4,5},{5,4},{6,7},{7,6},{8,9},{9,8},{10,11... | collective-permute-start | bytes 3538952 | tf_op jit(solution)/shard_map/ppermute | solution.py:529
  386.5 67.0 %collective-permute-start.117 = (bf16[768,768]{1,0:T(8,128)(2,1)}, bf16[768,768]{1,0:T(8,128)(2,1)}, u32[]{:S(2)}, u32[]{:S(2)}) collective-permute-start(bf16[768,768]{1,0:T(8,128)(2,1)} %fusion.64), channel_id=1, source_target_pairs={{0,1},{1,0},{2,3},{3,2},{4,5},{5,4},{6,7},{7,6},{8,9},{9,8},{10,11... | collective-permute-start | bytes 3538952 | tf_op jit(solution)/shard_map/ppermute | solution.py:529
  396.8 41.2 %collective-permute-start.109 = (bf16[768,128]{1,0:T(8,128)(2,1)S(1)}, bf16[768,128]{1,0:T(8,128)(2,1)S(1)}, u32[]{:S(2)}, u32[]{:S(2)}) collective-permute-start(bf16[768,128]{1,0:T(8,128)(2,1)S(1)} %convolution_convert_fusion.8), channel_id=1, source_target_pairs={{0,1},{1,0},{2,3},{3,2},{4,5},{5,4},{6,7},{7,6},{8,9},{9,8},{10,11... | collective-permute-start | bytes 589832 | tf_op jit(solution)/shard_map/ppermute | solution.py:529
  446.4 44.4 %collective-permute-start.64 = (bf16[512,1536]{0,1:T(8,128)(2,1)}, bf16[512,1536]{0,1:T(8,128)(2,1)S(1)}, u32[]{:S(2)}, u32[]{:S(2)}) collective-permute-start(bf16[512,1536]{0,1:T(8,128)(2,1)} %convolution_convert_fusion), channel_id=1, source_target_pairs={{0,8},{8,0},{16,24},{24,16},{1,9},{9,1},{17,25},{25,17},{2,10},{10... | collective-permute-start | bytes 4718600 | tf_op jit(solution)/shard_map/ppermute | solution.py:529
  446.4 53.0 %collective-permute-start.70 = (bf16[512,1536]{0,1:T(8,128)(2,1)}, bf16[512,1536]{0,1:T(8,128)(2,1)S(1)}, u32[]{:S(2)}, u32[]{:S(2)}) collective-permute-start(bf16[512,1536]{0,1:T(8,128)(2,1)} %fusion.34), channel_id=1, source_target_pairs={{0,8},{8,0},{16,24},{24,16},{1,9},{9,1},{17,25},{25,17},{2,10},{10... | collective-permute-start | bytes 4718600 | tf_op jit(solution)/shard_map/ppermute | solution.py:529
  478.6 59.6 %collective-permute-start.100 = (bf16[192,768]{1,0:T(8,128)(2,1)S(1)}, bf16[192,768]{1,0:T(8,128)(2,1)S(1)}, u32[]{:S(2)}, u32[]{:S(2)}) collective-permute-start(bf16[192,768]{1,0:T(8,128)(2,1)S(1)} %get-tuple-element.196), channel_id=1, source_target_pairs={{0,2},{1,3},{2,4},{3,5},{4,6},{5,7},{6,0},{7,1},{8,10},{9,11},{10,... | collective-permute-start | bytes 884744 | tf_op jit(solution)/shard_map/ppermute | solution.py:538
  478.7 61.0 %collective-permute-start.99 = (bf16[192,768]{1,0:T(8,128)(2,1)S(1)}, bf16[192,768]{1,0:T(8,128)(2,1)S(1)}, u32[]{:S(2)}, u32[]{:S(2)}) collective-permute-start(bf16[192,768]{1,0:T(8,128)(2,1)S(1)} %get-tuple-element.197), channel_id=1, source_target_pairs={{0,4},{1,5},{2,6},{3,7},{4,0},{5,1},{6,2},{7,3},{8,12},{9,13},{10,... | collective-permute-start | bytes 884744 | tf_op jit(solution)/shard_map/ppermute | solution.py:538
  489.8 52.9 %collective-permute-start.98 = (bf16[192,768]{1,0:T(8,128)(2,1)S(1)}, bf16[192,768]{1,0:T(8,128)(2,1)S(1)}, u32[]{:S(2)}, u32[]{:S(2)}) collective-permute-start(bf16[192,768]{1,0:T(8,128)(2,1)S(1)} %get-tuple-element.195), channel_id=1, source_target_pairs={{0,6},{1,7},{2,0},{3,1},{4,2},{5,3},{6,4},{7,5},{8,14},{9,15},{10,... | collective-permute-start | bytes 884744 | tf_op jit(solution)/shard_map/ppermute | solution.py:538
  490.8 73.1 %collective-permute-start.120 = (bf16[192,768]{1,0:T(8,128)(2,1)S(1)}, bf16[192,768]{1,0:T(8,128)(2,1)S(1)}, u32[]{:S(2)}, u32[]{:S(2)}) collective-permute-start(bf16[192,768]{1,0:T(8,128)(2,1)S(1)} %get-tuple-element.190), channel_id=1, source_target_pairs={{0,2},{1,3},{2,4},{3,5},{4,6},{5,7},{6,0},{7,1},{8,10},{9,11},{10,... | collective-permute-start | bytes 884744 | tf_op jit(solution)/shard_map/ppermute | solution.py:538
  626.6 68.3 %collective-permute-start.85 = (bf16[768,768]{1,0:T(8,128)(2,1)}, bf16[768,768]{1,0:T(8,128)(2,1)}, u32[]{:S(2)}, u32[]{:S(2)}) collective-permute-start(bf16[768,768]{1,0:T(8,128)(2,1)} %convolution_convert_fusion.7), channel_id=1, source_target_pairs={{0,1},{1,0},{2,3},{3,2},{4,5},{5,4},{6,7},{7,6},{8,9},{9,8},{10,11... | collective-permute-start | bytes 3538952 | tf_op jit(solution)/shard_map/ppermute | solution.py:529
  627.3 74.3 %collective-permute-start.93 = (bf16[768,768]{1,0:T(8,128)(2,1)}, bf16[768,768]{1,0:T(8,128)(2,1)}, u32[]{:S(2)}, u32[]{:S(2)}) collective-permute-start(bf16[768,768]{1,0:T(8,128)(2,1)} %convolution_convert_fusion.5), channel_id=1, source_target_pairs={{0,1},{1,0},{2,3},{3,2},{4,5},{5,4},{6,7},{7,6},{8,9},{9,8},{10,11... | collective-permute-start | bytes 3538952 | tf_op jit(solution)/shard_map/ppermute | solution.py:529
  640.1 44.2 %collective-permute-start.103 = (bf16[768,128]{1,0:T(8,128)(2,1)S(1)}, bf16[768,128]{1,0:T(8,128)(2,1)S(1)}, u32[]{:S(2)}, u32[]{:S(2)}) collective-permute-start(bf16[768,128]{1,0:T(8,128)(2,1)S(1)} %fusion.81), channel_id=1, source_target_pairs={{0,1},{1,0},{2,3},{3,2},{4,5},{5,4},{6,7},{7,6},{8,9},{9,8},{10,11... | collective-permute-start | bytes 589832 | tf_op jit(solution)/shard_map/ppermute | solution.py:529
  691.1 31.7 %collective-permute-start.76 = (bf16[512,1536]{0,1:T(8,128)(2,1)}, bf16[512,1536]{0,1:T(8,128)(2,1)}, u32[]{:S(2)}, u32[]{:S(2)}) collective-permute-start(bf16[512,1536]{0,1:T(8,128)(2,1)} %fusion.33), channel_id=1, source_target_pairs={{0,8},{8,0},{16,24},{24,16},{1,9},{9,1},{17,25},{25,17},{2,10},{10... | collective-permute-start | bytes 4718600 | tf_op jit(solution)/shard_map/ppermute | solution.py:529
  698.2 28.9 %collective-permute-start.88 = (bf16[192,768]{1,0:T(8,128)(2,1)S(1)}, bf16[192,768]{1,0:T(8,128)(2,1)S(1)}, u32[]{:S(2)}, u32[]{:S(2)}) collective-permute-start(bf16[192,768]{1,0:T(8,128)(2,1)S(1)} %get-tuple-element.199), channel_id=1, source_target_pairs={{0,2},{1,3},{2,4},{3,5},{4,6},{5,7},{6,0},{7,1},{8,10},{9,11},{10,... | collective-permute-start | bytes 884744 | tf_op jit(solution)/shard_map/ppermute | solution.py:538
  698.9 31.9 %collective-permute-start.87 = (bf16[192,768]{1,0:T(8,128)(2,1)S(1)}, bf16[192,768]{1,0:T(8,128)(2,1)S(1)}, u32[]{:S(2)}, u32[]{:S(2)}) collective-permute-start(bf16[192,768]{1,0:T(8,128)(2,1)S(1)} %get-tuple-element.200), channel_id=1, source_target_pairs={{0,4},{1,5},{2,6},{3,7},{4,0},{5,1},{6,2},{7,3},{8,12},{9,13},{10,... | collective-permute-start | bytes 884744 | tf_op jit(solution)/shard_map/ppermute | solution.py:538
  701.6 29.3 %collective-permute-start.86 = (bf16[192,768]{1,0:T(8,128)(2,1)S(1)}, bf16[192,768]{1,0:T(8,128)(2,1)S(1)}, u32[]{:S(2)}, u32[]{:S(2)}) collective-permute-start(bf16[192,768]{1,0:T(8,128)(2,1)S(1)} %get-tuple-element.198), channel_id=1, source_target_pairs={{0,6},{1,7},{2,0},{3,1},{4,2},{5,3},{6,4},{7,5},{8,14},{9,15},{10,... | collective-permute-start | bytes 884744 | tf_op jit(solution)/shard_map/ppermute | solution.py:538
  722.7 35.9 %collective-permute-start.95 = (bf16[192,768]{1,0:T(8,128)(2,1)S(1)}, bf16[192,768]{1,0:T(8,128)(2,1)S(1)}, u32[]{:S(2)}, u32[]{:S(2)}) collective-permute-start(bf16[192,768]{1,0:T(8,128)(2,1)S(1)} %get-tuple-element.194), channel_id=1, source_target_pairs={{0,4},{1,5},{2,6},{3,7},{4,0},{5,1},{6,2},{7,3},{8,12},{9,13},{10,... | collective-permute-start | bytes 884744 | tf_op jit(solution)/shard_map/ppermute | solution.py:538
  727.1 33.8 %collective-permute-start.94 = (bf16[192,768]{1,0:T(8,128)(2,1)S(1)}, bf16[192,768]{1,0:T(8,128)(2,1)S(1)}, u32[]{:S(2)}, u32[]{:S(2)}) collective-permute-start(bf16[192,768]{1,0:T(8,128)(2,1)S(1)} %get-tuple-element.192), channel_id=1, source_target_pairs={{0,6},{1,7},{2,0},{3,1},{4,2},{5,3},{6,4},{7,5},{8,14},{9,15},{10,... | collective-permute-start | bytes 884744 | tf_op jit(solution)/shard_map/ppermute | solution.py:538
  730.8 31.1 %collective-permute-start.116 = (bf16[192,768]{1,0:T(8,128)(2,1)S(1)}, bf16[192,768]{1,0:T(8,128)(2,1)S(1)}, u32[]{:S(2)}, u32[]{:S(2)}) collective-permute-start(bf16[192,768]{1,0:T(8,128)(2,1)S(1)} %get-tuple-element.187), channel_id=1, source_target_pairs={{0,2},{1,3},{2,4},{3,5},{4,6},{5,7},{6,0},{7,1},{8,10},{9,11},{10,... | collective-permute-start | bytes 884744 | tf_op jit(solution)/shard_map/ppermute | solution.py:538
  730.9 40.4 %collective-permute-start.115 = (bf16[192,768]{1,0:T(8,128)(2,1)S(1)}, bf16[192,768]{1,0:T(8,128)(2,1)S(1)}, u32[]{:S(2)}, u32[]{:S(2)}) collective-permute-start(bf16[192,768]{1,0:T(8,128)(2,1)S(1)} %get-tuple-element.188), channel_id=1, source_target_pairs={{0,4},{1,5},{2,6},{3,7},{4,0},{5,1},{6,2},{7,3},{8,12},{9,13},{10,... | collective-permute-start | bytes 884744 | tf_op jit(solution)/shard_map/ppermute | solution.py:538
  739.8 31.5 %collective-permute-start.114 = (bf16[192,768]{1,0:T(8,128)(2,1)S(1)}, bf16[192,768]{1,0:T(8,128)(2,1)S(1)}, u32[]{:S(2)}, u32[]{:S(2)}) collective-permute-start(bf16[192,768]{1,0:T(8,128)(2,1)S(1)} %get-tuple-element.186), channel_id=1, source_target_pairs={{0,6},{1,7},{2,0},{3,1},{4,2},{5,3},{6,4},{7,5},{8,14},{9,15},{10,... | collective-permute-start | bytes 884744 | tf_op jit(solution)/shard_map/ppermute | solution.py:538
  (227 other events, 3762.3 us)

commit v2 on v1

--- a/solution.py
+++ b/solution.py
@@ -78,7 +78,7 @@
 
 
 def scan_fwd_kernel(
-    with_cross,
+    me_ref,
     x_ref,
     bcdt_ref,
     gate_ref,
@@ -92,12 +92,14 @@
     skip_ref,
     gain_ref,
     spread_ref,
-    *rest,
+    u_ref,
+    y_ref,
+    sq_ref,
+    kept_ref,
+    state,
+    tail_x,
+    tail_bc,
 ):
-    if with_cross:
-        gs_ref, u_ref, y_ref, sq_ref, kept_ref, state, tail_x, tail_bc = rest
-    else:
-        u_ref, y_ref, sq_ref, kept_ref, state, tail_x, tail_bc = rest
     width = x_ref.shape[1]
 
     @pl.when(pl.program_id(0) == 0)
@@ -128,7 +130,6 @@
     carried = mm(c_low, state_low)
     low_lanes = iota((CHUNK, LANES), 1) < HEAD_DIM
     squares = jnp.zeros((CHUNK, LANES), F32)
-    crosses = jnp.zeros((CHUNK, LANES), F32)
     for pair in range(width // LANES):
         at = slice(pair * LANES, (pair + 1) * LANES)
         now = x_ref[:, at]
@@ -151,76 +152,71 @@
         grown = gated * gain_ref[:, at]
         u_ref[:, at] = grown.astype(BF16)
         squares = squares + gated * gated
-        if with_cross:
-            crosses = crosses + grown * gs_ref[:, at].astype(F32)
     ones = jnp.ones((8, LANES), F32)
     sums = lax.dot_general(
         ones, squares, (((1,), (1,)), ((), ())), precision=PRECISE, preferred_element_type=F32
     )
-    if with_cross:
-        more = lax.dot_general(
-            ones, crosses, (((1,), (1,)), ((), ())), precision=PRECISE, preferred_element_type=F32
-        )
-        sums = jnp.where(iota((8, CHUNK), 0) == 0, sums, more)
     sq_ref[...] = sums
 
 
 def whole(shape):
-    return pl.BlockSpec(shape, lambda c: (0,) * len(shape))
-
-
-def scan_fwd(x_pre, bcdt_pre, gate_pre, side, weights, gs=None, y_dtype=F32):
+    return pl.BlockSpec(shape, lambda *_: (0,) * len(shape))
+
+
+def place_of(chunk, chunks, me_ref):
+    part = chunks // 4
+    return (chunk // part ^ me_ref[0]) * part + chunk % part
+
+
+def scan_fwd(me, x_pre, bcdt_pre, gate_pre, side, weights):
     length, width = x_pre.shape
     chunks = length // CHUNK
     aux, seg_rows = side
-    taps, bias, bc_taps, bc_bias, head, skip, gain, spread = weights
-    tile = lambda columns: pl.BlockSpec((CHUNK, columns), lambda c: (c, 0))
+    at = lambda c, m: (place_of(c, chunks, m), 0)
+    tile = lambda columns: pl.BlockSpec((CHUNK, columns), at)
     in_specs = [
         tile(width),
         tile(bcdt_pre.shape[1]),
         tile(width),
-        tile(LANES),
-        pl.BlockSpec((1, 1, CHUNK), lambda c: (c, 0, 0)),
+        pl.BlockSpec((CHUNK, LANES), lambda c, m: (c, 0)),
+        pl.BlockSpec((1, 1, CHUNK), lambda c, m: (c, 0, 0)),
     ] + [whole(w.shape) for w in weights]
-    args = [x_pre, bcdt_pre, gate_pre, aux, seg_rows, *weights]
-    if gs is not None:
-        in_specs.append(tile(width))
-        args.append(gs)
-
-    def kernel(*refs):
-        scan_fwd_kernel(gs is not None, *refs)
-
     return pl.pallas_call(
-        kernel,
-        grid=(chunks,),
-        in_specs=in_specs,
-        out_specs=[
-            tile(width),
-            tile(width),
-            pl.BlockSpec((8, CHUNK), lambda c: (0, c)),
-            pl.BlockSpec((1, STATE, width), lambda c: (c, 0, 0)),
-        ],
+        scan_fwd_kernel,
+        grid_spec=pltpu.PrefetchScalarGridSpec(
+            num_scalar_prefetch=1,
+            grid=(chunks,),
+            in_specs=in_specs,
+            out_specs=[
+                tile(width),
+                tile(width),
+                pl.BlockSpec((8, CHUNK), lambda c, m: (0, c)),
+                pl.BlockSpec((1, STATE, width), lambda c, m: (c, 0, 0)),
+            ],
+            scratch_shapes=[
+                pltpu.VMEM((STATE, width), F32),
+                pltpu.VMEM((TAIL, width), F32),
+                pltpu.VMEM((TAIL, 2 * STATE), F32),
+            ],
+        ),
         out_shape=[
             jax.ShapeDtypeStruct((length, width), BF16),
-            jax.ShapeDtypeStruct((length, width), y_dtype),
+            jax.ShapeDtypeStruct((length, width), F32),
             jax.ShapeDtypeStruct((8, length), F32),
             jax.ShapeDtypeStruct((chunks, STATE, width), BF16),
         ],
-        scratch_shapes=[
-            pltpu.VMEM((STATE, width), F32),
-            pltpu.VMEM((TAIL, width), F32),
-            pltpu.VMEM((TAIL, 2 * STATE), F32),
-        ],
         compiler_params=pltpu.CompilerParams(vmem_limit_bytes=VMEM_BYTES),
         cost_estimate=pl.CostEstimate(
-            flops=16 * length * width * LANES, bytes_accessed=16 * length * width, transcendentals=0
+            flops=140 * length * width * LANES,
+            bytes_accessed=20 * length * width,
+            transcendentals=0,
         ),
         name="scan_fwd",
-    )(*args)
+    )(me, x_pre, bcdt_pre, gate_pre, aux, seg_rows, *weights)
 
 
 def gate_bwd_kernel(
-    gs_ref, y_ref, gate_ref, col_ref, gain_ref, g_gate_ref, g_y_ref, scaled_ref, d_gain_ref
+    me_ref, gs_ref, y_ref, gate_ref, col_ref, gain_ref, g_gate_ref, g_y_ref, d_gain_ref
 ):
     @pl.when(pl.program_id(0) == 0)
     def _():
@@ -236,37 +232,41 @@
         sig = jax.nn.sigmoid(gate)
         act = gate * sig
         gated = y * act
-        normal = gated * inv
-        gain = gain_ref[:, at]
-        d_gain_ref[:, at] += jnp.sum(gs * normal, 0, keepdims=True)
-        g_gated = inv * (gs * gain) - gated * pull
-        scaled_ref[:, at] = (normal * gain).astype(BF16)
+        grown = gs * inv
+        d_gain_ref[:, at] += jnp.sum(grown * gated, 0, keepdims=True)
+        g_gated = grown * gain_ref[:, at] - gated * pull
         g_y_ref[:, at] = (g_gated * act).astype(BF16)
         g_gate_ref[:, at] = (g_gated * y * sig * (1.0 + gate * (1.0 - sig))).astype(BF16)
 
 
-def gate_bwd(gs, y, gate_pre, columns, gain, rows=256):
+def gate_bwd(me, gs, y, gate_pre, columns, gain):
     length, width = gs.shape
-    tile = pl.BlockSpec((rows, width), lambda c: (c, 0))
+    rows = length // 4
+    tile = pl.BlockSpec((rows, width), lambda p, m: (p, 0))
     return pl.pallas_call(
         gate_bwd_kernel,
-        grid=(length // rows,),
-        in_specs=[
-            tile,
-            tile,
-            tile,
-            pl.BlockSpec((rows, columns.shape[1]), lambda c: (c, 0)),
-            whole(gain.shape),
-        ],
-        out_specs=[tile, tile, tile, whole((1, width))],
-        out_shape=[jax.ShapeDtypeStruct((length, width), BF16)] * 3
+        grid_spec=pltpu.PrefetchScalarGridSpec(
+            num_scalar_prefetch=1,
+            grid=(4,),
+            in_specs=[
+                tile,
+                tile,
+                tile,
+                pl.BlockSpec((rows, columns.shape[1]), lambda p, m: (p ^ m[0], 0)),
+                whole(gain.shape),
+            ],
+            out_specs=[tile, tile, whole((1, width))],
+        ),
+        out_shape=[jax.ShapeDtypeStruct((length, width), BF16)] * 2
         + [jax.ShapeDtypeStruct((1, width), F32)],
         compiler_params=pltpu.CompilerParams(vmem_limit_bytes=VMEM_BYTES),
         cost_estimate=pl.CostEstimate(
-            flops=20 * length * width, bytes_accessed=18 * length * width, transcendentals=0
+            flops=50 * length * width * LANES,
+            bytes_accessed=18 * length * width,
+            transcendentals=0,
         ),
         name="gate_bwd",
-    )(gs, y, gate_pre, columns, gain)
+    )(me, gs, y, gate_pre, columns, gain)
 
 
 def conv_bwd(joined, joined_grad, grad, taps, aux, acc_ref, at):
@@ -282,6 +282,7 @@
 
 
 def scan_bwd_kernel(
+    me_ref,
     g_ref,
     x_ref,
     x_tail_ref,
@@ -420,15 +421,19 @@
     ).astype(BF16)
 
 
-def scan_bwd(g_y, x_pre, bcdt_pre, kept, side, weights):
+def scan_bwd(me, g_y, x_pre, bcdt_pre, kept, side, weights):
     length, width = x_pre.shape
     chunks = length // CHUNK
     aux, seg_rows = side
     back = lambda c: chunks - 1 - c
-    tile = lambda columns: pl.BlockSpec((CHUNK, columns), lambda c: (back(c), 0))
-    tail = lambda columns: pl.BlockSpec(
-        (TAIL, columns), lambda c: (jnp.maximum(back(c) * (CHUNK // TAIL) - 1, 0), 0)
-    )
+    place = lambda c, m: place_of(back(c), chunks, m)
+    tile = lambda columns: pl.BlockSpec((CHUNK, columns), lambda c, m: (place(c, m), 0))
+
+    def tail_at(c, m):
+        before = place_of(jnp.maximum(back(c) - 1, 0), chunks, m)
+        return (before * (CHUNK // TAIL) + CHUNK // TAIL - 1, 0)
+
+    tail = lambda columns: pl.BlockSpec((TAIL, columns), tail_at)
     wide = bcdt_pre.shape[1]
     in_specs = [
         tile(width),
@@ -436,22 +441,30 @@
         tail(width),
         tile(wide),
         tail(wide),
-        pl.BlockSpec((1, STATE, width), lambda c: (back(c), 0, 0)),
-        tile(LANES),
-        pl.BlockSpec((1, 1, CHUNK), lambda c: (back(c), 0, 0)),
+        pl.BlockSpec((1, STATE, width), lambda c, m: (back(c), 0, 0)),
+        pl.BlockSpec((CHUNK, LANES), lambda c, m: (back(c), 0)),
+        pl.BlockSpec((1, 1, CHUNK), lambda c, m: (back(c), 0, 0)),
     ] + [whole(w.shape) for w in weights]
     return pl.pallas_call(
         scan_bwd_kernel,
-        grid=(chunks,),
-        in_specs=in_specs,
-        out_specs=[
-            tile(width),
-            tile(2 * STATE),
-            tile(LANES),
-            whole((8, width)),
-            whole((8, 2 * STATE)),
-            whole((8, width)),
-        ],
+        grid_spec=pltpu.PrefetchScalarGridSpec(
+            num_scalar_prefetch=1,
+            grid=(chunks,),
+            in_specs=in_specs,
+            out_specs=[
+                tile(width),
+                tile(2 * STATE),
+                tile(LANES),
+                whole((8, width)),
+                whole((8, 2 * STATE)),
+                whole((8, width)),
+            ],
+            scratch_shapes=[
+                pltpu.VMEM((STATE, width), F32),
+                pltpu.VMEM((TAIL, width), F32),
+                pltpu.VMEM((TAIL, 2 * STATE), F32),
+            ],
+        ),
         out_shape=[
             jax.ShapeDtypeStruct((length, width), BF16),
             jax.ShapeDtypeStruct((length, 2 * STATE), BF16),
@@ -460,17 +473,14 @@
             jax.ShapeDtypeStruct((8, 2 * STATE), F32),
             jax.ShapeDtypeStruct((8, width), F32),
         ],
-        scratch_shapes=[
-            pltpu.VMEM((STATE, width), F32),
-            pltpu.VMEM((TAIL, width), F32),
-            pltpu.VMEM((TAIL, 2 * STATE), F32),
-        ],
         compiler_params=pltpu.CompilerParams(vmem_limit_bytes=VMEM_BYTES),
         cost_estimate=pl.CostEstimate(
-            flops=40 * length * width * LANES, bytes_accessed=16 * length * width, transcendentals=0
+            flops=280 * length * width * LANES,
+            bytes_accessed=20 * length * width,
+            transcendentals=0,
         ),
         name="scan_bwd",
-    )(g_y, x_pre, x_pre, bcdt_pre, bcdt_pre, kept, aux, seg_rows, *weights)
+    )(me, g_y, x_pre, x_pre, bcdt_pre, bcdt_pre, kept, aux, seg_rows, *weights)
 
 
 def side_arrays(segments):
@@ -529,72 +539,78 @@
     return lax.ppermute(values, axis, partners(lax.axis_size(axis), step))
 
 
-def turn(values, blocks, ahead):
-    perm = [
-        (2 * block + side, 2 * ((block + ahead) % blocks) + side)
-        for block in range(blocks)
-        for side in range(2)
-    ]
-    return lax.ppermute(values, "dp", perm)
-
-
 def after(values, *earlier):
     return lax.optimization_barrier((values, *earlier))[0]
 
 
-def gather_rows(own, blocks):
-    slots = [own] + [turn(own, blocks, ahead) for ahead in range(1, blocks)]
-    across = [swap(slot, "dp", 1) for slot in slots]
-    return jnp.concatenate(slots + across, 0), slots[-1]
-
-
-def scatter_rows(left_part, right_part, blocks):
-    height = left_part.shape[0] // blocks
-    mine = right_part.astype(F32) + swap(left_part, "dp", 1).astype(F32)
-    total = mine[:height]
-    low = mine.astype(BF16)
-    for ahead in range(1, blocks):
-        piece = low[ahead * height : (ahead + 1) * height]
-        total = total + turn(piece, blocks, blocks - ahead).astype(F32)
-    return total
-
-
-def weight_grad(rows, grads, blocks):
+def dp_masks():
+    masks = []
+    step = lax.axis_size("dp") // 2
+    while step > 0:
+        masks.append(step)
+        step = step // 2
+    return masks
+
+
+def offsets(masks):
+    found = [0]
+    for mask in masks:
+        found = found + [offset ^ mask for offset in found]
+    return found
+
+
+def spread_stage(rows, mask):
+    got = swap(rows, "dp", mask)
+    return jnp.concatenate([rows, got], 0), got
+
+
+def gather_rows(own, masks):
+    stages = []
+    rows = own
+    for mask in masks:
+        rows, got = spread_stage(rows, mask)
+        stages.append(got)
+    return rows, stages
+
+
+def scatter_first(kept, got):
+    total = kept + got.astype(F32)
+    height = total.shape[0] // 2
+    return total[:height], total[height:].astype(BF16)
+
+
+def scatter_rest(kept, sent, masks):
+    for mask in reversed(masks[1:-1]):
+        kept, sent = scatter_first(kept, swap(sent, "dp", mask))
+    return kept + swap(sent, "dp", masks[0]).astype(F32)
+
+
+def grad_half(rows, grads, which):
     width = rows.shape[1] // 2
     dims = (((0,), (0,)), ((), ()))
-    sent = lax.dot_general(rows[:, width:], grads, dims, preferred_element_type=F32).astype(BF16)
-    kept = lax.dot_general(rows[:, :width], grads, dims, preferred_element_type=F32)
-    return scatter_rows(sent, kept, blocks)
-
-
-class Quarters:
-    def __init__(self, length):
-        place = lax.axis_index("tensor")
-        self.core = place % 2
-        self.far = place // 2
-        self.half = length // 2
-        self.size = length // 4
-
-    def own(self, values):
-        start = self.core * self.half + self.far * self.size
-        return lax.dynamic_slice_in_dim(values, start, self.size, 0)
-
-    def reduce(self, make):
-        sent = make((1 - self.core) * self.half).astype(BF16)
-        got = swap(sent, "tensor", 1)
-        mine = make(self.core * self.half) + got.astype(F32)
-        away = lax.dynamic_slice_in_dim(mine, (1 - self.far) * self.size, self.size, 0)
-        got = swap(away.astype(BF16), "tensor", 2)
-        near = lax.dynamic_slice_in_dim(mine, self.far * self.size, self.size, 0)
-        return near + got.astype(F32)
-
-    def join(self, values):
-        got = swap(values, "tensor", 2)
-        first = self.far == 0
-        half = jnp.concatenate([jnp.where(first, values, got), jnp.where(first, got, values)], 0)
-        got = swap(half, "tensor", 1)
-        first = self.core == 0
-        return jnp.concatenate([jnp.where(first, half, got), jnp.where(first, got, half)], 0)
+    taken = rows[:, which * width : (which + 1) * width]
+    return lax.dot_general(taken, grads, dims, preferred_element_type=F32)
+
+
+def sent_half(rows, grads):
+    return grad_half(rows, grads, 1).astype(BF16)
+
+
+def reordered(values, me):
+    size = values.shape[0] // 4
+    return jnp.concatenate(
+        [lax.dynamic_slice_in_dim(values, (part ^ me) * size, size, 0) for part in range(4)], 0
+    )
+
+
+def turned_over(values, size):
+    shaped = values.reshape(-1, 2, size, values.shape[1])
+    return shaped[:, ::-1].reshape(values.shape)
+
+
+def own_quarter(values, me):
+    size = values.shape[0] // 4
+    return lax.dynamic_slice_in_dim(values, me * size, size, 0)
 
 
 def tensor_sum(values):
@@ -618,16 +634,21 @@
     return lax.dot_general(lhs, rhs, (((1,), (1,)), ((), ())), preferred_element_type=F32)
 
 
-def turned_order(features, blocks):
+def own_order(features, masks):
     place = lax.axis_index("dp")
-    block, side = place // 2, place % 2
-    height = features // (2 * blocks)
-    index = lax.broadcasted_iota(jnp.int32, (features, features), 1)
+    found = offsets(masks)
+    height = features // len(found)
+    index = lax.broadcasted_iota(jnp.int32, (1, features), 1)
     part, within = index // height, index % height
-    source_side = lax.rem(side + part // blocks, 2)
-    source_block = lax.rem(block + blocks - part % blocks, blocks)
-    source = (2 * source_block + source_side) * height + within
+    away = jnp.zeros_like(part)
+    for position, offset in enumerate(found):
+        away = jnp.where(part == position, offset, away)
+    source = (away ^ place) * height + within
     return (lax.broadcasted_iota(jnp.int32, (features, features), 0) == source).astype(BF16)
+
+
+def rms_of(stream):
+    return lax.rsqrt(jnp.mean(stream * stream, -1, keepdims=True) + EPSILON)
 
 
 def on_device(
@@ -652,22 +673,65 @@
     length, features = hidden.shape
     width = w_x.shape[2]
     heads = dt_bias.shape[1]
-    blocks = lax.axis_size("dp") // 2
-    quarters = Quarters(length)
-    order = turned_order(features, blocks)
-
-    w_bcdt = jnp.concatenate([w_bc, in_groups(w_dt)], 2)
-    gathered = []
-    earlier = None
-    for layer in range(LAYERS):
-        row = []
-        for group in (w_bcdt[layer], w_x[layer], w_z[layer], w_out[layer]):
-            if earlier is not None:
-                group = after(group, earlier)
-            full, earlier = gather_rows(group, blocks)
-            row.append(full)
-        gathered.append(row)
-
+    masks = dp_masks()
+    place = lax.axis_index("tensor")
+    core, far = place % 2, place // 2
+    me = 2 * core + far
+    me_row = me.astype(jnp.int32)[None]
+    half = length // 2
+    quarter = length // 4
+
+    side_first = masks[-1:] + masks[:-1]
+    seated = [offsets(side_first).index(offset) for offset in offsets(masks)]
+    height = w_x.shape[1]
+    quart_bc = w_bc.shape[2] // 4
+    own_bc = lax.dynamic_slice_in_dim(w_bc, place * quart_bc, quart_bc, 2)
+    w_small = jnp.concatenate([own_bc[0], own_bc[1], w_dt[0], w_dt[1]], 1)
+    w_small = jnp.pad(w_small, ((0, 0), (0, 2 * LANES - w_small.shape[1])))
+
+    far_stage, near_stage = {}, {}
+
+    def gathered(name, own, over):
+        rows, stages = gather_rows(own, over)
+        far_stage[name], near_stage[name] = stages[0], stages[-1 if over is not masks else -2]
+        return rows
+
+    early = swap(w_out[1], "dp", 1)
+    x_rows = gathered("x0", w_x[0], masks)
+    small_rows = gathered("small", after(w_small, near_stage["x0"]), masks)
+    z_rows = gathered("z0", after(w_z[0], near_stage["x0"]), masks)
+    out_rows = gathered("out0", after(w_out[0], far_stage["z0"]), masks)
+    x_rows = [x_rows, gathered("x1", after(w_x[1], far_stage["out0"]), masks)]
+    z_rows = [z_rows, gathered("z1", after(w_z[1], far_stage["x1"]), masks)]
+    both_sides = after(jnp.concatenate([w_out[1], early], 0), far_stage["z1"])
+    rows = gathered("out1", both_sides, masks[:-1])
+    rows = [rows[seat * height : (seat + 1) * height] for seat in seated]
+    out_rows = [out_rows, jnp.concatenate(rows, 0)]
+
+    own_cols = small_rows[:, :LANES]
+    across = swap(own_cols, "tensor", 2)
+    beside = swap(jnp.concatenate([own_cols, across], 1), "tensor", 1)
+
+    def small_columns(layer):
+        low = layer * quart_bc
+        parts = [
+            own_cols[:, low : low + quart_bc],
+            across[:, low : low + quart_bc],
+            beside[:, low : low + quart_bc],
+            beside[:, LANES + low : LANES + low + quart_bc],
+        ]
+        first = core == 0
+        near = [jnp.where(first, parts[0], parts[2]), jnp.where(first, parts[2], parts[0])]
+        away = [jnp.where(first, parts[1], parts[3]), jnp.where(first, parts[3], parts[1])]
+        first = far == 0
+        ordered = [jnp.where(first, n, a) for n, a in zip(near, away)]
+        ordered += [jnp.where(first, a, n) for n, a in zip(near, away)]
+        at = LANES + layer * heads
+        return jnp.concatenate(ordered + [in_groups(small_rows[:, at : at + heads])], 1)
+
+    bcdt_rows = [small_columns(layer) for layer in range(LAYERS)]
+
+    order = lax.optimization_barrier(own_order(features, masks))
     side = side_arrays(segments)
     spread = spread_matrix(width)
     weights = [
@@ -684,93 +748,190 @@
         )
         for layer in range(LAYERS)
     ]
-    gains = mm(norm_gain, order.astype(F32), PRECISE)
-    hidden_low = dot(hidden, order).astype(BF16)
-    cotangent_low = dot(cotangent, order).astype(BF16)
-
-    def rms_of(stream):
-        return lax.rsqrt(jnp.mean(stream * stream, -1, keepdims=True) + EPSILON)
-
-    def half_of(values, start):
-        return lax.dynamic_slice_in_dim(values, start, quarters.half, 0)
-
-    streams, totals, saved = [], [], []
-    stream_full = hidden_low.astype(F32)
-    normed = (stream_full * rms_of(stream_full) * gains[0]).astype(BF16)
-    stream = quarters.own(hidden_low).astype(F32)
-    for layer in range(LAYERS):
-        wf_bcdt, wf_x, wf_z, wf_out = gathered[layer]
-        bcdt_pre = dot(normed, wf_bcdt)
-        x_pre = dot(normed, wf_x)
-        gate_pre = dot(normed, wf_z)
-        u, y, sq, kept = scan_fwd(x_pre, bcdt_pre, gate_pre, side, weights[layer])
-        inv = lax.rsqrt(tensor_sum(sq[0:1]) / INNER + EPSILON)[0]
-        total = quarters.reduce(lambda start: dot_t(half_of(u, start), wf_out))
-        streams.append(stream)
-        totals.append(total)
-        saved.append((normed, x_pre, bcdt_pre, gate_pre, u, y, kept, inv))
-        stream = stream + quarters.own(inv)[:, None] * total
-        if layer + 1 < LAYERS:
-            normed_own = (stream * rms_of(stream) * gains[layer + 1]).astype(BF16)
-            normed = quarters.join(normed_own)
-    mixed = quarters.join(dot_t(stream.astype(BF16), order).astype(BF16))
-
-    grad_low = cotangent_low
-    grad_stream = quarters.own(cotangent_low).astype(F32)
-    weight_parts = [None] * LAYERS
-    small_parts = [None] * LAYERS
-    for layer in reversed(range(LAYERS)):
-        wf_bcdt, wf_x, wf_z, wf_out = gathered[layer]
-        normed, x_pre, bcdt_pre, gate_pre, u, y, kept, inv = saved[layer]
-        grad_scaled = dot(grad_low, wf_out)
-        if layer + 1 == LAYERS:
-            cross = jnp.sum(grad_scaled * u.astype(F32), -1)
-            cross = tensor_sum(cross[None])[0]
-        else:
-            cross = quarters.join(jnp.sum(grad_low_own.astype(F32) * totals[layer], -1))
-        columns = jnp.stack([inv, inv * inv * inv * cross / INNER], 1)
-        g_gate, g_y, scaled, d_gain = gate_bwd(
-            grad_scaled, y, gate_pre, columns, gated_gain[layer][None]
+    order, side, weights = lax.optimization_barrier((order, side, weights))
+    hidden_now = after(reordered(hidden, me), far_stage["x0"], early)
+    hidden_low = dot(hidden_now, order).astype(BF16)
+    cotangent_now = after(reordered(cotangent, me), near_stage["x0"], hidden_low)
+    cotangent_low = dot(cotangent_now, order).astype(BF16)
+    gains = mm(after(norm_gain, near_stage["x0"]), order.astype(F32), PRECISE)
+    hidden_low, cotangent_low, gains, _, _ = lax.optimization_barrier(
+        (hidden_low, cotangent_low, gains, far_stage["small"], far_stage["z0"])
+    )
+
+    def columns_of(values, which):
+        return lax.dynamic_slice_in_dim(values, which * STATE, STATE, 1)
+
+    stream = hidden_low.astype(F32)
+    normed0 = (stream * rms_of(stream) * gains[0]).astype(BF16)
+    stream0 = hidden_low[:quarter].astype(F32)
+    x_pre0 = dot(after(normed0, near_stage["small"]), x_rows[0])
+    bcdt_pre0 = dot(after(normed0, near_stage["z0"], far_stage["out0"]), bcdt_rows[0])
+    gate_pre0 = dot(after(normed0, near_stage["out0"], far_stage["x1"]), z_rows[0])
+    gate_pre0 = after(gate_pre0, near_stage["x1"], far_stage["z1"])
+    u0, y0, sq, kept0 = scan_fwd(me_row, x_pre0, bcdt_pre0, gate_pre0, side, weights[0])
+    u_now = after(u0, near_stage["z1"])
+    sent = dot_t(u_now[half:], out_rows[0]).astype(BF16)
+    sq = sq[0:1]
+    sq = sq + swap(sq, "tensor", 1)
+    u_now = after(u_now, sent, sq)
+    mine = dot_t(u_now[:half], out_rows[0]) + swap(sent, "tensor", 1).astype(F32)
+    sq = sq + swap(sq, "tensor", 2)
+    away = after(mine[quarter:].astype(BF16), sq)
+    got = swap(away, "tensor", 2)
+    inv0 = lax.rsqrt(sq / INNER + EPSILON)[0]
+    total0 = mine[:quarter] + got.astype(F32)
+    stream1 = stream0 + own_quarter(inv0, me)[:, None] * total0
+    normed_own = (stream1 * rms_of(stream1) * gains[1]).astype(BF16)
+    normed_own = after(normed_own, far_stage["out1"])
+    normed_half = jnp.concatenate([normed_own, swap(normed_own, "tensor", 2)], 0)
+    normed1 = jnp.concatenate([normed_half, swap(normed_half, "tensor", 1)], 0)
+    scaled0 = (u0.astype(F32) * reordered(inv0, me)[:, None]).astype(BF16)
+
+    x_pre1 = dot(normed1, x_rows[1])
+    bcdt_pre1 = dot(normed1, bcdt_rows[1])
+    gate_pre1 = dot(after(normed1, near_stage["out1"]), z_rows[1])
+    u1, y1, sq, kept1 = scan_fwd(me_row, x_pre1, bcdt_pre1, gate_pre1, side, weights[1])
+    scaled_grad1 = dot(cotangent_low, out_rows[1])
+    cross = reordered(jnp.sum(scaled_grad1 * u1.astype(F32), -1), me)
+    both = tensor_sum(jnp.stack([sq[0], cross]))
+    mixed_sent = dot_t(u1[half:], out_rows[1]).astype(BF16)
+    mixed_mine = dot_t(u1[:half], out_rows[1])
+    mixed_mine = mixed_mine + swap(mixed_sent, "tensor", 1).astype(F32)
+    both = after(both, mixed_sent, mixed_mine)
+    mixed_got = swap(mixed_mine[quarter:].astype(BF16), "tensor", 2)
+    inv1 = lax.rsqrt(both[0] / INNER + EPSILON)
+
+    columns = jnp.stack([inv1, inv1 * inv1 * inv1 * both[1] / INNER], 1)
+    g_gate1, g_y, d_gain1 = gate_bwd(
+        me_row, scaled_grad1, y1, gate_pre1, columns, gated_gain[1][None]
+    )
+    z_sent = sent_half(normed1, g_gate1)
+    z_got = swap(z_sent, "dp", 1)
+    scaled1 = (u1.astype(F32) * reordered(inv1, me)[:, None]).astype(BF16)
+    out_sent = sent_half(cotangent_low, scaled1)
+    out_got = swap(out_sent, "dp", 1)
+    g_y = after(g_y, z_sent, out_sent)
+    g_x1, g_bc1, g_dt1, acc_x1, acc_bc1, acc_head1 = scan_bwd(
+        me_row, g_y, x_pre1, bcdt_pre1, kept1, side, weights[1]
+    )
+    g_x1 = after(g_x1, z_got, mixed_got)
+
+    def grad_rows(rows, g_gate, g_x, g_bcdt, layer):
+        return (
+            dot_t(g_gate[rows], z_rows[layer])
+            + dot_t(g_x[rows], x_rows[layer])
+            + dot_t(g_bcdt[rows], bcdt_rows[layer])
         )
-        d_out = weight_grad(grad_low, scaled, blocks)
-        d_z = weight_grad(normed, g_gate, blocks)
-        g_x, g_bc, g_dt, acc_x, acc_bc, acc_head = scan_bwd(
-            g_y, x_pre, bcdt_pre, kept, side, weights[layer]
-        )
-        d_x = weight_grad(normed, g_x, blocks)
-        g_bcdt = jnp.concatenate([g_bc, g_dt], 1)
-
-        def partial_rows(start):
-            return (
-                dot_t(half_of(g_gate, start), wf_z)
-                + dot_t(half_of(g_x, start), wf_x)
-                + dot_t(half_of(g_bcdt, start), wf_bcdt)
-            )
-
-        grad_normed = quarters.reduce(partial_rows)
-        stream = streams[layer]
-        rms = rms_of(stream)
-        normal = stream * rms
-        d_norm = jnp.sum(grad_normed * normal, 0)
-        grown = grad_normed * gains[layer]
-        grad_stream = grad_stream + rms * (
-            grown - normal * jnp.mean(grown * normal, -1, keepdims=True)
-        )
-        if layer > 0:
-            grad_low_own = grad_stream.astype(BF16)
-            grad_low = quarters.join(grad_low_own)
-        far_cols = lax.dynamic_slice_in_dim(g_bc, (1 - quarters.far) * STATE, STATE, 1)
-        near_cols = lax.dynamic_slice_in_dim(g_bc, quarters.far * STATE, STATE, 1)
-        bc_sum = near_cols.astype(F32) + swap(far_cols, "tensor", 2).astype(F32)
-        bc_sum = bc_sum + swap(bc_sum.astype(BF16), "tensor", 1).astype(F32)
-        rolled = jnp.roll(bc_sum, STATE // 2, 1)
-        own_bc = jnp.where(quarters.core == 0, bc_sum, rolled)[:, : STATE // 2].astype(BF16)
-        own_bcdt = jnp.concatenate([own_bc, g_dt[:, : STATE // 2]], 1)
-        d_bcdt = weight_grad(normed, own_bcdt, blocks)
-        weight_parts[layer] = (d_z, d_x, d_bcdt, d_out)
-        small_parts[layer] = (d_norm, acc_x, acc_bc, acc_head, d_gain)
-
-    d_hidden = quarters.join(dot_t(grad_stream.astype(BF16), order).astype(BF16)).astype(F32)
+
+    g_bcdt = jnp.concatenate([g_bc1, g_dt1], 1)
+    sent = grad_rows(slice(half, length), g_gate1, g_x1, g_bcdt, 1).astype(BF16)
+    own = grad_rows(slice(0, half), after(g_gate1, sent), g_x1, g_bcdt, 1)
+    mine = own + swap(sent, "tensor", 1).astype(F32)
+    away = mine[quarter:].astype(BF16)
+    got = swap(away, "tensor", 2)
+    normed_now, cotangent_now, _ = lax.optimization_barrier((normed1, cotangent_low, away))
+    z_kept, z_next = scatter_first(grad_half(normed_now, g_gate1, 0), z_got)
+    x_got = swap(sent_half(normed_now, g_x1), "dp", 1)
+    out_kept, out_next = scatter_first(grad_half(cotangent_now, scaled1, 0), out_got)
+    x_kept_half = grad_half(normed_now, g_x1, 0)
+    total = mine[:quarter] + got.astype(F32)
+    rms = rms_of(stream1)
+    normal = stream1 * rms
+    d_norm1 = jnp.sum(total * normal, 0)
+    grown = total * gains[1]
+    grad_stream = cotangent_low[:quarter].astype(F32) + rms * (
+        grown - normal * jnp.mean(grown * normal, -1, keepdims=True)
+    )
+    grad_own = grad_stream.astype(BF16)
+    cross = jnp.sum(grad_own.astype(F32) * total0, -1)
+    grad_half_rows = jnp.concatenate([grad_own, swap(grad_own, "tensor", 2)], 0)
+    cross = jnp.concatenate([cross, swap(cross, "tensor", 2)], 0)
+    grad_half_rows, cross = lax.optimization_barrier((grad_half_rows, cross))
+    grad0 = jnp.concatenate([grad_half_rows, swap(grad_half_rows, "tensor", 1)], 0)
+    cross = reordered(jnp.concatenate([cross, swap(cross, "tensor", 1)], 0), me)
+    x_kept, x_next = scatter_first(x_kept_half, x_got)
+    x_next = after(x_next, grad0)
+    x_near = swap(x_next, "dp", masks[-2])
+
+    out_sent0 = sent_half(grad0, scaled0)
+    out_got0 = swap(out_sent0, "dp", 1)
+    scaled_grad0 = dot(after(grad0, out_sent0), out_rows[0])
+    columns = jnp.stack([inv0, inv0 * inv0 * inv0 * cross / INNER], 1)
+    g_gate0, g_y, d_gain0 = gate_bwd(
+        me_row, scaled_grad0, y0, gate_pre0, columns, gated_gain[0][None]
+    )
+    z_sent0 = sent_half(normed0, g_gate0)
+    z_got0 = swap(z_sent0, "dp", 1)
+    d_z1 = scatter_rest(z_kept, z_next, masks)
+    mixed_total = mixed_mine[:quarter] + mixed_got.astype(F32)
+    last = stream1 + own_quarter(inv1, me)[:, None] * mixed_total
+    last = after(last, grad0)
+    mixed_own = dot_t(last.astype(BF16), order).astype(BF16)
+    mixed_half = jnp.concatenate([mixed_own, swap(mixed_own, "tensor", 2)], 0)
+    g_y = after(g_y, z_sent0, mixed_own, x_near)
+    g_x0, g_bc0, g_dt0, acc_x0, acc_bc0, acc_head0 = scan_bwd(
+        me_row, g_y, x_pre0, bcdt_pre0, kept0, side, weights[0]
+    )
+    away1 = after(columns_of(g_bc1, 1 - far), grad0)
+    away1 = swap(away1, "tensor", 2)
+    away0 = swap(columns_of(g_bc0, 1 - far), "tensor", 2)
+    g_x0 = after(g_x0, out_got0, mixed_half, away1)
+    x_sent0 = sent_half(normed0, g_x0)
+    x_got0 = swap(x_sent0, "dp", 1)
+    g_x0 = after(g_x0, x_sent0)
+    g_bcdt = jnp.concatenate([g_bc0, g_dt0], 1)
+    sent = grad_rows(slice(half, length), g_gate0, g_x0, g_bcdt, 0).astype(BF16)
+    own = grad_rows(slice(0, half), after(g_gate0, sent), g_x0, g_bcdt, 0)
+    mine = own + swap(sent, "tensor", 1).astype(F32)
+    away = mine[quarter:].astype(BF16)
+    got = swap(away, "tensor", 2)
+    normed_now, grad_now, _ = lax.optimization_barrier((normed0, grad0, away))
+    z_kept0, z_next0 = scatter_first(grad_half(normed_now, g_gate0, 0), z_got0)
+    out_kept0, out_next0 = scatter_first(grad_half(grad_now, scaled0, 0), out_got0)
+    x_kept0, x_next0 = scatter_first(grad_half(normed_now, g_x0, 0), x_got0)
+    total = mine[:quarter] + got.astype(F32)
+    rms = rms_of(stream0)
+    normal = stream0 * rms
+    d_norm0 = jnp.sum(total * normal, 0)
+    grown = total * gains[0]
+    grad_stream = grad_stream + rms * (
+        grown - normal * jnp.mean(grown * normal, -1, keepdims=True)
+    )
+    d_hidden = dot_t(grad_stream.astype(BF16), order).astype(BF16)
+    d_hidden = jnp.concatenate([d_hidden, swap(d_hidden, "tensor", 2)], 0)
+    d_hidden = jnp.concatenate([d_hidden, swap(d_hidden, "tensor", 1)], 0)
+    d_hidden = reordered(d_hidden, me).astype(F32)
+    mixed = jnp.concatenate([mixed_half, swap(mixed_half, "tensor", 1)], 0)
+    mixed = reordered(mixed, me)
+
+    d_out1 = scatter_rest(out_kept, out_next, masks)
+    d_x1 = scatter_rest(*scatter_first(x_kept, x_near), masks[:1] + masks[2:])
+    d_out0 = scatter_rest(out_kept0, out_next0, masks)
+    d_z0 = scatter_rest(z_kept0, z_next0, masks)
+    d_x0 = scatter_rest(x_kept0, x_next0, masks)
+
+    near_cols = jnp.concatenate([columns_of(v, far) for v in (g_bc0, g_bc1)], 1)
+    away_cols = jnp.concatenate([away0, away1], 1)
+    bc_sum = near_cols.astype(F32) + turned_over(away_cols, quarter).astype(F32)
+    across_sum = swap(after(bc_sum.astype(BF16), away), "tensor", 1)
+    bc_sum = bc_sum + turned_over(across_sum, half).astype(F32)
+    small_sent, small_kept = [], []
+    for layer, (rows, g_dt) in enumerate(((normed0, g_dt0), (normed1, g_dt1))):
+        summed = bc_sum[:, layer * STATE : (layer + 1) * STATE]
+        rolled = jnp.roll(summed, STATE // 2, 1)
+        own_cols = jnp.where(core == 0, summed, rolled)[:, : STATE // 2].astype(BF16)
+        own_cols = jnp.concatenate([own_cols, g_dt[:, : STATE // 2]], 1)
+        small_sent.append(sent_half(rows, own_cols))
+        small_kept.append(grad_half(rows, own_cols, 0))
+    small_sent = after(jnp.concatenate(small_sent, 1), x_got0)
+    small_got = swap(small_sent, "dp", 1)
+    small_kept, small_next = scatter_first(jnp.concatenate(small_kept, 1), small_got)
+    d_small = scatter_rest(small_kept, small_next, masks)
+    d_small = jnp.stack([d_small[:, layer * LANES : (layer + 1) * LANES] for layer in range(LAYERS)])
+    small_parts = [
+        (d_norm0, acc_x0, acc_bc0, acc_head0, d_gain0),
+        (d_norm1, acc_x1, acc_bc1, acc_head1, d_gain1),
+    ]
 
     norm_part = mm(
         jnp.stack([part[0] for part in small_parts]), order.astype(F32).T, PRECISE
@@ -813,16 +974,15 @@
         head_acc.append(take(3, heads))
     x_acc = jnp.stack(x_acc)
     head_acc = jnp.stack(head_acc)
-    stacked = [jnp.stack([weight_parts[layer][m] for layer in range(LAYERS)]) for m in range(4)]
     own_width = STATE // 2
     return (
         mixed,
         d_hidden,
         d_norm_gain,
-        stacked[0],
-        stacked[1],
-        stacked[2][:, :, :own_width],
-        stacked[2][:, :, own_width : own_width + heads],
+        jnp.stack([d_z0, d_z1]),
+        jnp.stack([d_x0, d_x1]),
+        d_small[:, :, :own_width],
+        d_small[:, :, own_width : own_width + heads],
         x_acc[:, :4],
         x_acc[:, 4],
         bc_acc[:, :4],
@@ -831,7 +991,7 @@
         head_acc[:, 1],
         head_acc[:, 2],
         jnp.stack(gain_acc),
-        stacked[3],
+        jnp.stack([d_out0, d_out1]),
     )
 
 

time: 845 us -> 634 us (0.75)
  waiting for transfers between devices: 362 us -> 193 us
  starting transfers between devices: 148 us -> 66.7 us
  other arithmetic: 49.7 us -> 73.2 us
  local copies, waits for them, and re-layouts: 45.2 us -> 65.6 us
    ppermute x48 -> x0, waiting for transfers between devices: 98.7 us -> none  [turn(): return lax.ppermute(values, 'dp', perm)]
    ppermute x48 -> x0, starting transfers between devices: 89.6 us -> none  [turn(): return lax.ppermute(values, 'dp', perm)]
    ppermute x73 -> x74, waiting for transfers between devices: 263 us -> 193 us  [swap(): return lax.ppermute(values, axis, partners(lax.axis_size(axis), step))]
    concatenate x7 -> x31, other arithmetic: 7.54 us -> 32.2 us  [the longest x13 10.9 us: spread_stage(): return (jnp.concatenate([rows, got], 0), got)]
    slice x13 -> x27, local copies, waits for them, and re-layouts: 0.69 us -> 11 us  [the longest x14 6.36 us: scatter_first(): return (total[:height], total[height:].astype(BF16))]
    ppermute x73 -> x74, starting transfers between devices: 58.1 us -> 66.7 us  [swap(): return lax.ppermute(values, axis, partners(lax.axis_size(axis), step))]
    unnamed x342 -> x334, local copies, waits for them, and re-layouts: 29.3 us -> 29.6 us
  transfers between devices with their start and end apart: 121 -> 74, of which waited for: 51 -> 33; matrix products, arithmetic and copies ran while one was open for 19% -> 35% of each run, Pallas kernels for 2% -> 12%
where the time goes in v2:
time: 634 us; the launch traced here: 624 us
  waiting for transfers between devices  193 us (30%)
  matrix products  131 us (21%)
  Pallas kernels  90.6 us (14%)
  other arithmetic  73.2 us (12%)
  starting transfers between devices  66.7 us (11%)
  local copies, waits for them, and re-layouts  65.6 us (10%)
    ppermute x74, waiting for transfers between devices, swap(): return lax.ppermute(values, axis, partners(lax.axis_size(axis), step))  193 us
    ppermute x74, starting transfers between devices, swap(): return lax.ppermute(values, axis, partners(lax.axis_size(axis), step))  66.7 us
    pallas_call x2, Pallas kernels, scan_bwd(): pl.pallas_call(scan_bwd_kernel, grid_spec=pltpu.PrefetchScalarGridSpec(nu...  53 us
    dot_general x18, matrix products, dot_t(): lax.dot_general(lhs, rhs, (((1,), (1,)), ((), ())), preferred_element_typ...  46.1 us
    dot_general x10, matrix products, dot(): lax.dot_general(lhs, rhs, (((1,), (0,)), ((), ())), preferred_element_typ...  45.3 us
    dot_general x16, matrix products, grad_half(): return lax.dot_general(taken, grads, dims, preferred_element_type=F32)  34.3 us
    unnamed x334, local copies, waits for them, and re-layouts  29.6 us
    pallas_call x2, Pallas kernels, scan_fwd(): pl.pallas_call(scan_fwd_kernel, grid_spec=pltpu.PrefetchScalarGridSpec(nu...  26.9 us
  transfers between devices with their start and end apart: 74, of which 33 were waited for; matrix products, arithmetic and copies ran while one was open for 35% of the time, Pallas kernels for 12%

profile of v2, /device:TPU:0, one launch (start us, length us, event | category | flops | bytes accessed | tf_op | source)
XLA Modules:
  0.0 624.3 jit_solution(15744527322781578708)
XLA Ops:
  17.1 4.3 fusion
  30.8 8.2 %convolution_convert_fusion.1 = bf16[1024,1536]{1,0:T(8,128)(2,1)S(1)} fusion(bf16[1024,1536]{1,0:T(8,128)(2,1)} %pad_maximum_fusion, bf16[1536,1536]{1,0:T(8,128)(2,1)} %fusion), kind=kOutput, calls=%fused_computation.10 | convolution fusion | flops 4833411072 | bytes 11010048 | tf_op jit(solution)/shard_map/dot_general | solution.py:630
  39.0 4.7 collective-permute-done.2
  49.3 6.5 %convolution_convert_fusion = bf16[1024,1536]{1,0:T(8,128)(2,1)} fusion(bf16[1024,1536]{1,0:T(8,128)(2,1)S(1)} %copy-done.67, bf16[1536,1536]{1,0:T(8,128)(2,1)S(1)} %bitcast.197), kind=kOutput, calls=%fused_computation.9 | convolution fusion | flops 4833411072 | bytes 11010048 | tf_op jit(solution)/shard_map/dot_general | solution.py:630
  89.0 5.0 collective-permute-done.13
  95.5 7.6 %collective-permute-done.7 = bf16[384,768]{1,0:T(8,128)(2,1)} collective-permute-done((bf16[384,768]{1,0:T(8,128)(2,1)}, bf16[384,768]{1,0:T(8,128)(2,1)}, u32[]{:S(2)}, u32[]{:S(2)}) %collective-permute-start.7) | collective-permute-done | bytes 589856 | tf_op jit(solution)/shard_map/ppermute | solution.py:539
  110.1 5.7 collective-permute-done.12
  119.4 5.7 fusion.162.x_ref.x_tail_ref
  127.8 6.6 %collective-permute-done.14 = bf16[768,768]{1,0:T(8,128)(2,1)S(1)} collective-permute-done((bf16[768,768]{1,0:T(8,128)(2,1)S(1)}, bf16[768,768]{1,0:T(8,128)(2,1)S(1)}, u32[]{:S(2)}, u32[]{:S(2)}) %collective-permute-start.14) | collective-permute-done | bytes 1179680 | tf_op jit(solution)/shard_map/ppermute | solution.py:539
  134.5 4.3 fusion.179.gate_ref
  138.9 13.4 %scan_fwd.2 = (bf16[1024,768]{1,0:T(8,128)(2,1)S(1)}, f32[1024,768]{1,0:T(8,128)}, f32[8,1024]{1,0:T(8,128)S(1)}, bf16[8,128,768]{2,1,0:T(8,128)(2,1)S(1)}) custom-call(s32[1]{0:T(128)} %bitcast.30.me_ref, f32[1024,768]{1,0:T(8,128)} %fusion.162.x_ref.x_tail_ref, f32[1024,384]{1,0:T(8,128)S(1)} %fusion.178.bcdt_ref.bc_tail_ref, ...), custom_call_target="tpu_custom_call" | custom-call | flops 14092861440 | bytes 15728640 | tf_op jit(solution)/shard_map/scan_fwd/pallas_call | solution.py:184
  152.3 6.3 %collective-permute-done.20 = bf16[768,768]{1,0:T(8,128)(2,1)S(1)} collective-permute-done((bf16[768,768]{1,0:T(8,128)(2,1)S(1)}, bf16[768,768]{1,0:T(8,128)(2,1)S(1)}, u32[]{:S(2)}, u32[]{:S(2)}) %collective-permute-start.20) | collective-permute-done | bytes 1179680 | tf_op jit(solution)/shard_map/ppermute | solution.py:539
  178.4 16.1 %collective-permute-done.23 = bf16[384,768]{1,0:T(8,128)(2,1)S(1)} collective-permute-done((bf16[384,768]{1,0:T(8,128)(2,1)S(1)}, bf16[384,768]{1,0:T(8,128)(2,1)S(1)}, u32[]{:S(2)}, u32[]{:S(2)}) %collective-permute-start.23) | collective-permute-done | bytes 589856 | tf_op jit(solution)/shard_map/ppermute | solution.py:539
  199.8 22.4 %collective-permute-done.27 = bf16[768,768]{1,0:T(8,128)(2,1)S(1)} collective-permute-done((bf16[768,768]{1,0:T(8,128)(2,1)S(1)}, bf16[768,768]{1,0:T(8,128)(2,1)S(1)}, u32[]{:S(2)}, u32[]{:S(2)}) %collective-permute-start.27) | collective-permute-done | bytes 1179680 | tf_op jit(solution)/shard_map/ppermute | solution.py:539
  227.8 4.3 fusion.180.x_ref.x_tail_ref
  232.1 4.2 fusion.182.gate_ref
  236.3 13.5 %scan_fwd.3 = (bf16[1024,768]{1,0:T(8,128)(2,1)S(1)}, f32[1024,768]{1,0:T(8,128)}, f32[8,1024]{1,0:T(8,128)S(1)}, bf16[8,128,768]{2,1,0:T(8,128)(2,1)S(1)}) custom-call(s32[1]{0:T(128)} %bitcast.30.me_ref, f32[1024,768]{1,0:T(8,128)} %fusion.180.x_ref.x_tail_ref, f32[1024,384]{1,0:T(8,128)S(1)} %fusion.181.bcdt_ref.bc_tail_ref, ...), custom_call_target="tpu_custom_call" | custom-call | flops 14092861440 | bytes 15728640 | tf_op jit(solution)/shard_map/scan_fwd/pallas_call | solution.py:184
  252.9 4.4 fusion.10
  267.6 5.5 gate_bwd.2
  280.1 26.4 %scan_bwd.2 = (bf16[1024,768]{1,0:T(8,128)(2,1)S(1)}, bf16[1024,256]{1,0:T(8,128)(2,1)S(1)}, bf16[1024,128]{1,0:T(8,128)(2,1)S(1)}, f32[8,768]{1,0:T(8,128)S(1)}...) custom-call(s32[1]{0:T(128)} %bitcast.30.me_ref, bf16[1024,768]{1,0:T(8,128)(2,1)S(1)} %get-tuple-element.150.g_ref, ...), custom_call_target="tpu_custom_call" | custom-call | flops 28185722880 | bytes 15728640 | tf_op jit(solution)/shard_map/scan_bwd/pallas_call | solution.py:448
  309.5 20.6 %collective-permute-done.33 = bf16[768,768]{1,0:T(8,128)(2,1)S(1)} collective-permute-done((bf16[768,768]{1,0:T(8,128)(2,1)S(1)}, bf16[768,768]{1,0:T(8,128)(2,1)S(1)}, u32[]{:S(2)}, u32[]{:S(2)}) %collective-permute-start.33) | collective-permute-done | bytes 1179680 | tf_op jit(solution)/shard_map/ppermute | solution.py:539
  356.1 9.7 %collective-permute-done.35 = bf16[256,1536]{1,0:T(8,128)(2,1)S(1)} collective-permute-done((bf16[256,1536]{1,0:T(8,128)(2,1)S(1)}, bf16[256,1536]{1,0:T(8,128)(2,1)S(1)}, u32[]{:S(2)}, u32[]{:S(2)}) %collective-permute-start.35) | collective-permute-done | bytes 786464 | tf_op jit(solution)/shard_map/ppermute | solution.py:539
  371.3 14.1 %collective-permute-done.72 = bf16[384,768]{1,0:T(8,128)(2,1)S(1)} collective-permute-done((bf16[384,768]{1,0:T(8,128)(2,1)S(1)}, bf16[384,768]{1,0:T(8,128)(2,1)S(1)}, u32[]{:S(2)}, u32[]{:S(2)}) %collective-permute-start.72) | collective-permute-done | bytes 589856 | tf_op jit(solution)/shard_map/ppermute | solution.py:539
  389.7 11.3 %collective-permute-done.73 = bf16[192,768]{1,0:T(8,128)(2,1)S(1)} collective-permute-done((bf16[192,768]{1,0:T(8,128)(2,1)S(1)}, bf16[192,768]{1,0:T(8,128)(2,1)S(1)}, u32[]{:S(2)}, u32[]{:S(2)}) %collective-permute-start.73) | collective-permute-done | bytes 294944 | tf_op jit(solution)/shard_map/ppermute | solution.py:539
  415.5 4.8 convolution_convert_fusion.5
  422.3 4.2 fusion.183.gs_ref
  426.6 5.3 gate_bwd.3
  438.1 26.6 %scan_bwd.3 = (bf16[1024,768]{1,0:T(8,128)(2,1)S(1)}, bf16[1024,256]{1,0:T(8,128)(2,1)S(1)}, bf16[1024,128]{1,0:T(8,128)(2,1)S(1)}, f32[8,768]{1,0:T(8,128)S(1)}...) custom-call(s32[1]{0:T(128)} %bitcast.30.me_ref, bf16[1024,768]{1,0:T(8,128)(2,1)S(1)} %copy-done.28, ...), custom_call_target="tpu_custom_call" | custom-call | flops 28185722880 | bytes 15728640 | tf_op jit(solution)/shard_map/scan_bwd/pallas_call | solution.py:448
  539.3 12.1 %collective-permute-done.69 = bf16[384,768]{1,0:T(8,128)(2,1)} collective-permute-done((bf16[384,768]{1,0:T(8,128)(2,1)S(1)}, bf16[384,768]{1,0:T(8,128)(2,1)}, u32[]{:S(2)}, u32[]{:S(2)}) %collective-permute-start.69) | collective-permute-done | bytes 589856 | tf_op jit(solution)/shard_map/ppermute | solution.py:539
  553.5 10.9 %collective-permute-done.61 = bf16[384,768]{1,0:T(8,128)(2,1)} collective-permute-done((bf16[384,768]{1,0:T(8,128)(2,1)}, bf16[384,768]{1,0:T(8,128)(2,1)}, u32[]{:S(2)}, u32[]{:S(2)}) %collective-permute-start.61) | collective-permute-done | bytes 589856 | tf_op jit(solution)/shard_map/ppermute | solution.py:539
  574.9 6.0 convolution_convert_fusion.4
  609.1 6.4 %collective-permute-done.68 = bf16[192,256]{0,1:T(8,128)(2,1)S(1)} collective-permute-done((bf16[192,256]{0,1:T(8,128)(2,1)S(1)}, bf16[192,256]{0,1:T(8,128)(2,1)S(1)}, u32[]{:S(2)}, u32[]{:S(2)}) %collective-permute-start.68) | collective-permute-done | bytes 98336 | tf_op jit(solution)/shard_map/ppermute | solution.py:539
  (741 shorter events, 313.3 us)
Async XLA Ops:
  2.7 25.2 %collective-permute-start = (bf16[192,768]{1,0:T(8,128)(2,1)}, bf16[192,768]{1,0:T(8,128)(2,1)}, u32[]{:S(2)}, u32[]{:S(2)}) collective-permute-start(bf16[192,768]{1,0:T(8,128)(2,1)} %get-tuple-element.297), channel_id=1, source_target_pairs={{0,4},{1,5},{2,6},{3,7},{4,0},{5,1},{6,2},{7,3},{8,12},{9,13},{10,... | collective-permute-start | bytes 884744 | tf_op jit(solution)/shard_map/ppermute | solution.py:539
  8.6 22.2 %collective-permute-start.1 = (bf16[192,768]{1,0:T(8,128)(2,1)}, bf16[192,768]{1,0:T(8,128)(2,1)}, u32[]{:S(2)}, u32[]{:S(2)}) collective-permute-start(bf16[192,768]{1,0:T(8,128)(2,1)} %get-tuple-element.298), channel_id=1, source_target_pairs={{0,1},{1,0},{2,3},{3,2},{4,5},{5,4},{6,7},{7,6},{8,9},{9,8},{10,11... | collective-permute-start | bytes 884744 | tf_op jit(solution)/shard_map/ppermute | solution.py:539
  48.8 70.0 %collective-permute-start.6 = (bf16[768,768]{1,0:T(8,128)(2,1)}, bf16[768,768]{1,0:T(8,128)(2,1)}, u32[]{:S(2)}, u32[]{:S(2)}) collective-permute-start(bf16[768,768]{1,0:T(8,128)(2,1)} %pad_maximum_fusion.10), channel_id=1, source_target_pairs={{0,1},{1,0},{2,3},{3,2},{4,5},{5,4},{6,7},{7,6},{8,9},{9,8},{10,11... | collective-permute-start | bytes 3538952 | tf_op jit(solution)/shard_map/ppermute | solution.py:539
  70.7 32.4 %collective-permute-start.7 = (bf16[384,768]{1,0:T(8,128)(2,1)}, bf16[384,768]{1,0:T(8,128)(2,1)}, u32[]{:S(2)}, u32[]{:S(2)}) collective-permute-start(bf16[384,768]{1,0:T(8,128)(2,1)} %pad_maximum_fusion.21), channel_id=1, source_target_pairs={{0,2},{1,3},{2,0},{3,1},{4,6},{5,7},{6,4},{7,5},{8,10},{9,11},{10,... | collective-permute-start | bytes 1769480 | tf_op jit(solution)/shard_map/ppermute | solution.py:539
  78.6 37.1 %collective-permute-start.12 = (bf16[384,768]{1,0:T(8,128)(2,1)}, bf16[384,768]{1,0:T(8,128)(2,1)}, u32[]{:S(2)}, u32[]{:S(2)}) collective-permute-start(bf16[384,768]{1,0:T(8,128)(2,1)} %pad_maximum_fusion.22), channel_id=1, source_target_pairs={{0,2},{1,3},{2,0},{3,1},{4,6},{5,7},{6,4},{7,5},{8,10},{9,11},{10,... | collective-permute-start | bytes 1769480 | tf_op jit(solution)/shard_map/ppermute | solution.py:539
  103.1 35.7 %collective-permute-start.15 = (bf16[384,768]{1,0:T(8,128)(2,1)S(1)}, bf16[384,768]{1,0:T(8,128)(2,1)S(1)}, u32[]{:S(2)}, u32[]{:S(2)}) collective-permute-start(bf16[384,768]{1,0:T(8,128)(2,1)S(1)} %pad_maximum_fusion.23), channel_id=1, source_target_pairs={{0,2},{1,3},{2,0},{3,1},{4,6},{5,7},{6,4},{7,5},{8,10},{9,11},{10,... | collective-permute-start | bytes 1769480 | tf_op jit(solution)/shard_map/ppermute | solution.py:539
  105.5 28.9 %collective-permute-start.14 = (bf16[768,768]{1,0:T(8,128)(2,1)S(1)}, bf16[768,768]{1,0:T(8,128)(2,1)S(1)}, u32[]{:S(2)}, u32[]{:S(2)}) collective-permute-start(bf16[768,768]{1,0:T(8,128)(2,1)S(1)} %pad_maximum_fusion.11), channel_id=1, source_target_pairs={{0,1},{1,0},{2,3},{3,2},{4,5},{5,4},{6,7},{7,6},{8,9},{9,8},{10,11... | collective-permute-start | bytes 3538952 | tf_op jit(solution)/shard_map/ppermute | solution.py:539
  115.7 36.6 %collective-permute-start.19 = (bf16[384,768]{1,0:T(8,128)(2,1)S(1)}, bf16[384,768]{1,0:T(8,128)(2,1)S(1)}, u32[]{:S(2)}, u32[]{:S(2)}) collective-permute-start(bf16[384,768]{1,0:T(8,128)(2,1)S(1)} %pad_maximum_fusion.24), channel_id=1, source_target_pairs={{0,2},{1,3},{2,0},{3,1},{4,6},{5,7},{6,4},{7,5},{8,10},{9,11},{10,... | collective-permute-start | bytes 1769480 | tf_op jit(solution)/shard_map/ppermute | solution.py:539
  118.8 39.9 %collective-permute-start.20 = (bf16[768,768]{1,0:T(8,128)(2,1)S(1)}, bf16[768,768]{1,0:T(8,128)(2,1)S(1)}, u32[]{:S(2)}, u32[]{:S(2)}) collective-permute-start(bf16[768,768]{1,0:T(8,128)(2,1)S(1)} %pad_maximum_fusion.12), channel_id=1, source_target_pairs={{0,1},{1,0},{2,3},{3,2},{4,5},{5,4},{6,7},{7,6},{8,9},{9,8},{10,11... | collective-permute-start | bytes 3538952 | tf_op jit(solution)/shard_map/ppermute | solution.py:539
  165.2 29.3 %collective-permute-start.23 = (bf16[384,768]{1,0:T(8,128)(2,1)S(1)}, bf16[384,768]{1,0:T(8,128)(2,1)S(1)}, u32[]{:S(2)}, u32[]{:S(2)}) collective-permute-start(bf16[384,768]{1,0:T(8,128)(2,1)S(1)} %pad_maximum_fusion.25), channel_id=1, source_target_pairs={{0,4},{1,5},{2,6},{3,7},{4,0},{5,1},{6,2},{7,3},{8,12},{9,13},{10,... | collective-permute-start | bytes 1769480 | tf_op jit(solution)/shard_map/ppermute | solution.py:539
  170.8 28.9 %collective-permute-start.26 = (bf16[768,768]{1,0:T(8,128)(2,1)S(1)}, bf16[768,768]{1,0:T(8,128)(2,1)S(1)}, u32[]{:S(2)}, u32[]{:S(2)}) collective-permute-start(bf16[768,768]{1,0:T(8,128)(2,1)S(1)} %pad_maximum_fusion.13), channel_id=1, source_target_pairs={{0,1},{1,0},{2,3},{3,2},{4,5},{5,4},{6,7},{7,6},{8,9},{9,8},{10,11... | collective-permute-start | bytes 3538952 | tf_op jit(solution)/shard_map/ppermute | solution.py:539
  177.1 46.8 %collective-permute-start.28 = (bf16[768,768]{1,0:T(8,128)(2,1)S(1)}, bf16[768,768]{1,0:T(8,128)(2,1)S(1)}, u32[]{:S(2)}, u32[]{:S(2)}) collective-permute-start(bf16[768,768]{1,0:T(8,128)(2,1)S(1)} %pad_maximum_fusion.15), channel_id=1, source_target_pairs={{0,1},{1,0},{2,3},{3,2},{4,5},{5,4},{6,7},{7,6},{8,9},{9,8},{10,11... | collective-permute-start | bytes 3538952 | tf_op jit(solution)/shard_map/ppermute | solution.py:539
  194.5 27.6 %collective-permute-start.27 = (bf16[768,768]{1,0:T(8,128)(2,1)S(1)}, bf16[768,768]{1,0:T(8,128)(2,1)S(1)}, u32[]{:S(2)}, u32[]{:S(2)}) collective-permute-start(bf16[768,768]{1,0:T(8,128)(2,1)S(1)} %pad_maximum_fusion.14), channel_id=1, source_target_pairs={{0,2},{1,3},{2,0},{3,1},{4,6},{5,7},{6,4},{7,5},{8,10},{9,11},{10,... | collective-permute-start | bytes 3538952 | tf_op jit(solution)/shard_map/ppermute | solution.py:539
  197.0 25.2 %collective-permute-start.24 = (bf16[256,1536]{1,0:T(8,128)(2,1)S(1)}, bf16[256,1536]{1,0:T(8,128)(2,1)S(1)}, u32[]{:S(2)}, u32[]{:S(2)}) collective-permute-start(bf16[256,1536]{1,0:T(8,128)(2,1)S(1)} %multiply_convert_fusion.1), channel_id=1, source_target_pairs={{0,16},{8,24},{16,0},{24,8},{1,17},{9,25},{17,1},{25,9},{2,18},{10... | collective-permute-start | bytes 2359304 | tf_op jit(solution)/shard_map/ppermute | solution.py:539
  266.0 43.5 %collective-permute-start.32 = (bf16[256,1536]{1,0:T(8,128)(2,1)}, bf16[256,1536]{1,0:T(8,128)(2,1)S(1)}, u32[]{:S(2)}, u32[]{:S(2)}) collective-permute-start(bf16[256,1536]{1,0:T(8,128)(2,1)} %slice.1101), channel_id=1, source_target_pairs={{0,16},{8,24},{16,0},{24,8},{1,17},{9,25},{17,1},{25,9},{2,18},{10... | collective-permute-start | bytes 2359304 | tf_op jit(solution)/shard_map/ppermute | solution.py:539
  278.0 68.3 %collective-permute-start.71 = (bf16[768,768]{1,0:T(8,128)(2,1)}, bf16[768,768]{1,0:T(8,128)(2,1)}, u32[]{:S(2)}, u32[]{:S(2)}) collective-permute-start(bf16[768,768]{1,0:T(8,128)(2,1)} %fusion.44), channel_id=1, source_target_pairs={{0,1},{1,0},{2,3},{3,2},{4,5},{5,4},{6,7},{7,6},{8,9},{9,8},{10,11... | collective-permute-start | bytes 3538952 | tf_op jit(solution)/shard_map/ppermute | solution.py:539
  279.0 51.1 %collective-permute-start.33 = (bf16[768,768]{1,0:T(8,128)(2,1)S(1)}, bf16[768,768]{1,0:T(8,128)(2,1)S(1)}, u32[]{:S(2)}, u32[]{:S(2)}) collective-permute-start(bf16[768,768]{1,0:T(8,128)(2,1)S(1)} %convolution_convert_fusion.8), channel_id=1, source_target_pairs={{0,1},{1,0},{2,3},{3,2},{4,5},{5,4},{6,7},{7,6},{8,9},{9,8},{10,11... | collective-permute-start | bytes 3538952 | tf_op jit(solution)/shard_map/ppermute | solution.py:539
  351.4 34.0 %collective-permute-start.72 = (bf16[384,768]{1,0:T(8,128)(2,1)S(1)}, bf16[384,768]{1,0:T(8,128)(2,1)S(1)}, u32[]{:S(2)}, u32[]{:S(2)}) collective-permute-start(bf16[384,768]{1,0:T(8,128)(2,1)S(1)} %slice.1103), channel_id=1, source_target_pairs={{0,2},{1,3},{2,0},{3,1},{4,6},{5,7},{6,4},{7,5},{8,10},{9,11},{10,... | collective-permute-start | bytes 1769480 | tf_op jit(solution)/shard_map/ppermute | solution.py:539
  354.6 47.3 %collective-permute-start.42 = (bf16[768,768]{1,0:T(8,128)(2,1)S(1)}, bf16[768,768]{1,0:T(8,128)(2,1)S(1)}, u32[]{:S(2)}, u32[]{:S(2)}) collective-permute-start(bf16[768,768]{1,0:T(8,128)(2,1)S(1)} %fusion.47), channel_id=1, source_target_pairs={{0,1},{1,0},{2,3},{3,2},{4,5},{5,4},{6,7},{7,6},{8,9},{9,8},{10,11... | collective-permute-start | bytes 3538952 | tf_op jit(solution)/shard_map/ppermute | solution.py:539
  414.3 65.7 %collective-permute-start.44 = (bf16[768,768]{1,0:T(8,128)(2,1)}, bf16[768,768]{1,0:T(8,128)(2,1)}, u32[]{:S(2)}, u32[]{:S(2)}) collective-permute-start(bf16[768,768]{1,0:T(8,128)(2,1)} %fusion.50), channel_id=1, source_target_pairs={{0,1},{1,0},{2,3},{3,2},{4,5},{5,4},{6,7},{7,6},{8,9},{9,8},{10,11... | collective-permute-start | bytes 3538952 | tf_op jit(solution)/shard_map/ppermute | solution.py:539
  420.3 59.7 %collective-permute-start.45 = (bf16[1024,128]{1,0:T(8,128)(2,1)}, bf16[1024,128]{1,0:T(8,128)(2,1)}, u32[]{:S(2)}, u32[]{:S(2)}) collective-permute-start(bf16[1024,128]{1,0:T(8,128)(2,1)} %get-tuple-element.169), channel_id=1, source_target_pairs={{0,16},{8,24},{16,0},{24,8},{1,17},{9,25},{17,1},{25,9},{2,18},{10... | collective-permute-start | bytes 786440 | tf_op jit(solution)/shard_map/ppermute | solution.py:539
  421.3 55.1 %collective-permute-start.39 = (bf16[256,1536]{1,0:T(8,128)(2,1)}, bf16[256,1536]{1,0:T(8,128)(2,1)}, u32[]{:S(2)}, u32[]{:S(2)}) collective-permute-start(bf16[256,1536]{1,0:T(8,128)(2,1)} %convolution_convert_fusion.5), channel_id=1, source_target_pairs={{0,16},{8,24},{16,0},{24,8},{1,17},{9,25},{17,1},{25,9},{2,18},{10... | collective-permute-start | bytes 2359304 | tf_op jit(solution)/shard_map/ppermute | solution.py:539
  437.1 74.1 %collective-permute-start.55 = (bf16[768,768]{1,0:T(8,128)(2,1)}, bf16[768,768]{1,0:T(8,128)(2,1)}, u32[]{:S(2)}, u32[]{:S(2)}) collective-permute-start(bf16[768,768]{1,0:T(8,128)(2,1)} %convolution_convert_fusion.7), channel_id=1, source_target_pairs={{0,1},{1,0},{2,3},{3,2},{4,5},{5,4},{6,7},{7,6},{8,9},{9,8},{10,11... | collective-permute-start | bytes 3538952 | tf_op jit(solution)/shard_map/ppermute | solution.py:539
  468.9 22.9 %collective-permute-start.63 = (bf16[192,768]{1,0:T(8,128)(2,1)}, bf16[192,768]{1,0:T(8,128)(2,1)}, u32[]{:S(2)}, u32[]{:S(2)}) collective-permute-start(bf16[192,768]{1,0:T(8,128)(2,1)} %slice.1111), channel_id=1, source_target_pairs={{0,4},{1,5},{2,6},{3,7},{4,0},{5,1},{6,2},{7,3},{8,12},{9,13},{10,... | collective-permute-start | bytes 884744 | tf_op jit(solution)/shard_map/ppermute | solution.py:539
  493.9 28.1 %collective-permute-start.60 = (bf16[768,768]{1,0:T(8,128)(2,1)}, bf16[768,768]{1,0:T(8,128)(2,1)S(1)}, u32[]{:S(2)}, u32[]{:S(2)}) collective-permute-start(bf16[768,768]{1,0:T(8,128)(2,1)} %convolution_convert_fusion.6), channel_id=1, source_target_pairs={{0,1},{1,0},{2,3},{3,2},{4,5},{5,4},{6,7},{7,6},{8,9},{9,8},{10,11... | collective-permute-start | bytes 3538952 | tf_op jit(solution)/shard_map/ppermute | solution.py:539
  507.1 59.7 %collective-permute-start.47 = (bf16[256,1536]{1,0:T(8,128)(2,1)}, bf16[256,1536]{1,0:T(8,128)(2,1)}, u32[]{:S(2)}, u32[]{:S(2)}) collective-permute-start(bf16[256,1536]{1,0:T(8,128)(2,1)} %slice.1099), channel_id=1, source_target_pairs={{0,16},{8,24},{16,0},{24,8},{1,17},{9,25},{17,1},{25,9},{2,18},{10... | collective-permute-start | bytes 2359304 | tf_op jit(solution)/shard_map/ppermute | solution.py:539
  515.9 35.4 %collective-permute-start.69 = (bf16[384,768]{1,0:T(8,128)(2,1)S(1)}, bf16[384,768]{1,0:T(8,128)(2,1)}, u32[]{:S(2)}, u32[]{:S(2)}) collective-permute-start(bf16[384,768]{1,0:T(8,128)(2,1)S(1)} %slice.1104), channel_id=1, source_target_pairs={{0,2},{1,3},{2,0},{3,1},{4,6},{5,7},{6,4},{7,5},{8,10},{9,11},{10,... | collective-permute-start | bytes 1769480 | tf_op jit(solution)/shard_map/ppermute | solution.py:539
  524.7 39.7 %collective-permute-start.61 = (bf16[384,768]{1,0:T(8,128)(2,1)}, bf16[384,768]{1,0:T(8,128)(2,1)}, u32[]{:S(2)}, u32[]{:S(2)}) collective-permute-start(bf16[384,768]{1,0:T(8,128)(2,1)} %slice.1105), channel_id=1, source_target_pairs={{0,2},{1,3},{2,0},{3,1},{4,6},{5,7},{6,4},{7,5},{8,10},{9,11},{10,... | collective-permute-start | bytes 1769480 | tf_op jit(solution)/shard_map/ppermute | solution.py:539
  532.7 64.2 %collective-permute-start.66 = (bf16[768,256]{0,1:T(8,128)(2,1)}, bf16[768,256]{0,1:T(8,128)(2,1)}, u32[]{:S(2)}, u32[]{:S(2)}) collective-permute-start(bf16[768,256]{0,1:T(8,128)(2,1)} %pad_maximum_fusion.31), channel_id=1, source_target_pairs={{0,1},{1,0},{2,3},{3,2},{4,5},{5,4},{6,7},{7,6},{8,9},{9,8},{10,11... | collective-permute-start | bytes 1179656 | tf_op jit(solution)/shard_map/ppermute | solution.py:539
  537.7 44.3 %collective-permute-start.57 = (bf16[192,768]{1,0:T(8,128)(2,1)}, bf16[192,768]{1,0:T(8,128)(2,1)}, u32[]{:S(2)}, u32[]{:S(2)}) collective-permute-start(bf16[192,768]{1,0:T(8,128)(2,1)} %slice.1114), channel_id=1, source_target_pairs={{0,4},{1,5},{2,6},{3,7},{4,0},{5,1},{6,2},{7,3},{8,12},{9,13},{10,... | collective-permute-start | bytes 884744 | tf_op jit(solution)/shard_map/ppermute | solution.py:539
  553.5 32.7 %collective-permute-start.70 = (bf16[192,768]{1,0:T(8,128)(2,1)}, bf16[192,768]{1,0:T(8,128)(2,1)}, u32[]{:S(2)}, u32[]{:S(2)}) collective-permute-start(bf16[192,768]{1,0:T(8,128)(2,1)} %slice.1110), channel_id=1, source_target_pairs={{0,4},{1,5},{2,6},{3,7},{4,0},{5,1},{6,2},{7,3},{8,12},{9,13},{10,... | collective-permute-start | bytes 884744 | tf_op jit(solution)/shard_map/ppermute | solution.py:539
  580.9 22.1 %collective-permute-start.48 = (bf16[256,1536]{1,0:T(8,128)(2,1)}, bf16[256,1536]{1,0:T(8,128)(2,1)S(1)}, u32[]{:S(2)}, u32[]{:S(2)}) collective-permute-start(bf16[256,1536]{1,0:T(8,128)(2,1)} %convolution_convert_fusion.4), channel_id=1, source_target_pairs={{0,16},{8,24},{16,0},{24,8},{1,17},{9,25},{17,1},{25,9},{2,18},{10... | collective-permute-start | bytes 2359304 | tf_op jit(solution)/shard_map/ppermute | solution.py:539
  (192 other events, 2571.3 us)

commit v3 on v2

--- a/solution.py
+++ b/solution.py
@@ -165,7 +165,8 @@
 
 def place_of(chunk, chunks, me_ref):
     part = chunks // 4
-    return (chunk // part ^ me_ref[0]) * part + chunk % part
+    away = chunk // part ^ me_ref[0]
+    return (2 * (away % 2) + away // 2) * part + chunk % part
 
 
 def scan_fwd(me, x_pre, bcdt_pre, gate_pre, side, weights):
@@ -201,7 +202,7 @@
         ),
         out_shape=[
             jax.ShapeDtypeStruct((length, width), BF16),
-            jax.ShapeDtypeStruct((length, width), F32),
+            jax.ShapeDtypeStruct((length, width), BF16),
             jax.ShapeDtypeStruct((8, length), F32),
             jax.ShapeDtypeStruct((chunks, STATE, width), BF16),
         ],
@@ -252,7 +253,7 @@
                 tile,
                 tile,
                 tile,
-                pl.BlockSpec((rows, columns.shape[1]), lambda p, m: (p ^ m[0], 0)),
+                pl.BlockSpec((rows, columns.shape[1]), lambda p, m: (2 * (p % 2) + p // 2 ^ m[0], 0)),
                 whole(gain.shape),
             ],
             out_specs=[tile, tile, whole((1, width))],
@@ -304,7 +305,6 @@
     gdt_ref,
     accx_ref,
     accbc_ref,
-    acch_ref,
     grad_state,
     next_x,
     next_bc,
@@ -318,7 +318,6 @@
         next_bc[...] = jnp.zeros_like(next_bc)
         accx_ref[...] = jnp.zeros_like(accx_ref)
         accbc_ref[...] = jnp.zeros_like(accbc_ref)
-        acch_ref[...] = jnp.zeros_like(acch_ref)
 
     aux = aux_ref[...]
     joined_bc = jnp.concatenate([bc_tail_ref[:, : 2 * STATE], bcdt_ref[:, : 2 * STATE]], 0)
@@ -389,7 +388,7 @@
         grad_inputs = local + leaving * to_end_now
         stacked = jnp.concatenate([coming * carried, ending * leaving, grad_inputs * x_conv], 0)
         head_sums = head_sums + mm_t(stacked.astype(BF16), spread[:, at])
-        acch_ref[0:1, at] += jnp.sum(g * x_conv, 0, keepdims=True)
+        accx_ref[5:6, at] += jnp.sum(g * x_conv, 0, keepdims=True)
         grad_conv = (grad_inputs * dt_wide[:, at] + g * skip_ref[:, at]) * (
             sig * (1.0 + pre * (1.0 - sig))
         )
@@ -408,8 +407,8 @@
     grad_dt = head_sums[2 * CHUNK :] + head_ref[1:2] * straddle
     grad_raw = jnp.where(lane < GROUP, grad_dt * jax.nn.sigmoid(raw), 0.0)
     gdt_ref[...] = grad_raw.astype(BF16)
-    acch_ref[1:2, :LANES] += jnp.sum(grad_raw, 0, keepdims=True)
-    acch_ref[2:3, :LANES] += jnp.sum(dt * straddle, 0, keepdims=True)
+    accx_ref[6:7, :LANES] += jnp.sum(grad_raw, 0, keepdims=True)
+    accx_ref[7:8, :LANES] += jnp.sum(dt * straddle, 0, keepdims=True)
     grad_meet_low = grad_meet.astype(BF16)
     grad_b = grad_b + mm(grad_meet_low, c_low)
     grad_c = grad_c + t_mm(grad_meet_low, b_low)
@@ -457,7 +456,6 @@
                 tile(LANES),
                 whole((8, width)),
                 whole((8, 2 * STATE)),
-                whole((8, width)),
             ],
             scratch_shapes=[
                 pltpu.VMEM((STATE, width), F32),
@@ -471,7 +469,6 @@
             jax.ShapeDtypeStruct((length, LANES), BF16),
             jax.ShapeDtypeStruct((8, width), F32),
             jax.ShapeDtypeStruct((8, 2 * STATE), F32),
-            jax.ShapeDtypeStruct((8, width), F32),
         ],
         compiler_params=pltpu.CompilerParams(vmem_limit_bytes=VMEM_BYTES),
         cost_estimate=pl.CostEstimate(
@@ -559,18 +556,20 @@
     return found
 
 
-def spread_stage(rows, mask):
-    got = swap(rows, "dp", mask)
-    return jnp.concatenate([rows, got], 0), got
-
-
-def gather_rows(own, masks):
-    stages = []
-    rows = own
-    for mask in masks:
-        rows, got = spread_stage(rows, mask)
-        stages.append(got)
-    return rows, stages
+class Rows:
+    def __init__(self, own):
+        self.rows = own
+
+    def stage(self, mask, *earlier):
+        got = swap(after(self.rows, *earlier), "dp", mask)
+        self.rows = jnp.concatenate([self.rows, got], 0)
+        return got
+
+    def begin(self, masks, *earlier):
+        for mask in masks[:-2]:
+            got = self.stage(mask, *earlier)
+            earlier = ()
+        return got
 
 
 def scatter_first(kept, got):
@@ -599,8 +598,19 @@
 def reordered(values, me):
     size = values.shape[0] // 4
     return jnp.concatenate(
-        [lax.dynamic_slice_in_dim(values, (part ^ me) * size, size, 0) for part in range(4)], 0
-    )
+        [lax.dynamic_slice_in_dim(values, (away ^ me) * size, size, 0) for away in (0, 2, 1, 3)], 0
+    )
+
+
+def restored(values, me):
+    size = values.shape[0] // 4
+    parts = []
+    for part in range(4):
+        away = part ^ me
+        parts.append(
+            lax.dynamic_slice_in_dim(values, (2 * (away % 2) + away // 2) * size, size, 0)
+        )
+    return jnp.concatenate(parts, 0)
 
 
 def turned_over(values, size):
@@ -634,8 +644,8 @@
     return lax.dot_general(lhs, rhs, (((1,), (1,)), ((), ())), preferred_element_type=F32)
 
 
-def own_order(features, masks):
-    place = lax.axis_index("dp")
+def own_order(features, masks, earlier):
+    place = after(lax.axis_index("dp"), earlier)
     found = offsets(masks)
     height = features // len(found)
     index = lax.broadcasted_iota(jnp.int32, (1, features), 1)
@@ -676,7 +686,7 @@
     masks = dp_masks()
     place = lax.axis_index("tensor")
     core, far = place % 2, place // 2
-    me = 2 * core + far
+    me = place
     me_row = me.astype(jnp.int32)[None]
     half = length // 2
     quarter = length // 4
@@ -689,24 +699,35 @@
     w_small = jnp.concatenate([own_bc[0], own_bc[1], w_dt[0], w_dt[1]], 1)
     w_small = jnp.pad(w_small, ((0, 0), (0, 2 * LANES - w_small.shape[1])))
 
-    far_stage, near_stage = {}, {}
-
-    def gathered(name, own, over):
-        rows, stages = gather_rows(own, over)
-        far_stage[name], near_stage[name] = stages[0], stages[-1 if over is not masks else -2]
-        return rows
-
-    early = swap(w_out[1], "dp", 1)
-    x_rows = gathered("x0", w_x[0], masks)
-    small_rows = gathered("small", after(w_small, near_stage["x0"]), masks)
-    z_rows = gathered("z0", after(w_z[0], near_stage["x0"]), masks)
-    out_rows = gathered("out0", after(w_out[0], far_stage["z0"]), masks)
-    x_rows = [x_rows, gathered("x1", after(w_x[1], far_stage["out0"]), masks)]
-    z_rows = [z_rows, gathered("z1", after(w_z[1], far_stage["x1"]), masks)]
-    both_sides = after(jnp.concatenate([w_out[1], early], 0), far_stage["z1"])
-    rows = gathered("out1", both_sides, masks[:-1])
-    rows = [rows[seat * height : (seat + 1) * height] for seat in seated]
-    out_rows = [out_rows, jnp.concatenate(rows, 0)]
+    x0, z0, out0 = Rows(w_x[0]), Rows(w_z[0]), Rows(w_out[0])
+    x1, z1, out1 = Rows(w_x[1]), Rows(w_z[1]), Rows(w_out[1])
+    small = Rows(w_small)
+    near_mask, side_mask = masks[-2:]
+    x0_far = x0.begin(masks)
+    out1_side = out1.stage(side_mask)
+    x0_near = x0.stage(near_mask)
+    small_far = small.begin(masks, x0_far)
+    z0_far = z0.begin(masks, x0_near, small_far)
+    small_near = small.stage(near_mask, x0_near)
+    x0.stage(side_mask)
+    out0_far = out0.begin(masks, small_near, z0_far)
+    z0_near = z0.stage(near_mask, small_near)
+    small.stage(side_mask)
+    x1_far = x1.begin(masks, z0_near, out0_far)
+    out0_near = out0.stage(near_mask, z0_near)
+    z0.stage(side_mask)
+    z1_far = z1.begin(masks, out0_near, x1_far)
+    x1_near = x1.stage(near_mask, out0_near)
+    out0.stage(side_mask)
+    out1_far = out1.begin(masks, x1_near, z1_far)
+    z1_near = z1.stage(near_mask, x1_near)
+    x1_side = x1.stage(side_mask)
+    out1_near = out1.stage(near_mask, z1_near)
+    z1_side = z1.stage(side_mask)
+    out1_rows = [out1.rows[seat * height : (seat + 1) * height] for seat in seated]
+    x_rows, z_rows = [x0.rows, x1.rows], [z0.rows, z1.rows]
+    out_rows = [out0.rows, jnp.concatenate(out1_rows, 0)]
+    small_rows = small.rows
 
     own_cols = small_rows[:, :LANES]
     across = swap(own_cols, "tensor", 2)
@@ -731,8 +752,8 @@
 
     bcdt_rows = [small_columns(layer) for layer in range(LAYERS)]
 
-    order = lax.optimization_barrier(own_order(features, masks))
-    side = side_arrays(segments)
+    order = lax.optimization_barrier(own_order(features, masks, x0_far))
+    side = side_arrays(after(segments, x0_far))
     spread = spread_matrix(width)
     weights = [
         scan_weights(
@@ -749,13 +770,13 @@
         for layer in range(LAYERS)
     ]
     order, side, weights = lax.optimization_barrier((order, side, weights))
-    hidden_now = after(reordered(hidden, me), far_stage["x0"], early)
-    hidden_low = dot(hidden_now, order).astype(BF16)
-    cotangent_now = after(reordered(cotangent, me), near_stage["x0"], hidden_low)
-    cotangent_low = dot(cotangent_now, order).astype(BF16)
-    gains = mm(after(norm_gain, near_stage["x0"]), order.astype(F32), PRECISE)
-    hidden_low, cotangent_low, gains, _, _ = lax.optimization_barrier(
-        (hidden_low, cotangent_low, gains, far_stage["small"], far_stage["z0"])
+    hidden_rows = reordered(after(hidden, x0_far), me)
+    hidden_low = dot(after(hidden_rows, x0_near, small_far, out1_side), order).astype(BF16)
+    cotangent_rows = reordered(after(cotangent, x0_far), me)
+    cotangent_low = dot(after(cotangent_rows, small_near, z0_far), order).astype(BF16)
+    gains = mm(after(norm_gain, small_near), order.astype(F32), PRECISE)
+    hidden_low, cotangent_low, gains = lax.optimization_barrier(
+        (hidden_low, cotangent_low, gains)
     )
 
     def columns_of(values, which):
@@ -764,12 +785,11 @@
     stream = hidden_low.astype(F32)
     normed0 = (stream * rms_of(stream) * gains[0]).astype(BF16)
     stream0 = hidden_low[:quarter].astype(F32)
-    x_pre0 = dot(after(normed0, near_stage["small"]), x_rows[0])
-    bcdt_pre0 = dot(after(normed0, near_stage["z0"], far_stage["out0"]), bcdt_rows[0])
-    gate_pre0 = dot(after(normed0, near_stage["out0"], far_stage["x1"]), z_rows[0])
-    gate_pre0 = after(gate_pre0, near_stage["x1"], far_stage["z1"])
+    x_pre0 = dot(normed0, x_rows[0])
+    bcdt_pre0 = dot(after(normed0, x_pre0, z0_near, out0_far), bcdt_rows[0])
+    gate_pre0 = dot(after(normed0, bcdt_pre0, out0_near, x1_far), z_rows[0]).astype(BF16)
     u0, y0, sq, kept0 = scan_fwd(me_row, x_pre0, bcdt_pre0, gate_pre0, side, weights[0])
-    u_now = after(u0, near_stage["z1"])
+    u_now = after(u0, x1_near, z1_far)
     sent = dot_t(u_now[half:], out_rows[0]).astype(BF16)
     sq = sq[0:1]
     sq = sq + swap(sq, "tensor", 1)
@@ -779,20 +799,23 @@
     away = after(mine[quarter:].astype(BF16), sq)
     got = swap(away, "tensor", 2)
     inv0 = lax.rsqrt(sq / INNER + EPSILON)[0]
+    got, mine, z1_near, out1_far, x1_side = lax.optimization_barrier(
+        (got, mine, z1_near, out1_far, x1_side)
+    )
     total0 = mine[:quarter] + got.astype(F32)
     stream1 = stream0 + own_quarter(inv0, me)[:, None] * total0
     normed_own = (stream1 * rms_of(stream1) * gains[1]).astype(BF16)
-    normed_own = after(normed_own, far_stage["out1"])
     normed_half = jnp.concatenate([normed_own, swap(normed_own, "tensor", 2)], 0)
+    normed_half, z1_side = lax.optimization_barrier((normed_half, z1_side))
     normed1 = jnp.concatenate([normed_half, swap(normed_half, "tensor", 1)], 0)
     scaled0 = (u0.astype(F32) * reordered(inv0, me)[:, None]).astype(BF16)
 
-    x_pre1 = dot(normed1, x_rows[1])
+    x_pre1 = dot(after(normed1, out1_near), x_rows[1])
     bcdt_pre1 = dot(normed1, bcdt_rows[1])
-    gate_pre1 = dot(after(normed1, near_stage["out1"]), z_rows[1])
+    gate_pre1 = dot(normed1, z_rows[1]).astype(BF16)
     u1, y1, sq, kept1 = scan_fwd(me_row, x_pre1, bcdt_pre1, gate_pre1, side, weights[1])
     scaled_grad1 = dot(cotangent_low, out_rows[1])
-    cross = reordered(jnp.sum(scaled_grad1 * u1.astype(F32), -1), me)
+    cross = restored(jnp.sum(scaled_grad1 * u1.astype(F32), -1), me)
     both = tensor_sum(jnp.stack([sq[0], cross]))
     mixed_sent = dot_t(u1[half:], out_rows[1]).astype(BF16)
     mixed_mine = dot_t(u1[:half], out_rows[1])
@@ -807,14 +830,11 @@
     )
     z_sent = sent_half(normed1, g_gate1)
     z_got = swap(z_sent, "dp", 1)
-    scaled1 = (u1.astype(F32) * reordered(inv1, me)[:, None]).astype(BF16)
-    out_sent = sent_half(cotangent_low, scaled1)
-    out_got = swap(out_sent, "dp", 1)
-    g_y = after(g_y, z_sent, out_sent)
-    g_x1, g_bc1, g_dt1, acc_x1, acc_bc1, acc_head1 = scan_bwd(
+    g_y = after(g_y, z_sent)
+    g_x1, g_bc1, g_dt1, acc_x1, acc_bc1 = scan_bwd(
         me_row, g_y, x_pre1, bcdt_pre1, kept1, side, weights[1]
     )
-    g_x1 = after(g_x1, z_got, mixed_got)
+    g_x1, z_got, mixed_got = lax.optimization_barrier((g_x1, z_got, mixed_got))
 
     def grad_rows(rows, g_gate, g_x, g_bcdt, layer):
         return (
@@ -825,34 +845,56 @@
 
     g_bcdt = jnp.concatenate([g_bc1, g_dt1], 1)
     sent = grad_rows(slice(half, length), g_gate1, g_x1, g_bcdt, 1).astype(BF16)
-    own = grad_rows(slice(0, half), after(g_gate1, sent), g_x1, g_bcdt, 1)
+    cotangent_now = after(cotangent_low, sent)
+    scaled1 = (u1.astype(F32) * reordered(inv1, me)[:, None]).astype(BF16)
+    out_sent = sent_half(cotangent_now, scaled1)
+    out_got = swap(out_sent, "dp", 1)
+    own = grad_rows(slice(0, half), after(g_gate1, out_sent), g_x1, g_bcdt, 1)
     mine = own + swap(sent, "tensor", 1).astype(F32)
     away = mine[quarter:].astype(BF16)
     got = swap(away, "tensor", 2)
-    normed_now, cotangent_now, _ = lax.optimization_barrier((normed1, cotangent_low, away))
+    normed_now = after(normed1, away)
     z_kept, z_next = scatter_first(grad_half(normed_now, g_gate1, 0), z_got)
-    x_got = swap(sent_half(normed_now, g_x1), "dp", 1)
-    out_kept, out_next = scatter_first(grad_half(cotangent_now, scaled1, 0), out_got)
+    z_near = swap(z_next, "dp", near_mask)
+    normed_now = after(normed_now, z_next)
+    x_sent = sent_half(normed_now, g_x1)
     x_kept_half = grad_half(normed_now, g_x1, 0)
+    out_kept_half = grad_half(after(cotangent_now, away), scaled1, 0)
+    mixed_total = mixed_mine[:quarter] + mixed_got.astype(F32)
+    last = stream1 + own_quarter(inv1, me)[:, None] * mixed_total
+    mixed_own = dot_t(last.astype(BF16), order).astype(BF16)
+    got, mine, out_got, z_near, x_sent, out_kept_half, x_kept_half, mixed_own = (
+        lax.optimization_barrier(
+            (got, mine, out_got, z_near, x_sent, out_kept_half, x_kept_half, mixed_own)
+        )
+    )
+    x_got = swap(x_sent, "dp", 1)
     total = mine[:quarter] + got.astype(F32)
     rms = rms_of(stream1)
     normal = stream1 * rms
-    d_norm1 = jnp.sum(total * normal, 0)
     grown = total * gains[1]
     grad_stream = cotangent_low[:quarter].astype(F32) + rms * (
         grown - normal * jnp.mean(grown * normal, -1, keepdims=True)
     )
     grad_own = grad_stream.astype(BF16)
+    out_kept, out_next = scatter_first(out_kept_half, out_got)
+    out_near = swap(out_next, "dp", near_mask)
+    z_kept, z_next = scatter_first(z_kept, z_near)
+    z_far = swap(z_next, "dp", masks[-3])
+    total_now = after(total, grad_own)
+    d_norm1 = jnp.sum(total_now * normal, 0)
     cross = jnp.sum(grad_own.astype(F32) * total0, -1)
     grad_half_rows = jnp.concatenate([grad_own, swap(grad_own, "tensor", 2)], 0)
     cross = jnp.concatenate([cross, swap(cross, "tensor", 2)], 0)
-    grad_half_rows, cross = lax.optimization_barrier((grad_half_rows, cross))
+    grad_half_rows, cross, z_far, out_near = lax.optimization_barrier(
+        (grad_half_rows, cross, z_far, out_near)
+    )
     grad0 = jnp.concatenate([grad_half_rows, swap(grad_half_rows, "tensor", 1)], 0)
-    cross = reordered(jnp.concatenate([cross, swap(cross, "tensor", 1)], 0), me)
-    x_kept, x_next = scatter_first(x_kept_half, x_got)
-    x_next = after(x_next, grad0)
-    x_near = swap(x_next, "dp", masks[-2])
-
+    cross = restored(jnp.concatenate([cross, swap(cross, "tensor", 1)], 0), me)
+    out_kept, out_next = scatter_first(out_kept, out_near)
+    out_far = swap(out_next, "dp", masks[-3])
+
+    grad0 = lax.optimization_barrier(grad0)
     out_sent0 = sent_half(grad0, scaled0)
     out_got0 = swap(out_sent0, "dp", 1)
     scaled_grad0 = dot(after(grad0, out_sent0), out_rows[0])
@@ -862,58 +904,80 @@
     )
     z_sent0 = sent_half(normed0, g_gate0)
     z_got0 = swap(z_sent0, "dp", 1)
-    d_z1 = scatter_rest(z_kept, z_next, masks)
-    mixed_total = mixed_mine[:quarter] + mixed_got.astype(F32)
-    last = stream1 + own_quarter(inv1, me)[:, None] * mixed_total
-    last = after(last, grad0)
-    mixed_own = dot_t(last.astype(BF16), order).astype(BF16)
-    mixed_half = jnp.concatenate([mixed_own, swap(mixed_own, "tensor", 2)], 0)
-    g_y = after(g_y, z_sent0, mixed_own, x_near)
-    g_x0, g_bc0, g_dt0, acc_x0, acc_bc0, acc_head0 = scan_bwd(
+    g_y, z_sent0, x_got, out_far = lax.optimization_barrier((g_y, z_sent0, x_got, out_far))
+    x_kept, x_next = scatter_first(x_kept_half, x_got)
+    x_near = swap(x_next, "dp", near_mask)
+    g_y = after(g_y, x_next)
+    mixed = lax.all_gather(after(mixed_own, grad0), "tensor", axis=0).reshape(length, features)
+    away1 = swap(after(columns_of(g_bc1, 1 - far), grad0), "tensor", 2)
+    g_x0, g_bc0, g_dt0, acc_x0, acc_bc0 = scan_bwd(
         me_row, g_y, x_pre0, bcdt_pre0, kept0, side, weights[0]
     )
-    away1 = after(columns_of(g_bc1, 1 - far), grad0)
-    away1 = swap(away1, "tensor", 2)
     away0 = swap(columns_of(g_bc0, 1 - far), "tensor", 2)
-    g_x0 = after(g_x0, out_got0, mixed_half, away1)
+    g_x0, away1, x_near, out_got0 = lax.optimization_barrier((g_x0, away1, x_near, out_got0))
     x_sent0 = sent_half(normed0, g_x0)
     x_got0 = swap(x_sent0, "dp", 1)
     g_x0 = after(g_x0, x_sent0)
     g_bcdt = jnp.concatenate([g_bc0, g_dt0], 1)
     sent = grad_rows(slice(half, length), g_gate0, g_x0, g_bcdt, 0).astype(BF16)
-    own = grad_rows(slice(0, half), after(g_gate0, sent), g_x0, g_bcdt, 0)
+    out_kept_half0 = grad_half(after(grad0, sent), scaled0, 0)
+    out_kept0, out_next0 = scatter_first(out_kept_half0, out_got0)
+    out_near0 = swap(out_next0, "dp", near_mask)
+    own = grad_rows(slice(0, half), after(g_gate0, out_next0), g_x0, g_bcdt, 0)
     mine = own + swap(sent, "tensor", 1).astype(F32)
     away = mine[quarter:].astype(BF16)
     got = swap(away, "tensor", 2)
-    normed_now, grad_now, _ = lax.optimization_barrier((normed0, grad0, away))
+    normed_now, z_got0, x_near, away0, _ = lax.optimization_barrier(
+        (normed0, z_got0, x_near, away0, away)
+    )
     z_kept0, z_next0 = scatter_first(grad_half(normed_now, g_gate0, 0), z_got0)
-    out_kept0, out_next0 = scatter_first(grad_half(grad_now, scaled0, 0), out_got0)
-    x_kept0, x_next0 = scatter_first(grad_half(normed_now, g_x0, 0), x_got0)
+    z_near0 = swap(z_next0, "dp", near_mask)
+    normed_now = after(normed_now, z_next0)
+    x_kept, x_next = scatter_first(x_kept, x_near)
+    x_kept_half0 = grad_half(normed_now, g_x0, 0)
+    x_kept_half0, out_near0, x_next = lax.optimization_barrier((x_kept_half0, out_near0, x_next))
+    x_far = swap(x_next, "dp", masks[-3])
+    out_kept0, out_next0 = scatter_first(out_kept0, out_near0)
+    out_far0 = swap(out_next0, "dp", masks[-3])
+    got, mine, x_got0, z_near0, out_next0 = lax.optimization_barrier(
+        (got, mine, x_got0, z_near0, out_next0)
+    )
     total = mine[:quarter] + got.astype(F32)
     rms = rms_of(stream0)
     normal = stream0 * rms
-    d_norm0 = jnp.sum(total * normal, 0)
     grown = total * gains[0]
     grad_stream = grad_stream + rms * (
         grown - normal * jnp.mean(grown * normal, -1, keepdims=True)
     )
     d_hidden = dot_t(grad_stream.astype(BF16), order).astype(BF16)
+    x_kept0, x_next0 = scatter_first(x_kept_half0, x_got0)
+    x_near0 = swap(x_next0, "dp", near_mask)
+    z_kept0, z_next0 = scatter_first(z_kept0, z_near0)
+    z_far0 = swap(z_next0, "dp", masks[-3])
+    total_now = after(total, d_hidden)
+    d_norm0 = jnp.sum(total_now * normal, 0)
     d_hidden = jnp.concatenate([d_hidden, swap(d_hidden, "tensor", 2)], 0)
     d_hidden = jnp.concatenate([d_hidden, swap(d_hidden, "tensor", 1)], 0)
-    d_hidden = reordered(d_hidden, me).astype(F32)
-    mixed = jnp.concatenate([mixed_half, swap(mixed_half, "tensor", 1)], 0)
-    mixed = reordered(mixed, me)
-
-    d_out1 = scatter_rest(out_kept, out_next, masks)
-    d_x1 = scatter_rest(*scatter_first(x_kept, x_near), masks[:1] + masks[2:])
-    d_out0 = scatter_rest(out_kept0, out_next0, masks)
-    d_z0 = scatter_rest(z_kept0, z_next0, masks)
-    d_x0 = scatter_rest(x_kept0, x_next0, masks)
+    d_hidden = restored(d_hidden, me).astype(F32)
+
+    def finished(kept, sent):
+        for mask in reversed(masks[:-3]):
+            kept, sent = scatter_first(kept, sent)
+            sent = swap(sent, "dp", mask)
+        return kept + sent.astype(F32)
+
+    x_kept0, x_next0 = scatter_first(x_kept0, x_near0)
+    d_out1 = finished(out_kept, out_far)
+    d_x1 = finished(x_kept, x_far)
+    d_z1 = finished(z_kept, z_far)
+    d_out0 = finished(out_kept0, out_far0)
+    d_z0 = finished(z_kept0, z_far0)
+    d_x0 = finished(x_kept0, swap(x_next0, "dp", masks[-3]))
 
     near_cols = jnp.concatenate([columns_of(v, far) for v in (g_bc0, g_bc1)], 1)
     away_cols = jnp.concatenate([away0, away1], 1)
     bc_sum = near_cols.astype(F32) + turned_over(away_cols, quarter).astype(F32)
-    across_sum = swap(after(bc_sum.astype(BF16), away), "tensor", 1)
+    across_sum = swap(bc_sum.astype(BF16), "tensor", 1)
     bc_sum = bc_sum + turned_over(across_sum, half).astype(F32)
     small_sent, small_kept = [], []
     for layer, (rows, g_dt) in enumerate(((normed0, g_dt0), (normed1, g_dt1))):
@@ -928,52 +992,21 @@
     small_kept, small_next = scatter_first(jnp.concatenate(small_kept, 1), small_got)
     d_small = scatter_rest(small_kept, small_next, masks)
     d_small = jnp.stack([d_small[:, layer * LANES : (layer + 1) * LANES] for layer in range(LAYERS)])
-    small_parts = [
-        (d_norm0, acc_x0, acc_bc0, acc_head0, d_gain0),
-        (d_norm1, acc_x1, acc_bc1, acc_head1, d_gain1),
-    ]
-
-    norm_part = mm(
-        jnp.stack([part[0] for part in small_parts]), order.astype(F32).T, PRECISE
-    )
-    pieces = []
-    for layer in range(LAYERS):
-        _, acc_x, acc_bc, acc_head, d_gain = small_parts[layer]
-        skips = acc_head[0].reshape(heads, HEAD_DIM).sum(1)
-        rates = -jnp.exp(a_log[layer])
-        pieces.append(
-            (
-                acc_x[:5].reshape(-1),
-                d_gain.reshape(-1),
-                jnp.concatenate([acc_head[1, :heads], acc_head[2, :heads] * rates, skips]),
-            )
-        )
+    found = jnp.array(offsets(masks), jnp.int32)
+    norm_part = jnp.stack([d_norm0, d_norm1]).reshape(LAYERS, len(found), 1, height)
+    here = (found ^ lax.axis_index("dp"))[:, None] == jnp.arange(len(found))[None]
+    norm_part = jnp.sum(jnp.where(here[None, :, :, None], norm_part, 0.0), 1)
     shared = jnp.concatenate(
-        [norm_part.reshape(-1)] + [small_parts[layer][2][:5].reshape(-1) for layer in range(LAYERS)]
-    )
-    flat = jnp.concatenate([tensor_sum(shared[None])[0]] + [v for piece in pieces for v in piece])
-    flat = dp_sum(flat[None])[0]
-
-    at = 0
-
-    def take(*shape):
-        nonlocal at
-        size = 1
-        for extent in shape:
-            size *= extent
-        values = flat[at : at + size].reshape(shape)
-        at += size
-        return values
-
-    d_norm_gain = take(LAYERS, features)
-    bc_acc = take(LAYERS, 5, 2 * STATE)
-    x_acc, gain_acc, head_acc = [], [], []
-    for layer in range(LAYERS):
-        x_acc.append(take(5, width))
-        gain_acc.append(take(width))
-        head_acc.append(take(3, heads))
-    x_acc = jnp.stack(x_acc)
-    head_acc = jnp.stack(head_acc)
+        [acc_bc0, acc_bc1, jnp.zeros((8, width - 4 * STATE), F32)], 1
+    )
+    shared = tensor_sum(jnp.concatenate([shared, norm_part.reshape(-1, width)], 0))
+    gains_part = jnp.concatenate([d_gain0, d_gain1], 0)
+    summed = dp_sum(jnp.concatenate([acc_x0, acc_x1, gains_part, shared], 0))
+    acc = summed[:16].reshape(LAYERS, 8, width)
+    shared = summed[16 + LAYERS :]
+    bc_acc = jnp.stack([shared[:8, : 2 * STATE], shared[:8, 2 * STATE : 4 * STATE]])
+    d_norm_gain = shared[8:].reshape(LAYERS, features)
+    d_skips = acc[:, 5].reshape(LAYERS, heads, HEAD_DIM).sum(2)
     own_width = STATE // 2
     return (
         mixed,
@@ -983,14 +1016,14 @@
         jnp.stack([d_x0, d_x1]),
         d_small[:, :, :own_width],
         d_small[:, :, own_width : own_width + heads],
-        x_acc[:, :4],
-        x_acc[:, 4],
+        acc[:, :4],
+        acc[:, 4],
         bc_acc[:, :4],
         bc_acc[:, 4],
-        head_acc[:, 0],
-        head_acc[:, 1],
-        head_acc[:, 2],
-        jnp.stack(gain_acc),
+        acc[:, 6, :heads],
+        acc[:, 7, :heads] * -jnp.exp(a_log),
+        d_skips,
+        summed[16 : 16 + LAYERS],
         jnp.stack([d_out0, d_out1]),
     )
 

time: 634 us -> 622 us (0.981)
  local copies, waits for them, and re-layouts: 65.6 us -> 37.5 us
  waiting for transfers between devices: 193 us -> 168 us
  starting transfers between devices: 66.7 us -> 82.9 us
  between operations: 3.89 us -> 17.4 us
  matrix products: 131 us -> 144 us
    ppermute x74 -> x72, waiting for transfers between devices: 193 us -> 168 us  [swap(): return lax.ppermute(values, axis, partners(lax.axis_size(axis), step))]
    ppermute x74 -> x72, starting transfers between devices: 66.7 us -> 82.8 us  [swap(): return lax.ppermute(values, axis, partners(lax.axis_size(axis), step))]
    unnamed x334 -> x365, local copies, waits for them, and re-layouts: 29.6 us -> 15.8 us
    dot_general x18, matrix products: 46.1 us -> 58.3 us  [dot_t(): lax.dot_general(lhs, rhs, (((1,), (1,)), ((), ())), preferred_element_typ...]
    concatenate x23 -> x21, other arithmetic: 25.5 us -> 17 us  [the longest x14 11.2 us: stage(): self.rows = jnp.concatenate([self.rows, got], 0)]
  transfers between devices with their start and end apart: 74 -> 73, of which waited for: 33 -> 31; matrix products, arithmetic and copies ran while one was open for 35% -> 33% of each run, Pallas kernels for 12% -> 12%
where the time goes in v3:
time: 622 us; the launch traced here: 612 us
  waiting for transfers between devices  168 us (27%)
  matrix products  144 us (23%)
  Pallas kernels  89.3 us (14%)
  starting transfers between devices  82.9 us (13%)
  other arithmetic  73.7 us (12%)
  local copies, waits for them, and re-layouts  37.5 us (6%)
  between operations  17.4 us (3%)
    ppermute x72, waiting for transfers between devices, swap(): return lax.ppermute(values, axis, partners(lax.axis_size(axis), step))  168 us
    ppermute x72, starting transfers between devices, swap(): return lax.ppermute(values, axis, partners(lax.axis_size(axis), step))  82.8 us
    dot_general x18, matrix products, dot_t(): lax.dot_general(lhs, rhs, (((1,), (1,)), ((), ())), preferred_element_typ...  58.3 us
    pallas_call x2, Pallas kernels, scan_bwd(): pl.pallas_call(scan_bwd_kernel, grid_spec=pltpu.PrefetchScalarGridSpec(nu...  53.7 us
    dot_general x10, matrix products, dot(): lax.dot_general(lhs, rhs, (((1,), (0,)), ((), ())), preferred_element_typ...  49.5 us
    dot_general x16, matrix products, grad_half(): return lax.dot_general(taken, grads, dims, preferred_element_type=F32)  33.9 us
    pallas_call x2, Pallas kernels, scan_fwd(): pl.pallas_call(scan_fwd_kernel, grid_spec=pltpu.PrefetchScalarGridSpec(nu...  26 us
    unnamed x365, local copies, waits for them, and re-layouts  15.8 us
  transfers between devices with their start and end apart: 73, of which 31 were waited for; matrix products, arithmetic and copies ran while one was open for 33% of the time, Pallas kernels for 12%

profile of v3, /device:TPU:0, one launch (start us, length us, event | category | flops | bytes accessed | tf_op | source)
XLA Modules:
  0.0 612.3 jit_solution(16560112332969537599)
XLA Ops:
  18.3 8.4 %collective-permute-done = bf16[192,768]{1,0:T(8,128)(2,1)S(1)} collective-permute-done((bf16[192,768]{1,0:T(8,128)(2,1)S(1)}, bf16[192,768]{1,0:T(8,128)(2,1)S(1)}, u32[]{:S(2)}, u32[]{:S(2)}) %collective-permute-start) | collective-permute-done | bytes 294944 | tf_op jit(solution)/shard_map/ppermute | solution.py:536
  41.4 5.7 collective-permute-done.1
  54.3 7.6 %convolution_convert_fusion.1 = bf16[1024,1536]{1,0:T(8,128)(2,1)S(1)} fusion(bf16[1024,1536]{1,0:T(8,128)(2,1)S(1)} %copy-done.64, bf16[1536,1536]{1,0:T(8,128)(2,1)} %fusion), kind=kOutput, calls=%fused_computation.10 | convolution fusion | flops 4833411072 | bytes 11010048 | tf_op jit(solution)/shard_map/dot_general | solution.py:640
  67.6 6.5 %convolution_convert_fusion = bf16[1024,1536]{1,0:T(8,128)(2,1)} fusion(bf16[1024,1536]{1,0:T(8,128)(2,1)S(1)} %copy-done.63, bf16[1536,1536]{1,0:T(8,128)(2,1)S(1)} %bitcast.170), kind=kOutput, calls=%fused_computation.9 | convolution fusion | flops 4833411072 | bytes 11010048 | tf_op jit(solution)/shard_map/dot_general | solution.py:640
  77.3 11.6 %collective-permute-done.16 = bf16[768,256]{0,1:T(8,128)(2,1)} collective-permute-done((bf16[768,256]{0,1:T(8,128)(2,1)S(1)}, bf16[768,256]{0,1:T(8,128)(2,1)}, u32[]{:S(2)}, u32[]{:S(2)}) %collective-permute-start.16) | collective-permute-done | bytes 393248 | tf_op jit(solution)/shard_map/ppermute | solution.py:536
  100.1 7.7 %collective-permute-done.8 = bf16[192,768]{1,0:T(8,128)(2,1)S(1)} collective-permute-done((bf16[192,768]{1,0:T(8,128)(2,1)}, bf16[192,768]{1,0:T(8,128)(2,1)S(1)}, u32[]{:S(2)}, u32[]{:S(2)}) %collective-permute-start.8) | collective-permute-done | bytes 294944 | tf_op jit(solution)/shard_map/ppermute | solution.py:536
  109.0 5.7 fusion.159.x_ref.x_tail_ref
  123.7 5.2 convolution_convert_fusion.7.gate_ref
  129.0 13.2 %scan_fwd.2 = (bf16[1024,768]{1,0:T(8,128)(2,1)S(1)}, bf16[1024,768]{1,0:T(8,128)(2,1)S(1)}, f32[8,1024]{1,0:T(8,128)S(1)}, bf16[8,128,768]{2,1,0:T(8,128)(2,1)S(1)}) custom-call(s32[1]{0:T(128)} %bitcast.me_ref, f32[1024,768]{1,0:T(8,128)} %fusion.159.x_ref.x_tail_ref, f32[1024,384]{1,0:T(8,128)} %fusion.175.bcdt_ref.bc_tail_ref, ...), custom_call_target="tpu_custom_call" | custom-call | flops 14092861440 | bytes 15728640 | tf_op jit(solution)/shard_map/scan_fwd/pallas_call | solution.py:185
  167.5 16.9 %collective-permute-done.12 = bf16[384,768]{1,0:T(8,128)(2,1)S(1)} collective-permute-done((bf16[384,768]{1,0:T(8,128)(2,1)S(1)}, bf16[384,768]{1,0:T(8,128)(2,1)S(1)}, u32[]{:S(2)}, u32[]{:S(2)}) %collective-permute-start.12) | collective-permute-done | bytes 589856 | tf_op jit(solution)/shard_map/ppermute | solution.py:536
  194.0 14.4 %collective-permute-done.26 = bf16[256,1536]{1,0:T(8,128)(2,1)S(1)} collective-permute-done((bf16[256,1536]{1,0:T(8,128)(2,1)S(1)}, bf16[256,1536]{1,0:T(8,128)(2,1)S(1)}, u32[]{:S(2)}, u32[]{:S(2)}) %collective-permute-start.26) | collective-permute-done | bytes 786464 | tf_op jit(solution)/shard_map/ppermute | solution.py:536
  208.5 4.8 collective-permute-done.27
  223.6 5.3 fusion.157.x_ref.x_tail_ref
  228.8 12.8 %scan_fwd.3 = (bf16[1024,768]{1,0:T(8,128)(2,1)S(1)}, bf16[1024,768]{1,0:T(8,128)(2,1)S(1)}, f32[8,1024]{1,0:T(8,128)S(1)}, bf16[8,128,768]{2,1,0:T(8,128)(2,1)S(1)}) custom-call(s32[1]{0:T(128)} %bitcast.me_ref, f32[1024,768]{1,0:T(8,128)} %fusion.157.x_ref.x_tail_ref, f32[1024,384]{1,0:T(8,128)} %fusion.176.bcdt_ref.bc_tail_ref, ...), custom_call_target="tpu_custom_call" | custom-call | flops 14092861440 | bytes 15728640 | tf_op jit(solution)/shard_map/scan_fwd/pallas_call | solution.py:185
  245.8 4.4 fusion.10
  262.4 4.8 gate_bwd.2
  271.8 26.7 %scan_bwd.2 = (bf16[1024,768]{1,0:T(8,128)(2,1)S(1)}, bf16[1024,256]{1,0:T(8,128)(2,1)S(1)}, bf16[1024,128]{1,0:T(8,128)(2,1)S(1)}, f32[8,768]{1,0:T(8,128)S(1)}, f32[8,256]{1,0:T(8,128)S(1)}) custom-call(s32[1]{0:T(128)} %bitcast.me_ref, bf16[1024,768]{1,0:T(8,128)(2,1)S(1)} %get-tuple-element.199.g_ref, f32[1024,768]{1,0:T(8,128)} %fusion.157.x_ref.x_tail_ref, ...), custom_call_target="tpu_custom_call" | custom-call | flops 28185722880 | bytes 15728640 | tf_op jit(solution)/shard_map/scan_bwd/pallas_call | solution.py:447
  307.9 5.1 fusion.13
  316.4 4.3 fusion.88
  323.2 5.5 fusion.6
  338.7 5.8 collective-permute-done.36
  345.8 4.5 collective-permute-done.35
  358.8 11.2 %collective-permute-done.39 = f32[256]{0:T(256)S(1)} collective-permute-done((f32[256]{0:T(256)S(1)}, f32[256]{0:T(256)S(1)}, u32[]{:S(2)}, u32[]{:S(2)}) %collective-permute-start.39) | collective-permute-done | bytes 1056 | tf_op jit(solution)/shard_map/ppermute | solution.py:536
  390.3 5.3 fusion.158.gs_ref
  395.6 4.8 gate_bwd.3
  408.8 27.0 %scan_bwd.3 = (bf16[1024,768]{1,0:T(8,128)(2,1)S(1)}, bf16[1024,256]{1,0:T(8,128)(2,1)S(1)}, bf16[1024,128]{1,0:T(8,128)(2,1)S(1)}, f32[8,768]{1,0:T(8,128)S(1)}, f32[8,256]{1,0:T(8,128)S(1)}) custom-call(s32[1]{0:T(128)} %bitcast.me_ref, bf16[1024,768]{1,0:T(8,128)(2,1)S(1)} %get-tuple-element.230.g_ref, f32[1024,768]{1,0:T(8,128)} %fusion.159.x_ref.x_tail_ref, ...), custom_call_target="tpu_custom_call" | custom-call | flops 28185722880 | bytes 15728640 | tf_op jit(solution)/shard_map/scan_bwd/pallas_call | solution.py:447
  482.7 8.8 %collective-permute-done.71 = bf16[192,768]{1,0:T(8,128)(2,1)} collective-permute-done((bf16[192,768]{1,0:T(8,128)(2,1)}, bf16[192,768]{1,0:T(8,128)(2,1)}, u32[]{:S(2)}, u32[]{:S(2)}) %collective-permute-start.71) | collective-permute-done | bytes 294944 | tf_op jit(solution)/shard_map/ppermute | solution.py:536
  498.3 9.5 %collective-permute-done.66 = bf16[192,768]{1,0:T(8,128)(2,1)S(1)} collective-permute-done((bf16[192,768]{1,0:T(8,128)(2,1)}, bf16[192,768]{1,0:T(8,128)(2,1)S(1)}, u32[]{:S(2)}, u32[]{:S(2)}) %collective-permute-start.66) | collective-permute-done | bytes 294944 | tf_op jit(solution)/shard_map/ppermute | solution.py:536
  518.1 5.5 convolution_convert_fusion.4
  533.4 9.3 %collective-permute-done.60 = f32[30,768]{1,0:T(8,128)S(1)} collective-permute-done((f32[30,768]{1,0:T(8,128)S(1)}, f32[30,768]{1,0:T(8,128)S(1)}, u32[]{:S(2)}, u32[]{:S(2)}) %collective-permute-start.60) | collective-permute-done | bytes 92192 | tf_op jit(solution)/shard_map/ppermute | solution.py:536
  551.3 10.4 %collective-permute-done.62 = f32[30,768]{1,0:T(8,128)S(1)} collective-permute-done((f32[30,768]{1,0:T(8,128)S(1)}, f32[30,768]{1,0:T(8,128)S(1)}, u32[]{:S(2)}, u32[]{:S(2)}) %collective-permute-start.62) | collective-permute-done | bytes 92192 | tf_op jit(solution)/shard_map/ppermute | solution.py:536
  579.8 10.8 %collective-permute-done.70 = bf16[192,256]{0,1:T(8,128)(2,1)S(1)} collective-permute-done((bf16[192,256]{0,1:T(8,128)(2,1)S(1)}, bf16[192,256]{0,1:T(8,128)(2,1)S(1)}, u32[]{:S(2)}, u32[]{:S(2)}) %collective-permute-start.70) | collective-permute-done | bytes 98336 | tf_op jit(solution)/shard_map/ppermute | solution.py:536
  (749 shorter events, 305.5 us)
Async XLA Ops:
  7.3 590.1 %all-gather.3.cloned.1.call-start = ((), (), s32[]{:S(2)}) async-start(), calls=%async_computation | async-start | bytes 3932160 | tf_op jit(solution)/shard_map/all_gather | solution.py:911
  14.5 36.0 %collective-permute-start.3 = (bf16[192,768]{1,0:T(8,128)(2,1)S(1)}, bf16[192,768]{1,0:T(8,128)(2,1)S(1)}, u32[]{:S(2)}, u32[]{:S(2)}) collective-permute-start(bf16[192,768]{1,0:T(8,128)(2,1)S(1)} %get-tuple-element.380), channel_id=1, source_target_pairs={{0,1},{1,0},{2,3},{3,2},{4,5},{5,4},{6,7},{7,6},{8,9},{9,8},{10,11... | collective-permute-start | bytes 884744 | tf_op jit(solution)/shard_map/ppermute | solution.py:536
  52.8 56.1 %collective-permute-start.15 = (bf16[768,768]{1,0:T(8,128)(2,1)}, bf16[768,768]{1,0:T(8,128)(2,1)}, u32[]{:S(2)}, u32[]{:S(2)}) collective-permute-start(bf16[768,768]{1,0:T(8,128)(2,1)} %pad_maximum_fusion.13), channel_id=1, source_target_pairs={{0,1},{1,0},{2,3},{3,2},{4,5},{5,4},{6,7},{7,6},{8,9},{9,8},{10,11... | collective-permute-start | bytes 3538952 | tf_op jit(solution)/shard_map/ppermute | solution.py:536
  62.1 26.8 %collective-permute-start.16 = (bf16[768,256]{0,1:T(8,128)(2,1)S(1)}, bf16[768,256]{0,1:T(8,128)(2,1)}, u32[]{:S(2)}, u32[]{:S(2)}) collective-permute-start(bf16[768,256]{0,1:T(8,128)(2,1)S(1)} %pad_maximum_fusion.32), channel_id=1, source_target_pairs={{0,1},{1,0},{2,3},{3,2},{4,5},{5,4},{6,7},{7,6},{8,9},{9,8},{10,11... | collective-permute-start | bytes 1179656 | tf_op jit(solution)/shard_map/ppermute | solution.py:536
  65.5 27.5 %collective-permute-start.6 = (bf16[384,768]{1,0:T(8,128)(2,1)}, bf16[384,768]{1,0:T(8,128)(2,1)}, u32[]{:S(2)}, u32[]{:S(2)}) collective-permute-start(bf16[384,768]{1,0:T(8,128)(2,1)} %pad_maximum_fusion.24), channel_id=1, source_target_pairs={{0,2},{1,3},{2,0},{3,1},{4,6},{5,7},{6,4},{7,5},{8,10},{9,11},{10,... | collective-permute-start | bytes 1769480 | tf_op jit(solution)/shard_map/ppermute | solution.py:536
  65.6 26.4 %collective-permute-start.7 = (bf16[192,768]{1,0:T(8,128)(2,1)S(1)}, bf16[192,768]{1,0:T(8,128)(2,1)}, u32[]{:S(2)}, u32[]{:S(2)}) collective-permute-start(bf16[192,768]{1,0:T(8,128)(2,1)S(1)} %get-tuple-element.154), channel_id=1, source_target_pairs={{0,4},{1,5},{2,6},{3,7},{4,0},{5,1},{6,2},{7,3},{8,12},{9,13},{10,... | collective-permute-start | bytes 884744 | tf_op jit(solution)/shard_map/ppermute | solution.py:536
  95.3 28.5 %collective-permute-start.19 = (bf16[768,768]{1,0:T(8,128)(2,1)S(1)}, bf16[768,768]{1,0:T(8,128)(2,1)S(1)}, u32[]{:S(2)}, u32[]{:S(2)}) collective-permute-start(bf16[768,768]{1,0:T(8,128)(2,1)S(1)} %pad_maximum_fusion.14), channel_id=1, source_target_pairs={{0,1},{1,0},{2,3},{3,2},{4,5},{5,4},{6,7},{7,6},{8,9},{9,8},{10,11... | collective-permute-start | bytes 3538952 | tf_op jit(solution)/shard_map/ppermute | solution.py:536
  114.7 27.6 %collective-permute-start.10 = (bf16[384,768]{1,0:T(8,128)(2,1)S(1)}, bf16[384,768]{1,0:T(8,128)(2,1)S(1)}, u32[]{:S(2)}, u32[]{:S(2)}) collective-permute-start(bf16[384,768]{1,0:T(8,128)(2,1)S(1)} %pad_maximum_fusion.25), channel_id=1, source_target_pairs={{0,2},{1,3},{2,0},{3,1},{4,6},{5,7},{6,4},{7,5},{8,10},{9,11},{10,... | collective-permute-start | bytes 1769480 | tf_op jit(solution)/shard_map/ppermute | solution.py:536
  114.8 27.5 %collective-permute-start.11 = (bf16[192,768]{1,0:T(8,128)(2,1)S(1)}, bf16[192,768]{1,0:T(8,128)(2,1)S(1)}, u32[]{:S(2)}, u32[]{:S(2)}) collective-permute-start(bf16[192,768]{1,0:T(8,128)(2,1)S(1)} %copy-done.81), channel_id=1, source_target_pairs={{0,4},{1,5},{2,6},{3,7},{4,0},{5,1},{6,2},{7,3},{8,12},{9,13},{10,... | collective-permute-start | bytes 884744 | tf_op jit(solution)/shard_map/ppermute | solution.py:536
  116.7 29.8 %collective-permute-start.22 = (bf16[768,768]{1,0:T(8,128)(2,1)S(1)}, bf16[768,768]{1,0:T(8,128)(2,1)S(1)}, u32[]{:S(2)}, u32[]{:S(2)}) collective-permute-start(bf16[768,768]{1,0:T(8,128)(2,1)S(1)} %pad_maximum_fusion.15), channel_id=1, source_target_pairs={{0,1},{1,0},{2,3},{3,2},{4,5},{5,4},{6,7},{7,6},{8,9},{9,8},{10,11... | collective-permute-start | bytes 3538952 | tf_op jit(solution)/shard_map/ppermute | solution.py:536
  155.5 29.0 %collective-permute-start.12 = (bf16[384,768]{1,0:T(8,128)(2,1)S(1)}, bf16[384,768]{1,0:T(8,128)(2,1)S(1)}, u32[]{:S(2)}, u32[]{:S(2)}) collective-permute-start(bf16[384,768]{1,0:T(8,128)(2,1)S(1)} %pad_maximum_fusion.23), channel_id=1, source_target_pairs={{0,4},{1,5},{2,6},{3,7},{4,0},{5,1},{6,2},{7,3},{8,12},{9,13},{10,... | collective-permute-start | bytes 1769480 | tf_op jit(solution)/shard_map/ppermute | solution.py:536
  157.9 26.7 %collective-permute-start.13 = (bf16[384,768]{1,0:T(8,128)(2,1)S(1)}, bf16[384,768]{1,0:T(8,128)(2,1)S(1)}, u32[]{:S(2)}, u32[]{:S(2)}) collective-permute-start(bf16[384,768]{1,0:T(8,128)(2,1)S(1)} %pad_maximum_fusion.27), channel_id=1, source_target_pairs={{0,2},{1,3},{2,0},{3,1},{4,6},{5,7},{6,4},{7,5},{8,10},{9,11},{10,... | collective-permute-start | bytes 1769480 | tf_op jit(solution)/shard_map/ppermute | solution.py:536
  160.9 27.7 %collective-permute-start.25 = (bf16[768,768]{1,0:T(8,128)(2,1)S(1)}, bf16[768,768]{1,0:T(8,128)(2,1)S(1)}, u32[]{:S(2)}, u32[]{:S(2)}) collective-permute-start(bf16[768,768]{1,0:T(8,128)(2,1)S(1)} %pad_maximum_fusion.16), channel_id=1, source_target_pairs={{0,1},{1,0},{2,3},{3,2},{4,5},{5,4},{6,7},{7,6},{8,9},{9,8},{10,11... | collective-permute-start | bytes 3538952 | tf_op jit(solution)/shard_map/ppermute | solution.py:536
  184.5 28.8 %collective-permute-start.14 = (bf16[768,768]{1,0:T(8,128)(2,1)S(1)}, bf16[768,768]{1,0:T(8,128)(2,1)S(1)}, u32[]{:S(2)}, u32[]{:S(2)}) collective-permute-start(bf16[768,768]{1,0:T(8,128)(2,1)S(1)} %pad_maximum_fusion.12), channel_id=1, source_target_pairs={{0,2},{1,3},{2,0},{3,1},{4,6},{5,7},{6,4},{7,5},{8,10},{9,11},{10,... | collective-permute-start | bytes 3538952 | tf_op jit(solution)/shard_map/ppermute | solution.py:536
  185.9 27.4 %collective-permute-start.27 = (bf16[768,768]{1,0:T(8,128)(2,1)S(1)}, bf16[768,768]{1,0:T(8,128)(2,1)S(1)}, u32[]{:S(2)}, u32[]{:S(2)}) collective-permute-start(bf16[768,768]{1,0:T(8,128)(2,1)S(1)} %pad_maximum_fusion.17), channel_id=1, source_target_pairs={{0,1},{1,0},{2,3},{3,2},{4,5},{5,4},{6,7},{7,6},{8,9},{9,8},{10,11... | collective-permute-start | bytes 3538952 | tf_op jit(solution)/shard_map/ppermute | solution.py:536
  268.7 35.3 %collective-permute-start.32 = (bf16[768,768]{1,0:T(8,128)(2,1)S(1)}, bf16[768,768]{1,0:T(8,128)(2,1)S(1)}, u32[]{:S(2)}, u32[]{:S(2)}) collective-permute-start(bf16[768,768]{1,0:T(8,128)(2,1)S(1)} %convolution_convert_fusion.10), channel_id=1, source_target_pairs={{0,1},{1,0},{2,3},{3,2},{4,5},{5,4},{6,7},{7,6},{8,9},{9,8},{10,11... | collective-permute-start | bytes 3538952 | tf_op jit(solution)/shard_map/ppermute | solution.py:536
  270.3 33.8 %collective-permute-start.33 = (bf16[256,1536]{1,0:T(8,128)(2,1)S(1)}, bf16[256,1536]{1,0:T(8,128)(2,1)S(1)}, u32[]{:S(2)}, u32[]{:S(2)}) collective-permute-start(bf16[256,1536]{1,0:T(8,128)(2,1)S(1)} %copy-done.114), channel_id=1, source_target_pairs={{0,16},{8,24},{16,0},{24,8},{1,17},{9,25},{17,1},{25,9},{2,18},{10... | collective-permute-start | bytes 2359304 | tf_op jit(solution)/shard_map/ppermute | solution.py:536
  315.8 28.7 %collective-permute-start.36 = (bf16[768,768]{1,0:T(8,128)(2,1)}, bf16[768,768]{1,0:T(8,128)(2,1)}, u32[]{:S(2)}, u32[]{:S(2)}) collective-permute-start(bf16[768,768]{1,0:T(8,128)(2,1)} %fusion.53), channel_id=1, source_target_pairs={{0,1},{1,0},{2,3},{3,2},{4,5},{5,4},{6,7},{7,6},{8,9},{9,8},{10,11... | collective-permute-start | bytes 3538952 | tf_op jit(solution)/shard_map/ppermute | solution.py:536
  375.0 29.9 %collective-permute-start.44 = (bf16[768,768]{1,0:T(8,128)(2,1)}, bf16[768,768]{1,0:T(8,128)(2,1)}, u32[]{:S(2)}, u32[]{:S(2)}) collective-permute-start(bf16[768,768]{1,0:T(8,128)(2,1)} %fusion.56), channel_id=1, source_target_pairs={{0,1},{1,0},{2,3},{3,2},{4,5},{5,4},{6,7},{7,6},{8,9},{9,8},{10,11... | collective-permute-start | bytes 3538952 | tf_op jit(solution)/shard_map/ppermute | solution.py:536
  379.9 25.0 %collective-permute-start.45 = (bf16[192,768]{1,0:T(8,128)(2,1)}, bf16[192,768]{1,0:T(8,128)(2,1)}, u32[]{:S(2)}, u32[]{:S(2)}) collective-permute-start(bf16[192,768]{1,0:T(8,128)(2,1)} %slice.1029), channel_id=1, source_target_pairs={{0,4},{1,5},{2,6},{3,7},{4,0},{5,1},{6,2},{7,3},{8,12},{9,13},{10,... | collective-permute-start | bytes 884744 | tf_op jit(solution)/shard_map/ppermute | solution.py:536
  388.7 50.1 %collective-permute-start.48 = (bf16[768,768]{1,0:T(8,128)(2,1)}, bf16[768,768]{1,0:T(8,128)(2,1)}, u32[]{:S(2)}, u32[]{:S(2)}) collective-permute-start(bf16[768,768]{1,0:T(8,128)(2,1)} %fusion.59), channel_id=1, source_target_pairs={{0,1},{1,0},{2,3},{3,2},{4,5},{5,4},{6,7},{7,6},{8,9},{9,8},{10,11... | collective-permute-start | bytes 3538952 | tf_op jit(solution)/shard_map/ppermute | solution.py:536
  388.7 50.1 %collective-permute-start.46 = (bf16[1024,128]{1,0:T(8,128)(2,1)S(1)}, bf16[1024,128]{1,0:T(8,128)(2,1)S(1)}, u32[]{:S(2)}, u32[]{:S(2)}) collective-permute-start(bf16[1024,128]{1,0:T(8,128)(2,1)S(1)} %copy-done.129), channel_id=1, source_target_pairs={{0,16},{8,24},{16,0},{24,8},{1,17},{9,25},{17,1},{25,9},{2,18},{10... | collective-permute-start | bytes 786440 | tf_op jit(solution)/shard_map/ppermute | solution.py:536
  402.9 64.1 %collective-permute-start.52 = (bf16[768,768]{1,0:T(8,128)(2,1)}, bf16[768,768]{1,0:T(8,128)(2,1)}, u32[]{:S(2)}, u32[]{:S(2)}) collective-permute-start(bf16[768,768]{1,0:T(8,128)(2,1)} %convolution_convert_fusion.9), channel_id=1, source_target_pairs={{0,1},{1,0},{2,3},{3,2},{4,5},{5,4},{6,7},{7,6},{8,9},{9,8},{10,11... | collective-permute-start | bytes 3538952 | tf_op jit(solution)/shard_map/ppermute | solution.py:536
  406.6 32.2 %collective-permute-start.47 = (bf16[384,768]{1,0:T(8,128)(2,1)S(1)}, bf16[384,768]{1,0:T(8,128)(2,1)S(1)}, u32[]{:S(2)}, u32[]{:S(2)}) collective-permute-start(bf16[384,768]{1,0:T(8,128)(2,1)S(1)} %slice.1022), channel_id=1, source_target_pairs={{0,2},{1,3},{2,0},{3,1},{4,6},{5,7},{6,4},{7,5},{8,10},{9,11},{10,... | collective-permute-start | bytes 1769480 | tf_op jit(solution)/shard_map/ppermute | solution.py:536
  436.6 30.4 %collective-permute-start.53 = (bf16[1024,128]{1,0:T(8,128)(2,1)}, bf16[1024,128]{1,0:T(8,128)(2,1)}, u32[]{:S(2)}, u32[]{:S(2)}) collective-permute-start(bf16[1024,128]{1,0:T(8,128)(2,1)} %get-tuple-element.390), channel_id=1, source_target_pairs={{0,16},{8,24},{16,0},{24,8},{1,17},{9,25},{17,1},{25,9},{2,18},{10... | collective-permute-start | bytes 786440 | tf_op jit(solution)/shard_map/ppermute | solution.py:536
  457.7 58.2 %collective-permute-start.51 = (bf16[768,768]{1,0:T(8,128)(2,1)}, bf16[768,768]{1,0:T(8,128)(2,1)}, u32[]{:S(2)}, u32[]{:S(2)}) collective-permute-start(bf16[768,768]{1,0:T(8,128)(2,1)} %convolution_convert_fusion.8), channel_id=1, source_target_pairs={{0,1},{1,0},{2,3},{3,2},{4,5},{5,4},{6,7},{7,6},{8,9},{9,8},{10,11... | collective-permute-start | bytes 3538952 | tf_op jit(solution)/shard_map/ppermute | solution.py:536
  471.1 44.8 %collective-permute-start.54 = (bf16[384,768]{1,0:T(8,128)(2,1)}, bf16[384,768]{1,0:T(8,128)(2,1)}, u32[]{:S(2)}, u32[]{:S(2)}) collective-permute-start(bf16[384,768]{1,0:T(8,128)(2,1)} %slice.1020), channel_id=1, source_target_pairs={{0,2},{1,3},{2,0},{3,1},{4,6},{5,7},{6,4},{7,5},{8,10},{9,11},{10,... | collective-permute-start | bytes 1769480 | tf_op jit(solution)/shard_map/ppermute | solution.py:536
  471.9 44.0 %collective-permute-start.50 = (bf16[256,1536]{1,0:T(8,128)(2,1)}, bf16[256,1536]{1,0:T(8,128)(2,1)}, u32[]{:S(2)}, u32[]{:S(2)}) collective-permute-start(bf16[256,1536]{1,0:T(8,128)(2,1)} %slice.1015), channel_id=1, source_target_pairs={{0,16},{8,24},{16,0},{24,8},{1,17},{9,25},{17,1},{25,9},{2,18},{10... | collective-permute-start | bytes 2359304 | tf_op jit(solution)/shard_map/ppermute | solution.py:536
  482.6 26.1 %collective-permute-start.67 = (bf16[1024,256]{1,0:T(8,128)(2,1)S(1)}, bf16[1024,256]{1,0:T(8,128)(2,1)S(1)}, u32[]{:S(2)}, u32[]{:S(2)}) collective-permute-start(bf16[1024,256]{1,0:T(8,128)(2,1)S(1)} %fusion.75), channel_id=1, source_target_pairs={{0,8},{8,0},{16,24},{24,16},{1,9},{9,1},{17,25},{25,17},{2,10},{10... | collective-permute-start | bytes 1572872 | tf_op jit(solution)/shard_map/ppermute | solution.py:536
  528.4 43.3 %collective-permute-start.56 = (bf16[256,1536]{1,0:T(8,128)(2,1)}, bf16[256,1536]{1,0:T(8,128)(2,1)}, u32[]{:S(2)}, u32[]{:S(2)}) collective-permute-start(bf16[256,1536]{1,0:T(8,128)(2,1)} %convolution_convert_fusion.4), channel_id=1, source_target_pairs={{0,16},{8,24},{16,0},{24,8},{1,17},{9,25},{17,1},{25,9},{2,18},{10... | collective-permute-start | bytes 2359304 | tf_op jit(solution)/shard_map/ppermute | solution.py:536
  529.4 37.9 %collective-permute-start.68 = (bf16[768,256]{0,1:T(8,128)(2,1)}, bf16[768,256]{0,1:T(8,128)(2,1)}, u32[]{:S(2)}, u32[]{:S(2)}) collective-permute-start(bf16[768,256]{0,1:T(8,128)(2,1)} %pad_maximum_fusion.33), channel_id=1, source_target_pairs={{0,1},{1,0},{2,3},{3,2},{4,5},{5,4},{6,7},{7,6},{8,9},{9,8},{10,11... | collective-permute-start | bytes 1179656 | tf_op jit(solution)/shard_map/ppermute | solution.py:536
  545.8 32.1 %collective-permute-start.64 = (bf16[384,768]{1,0:T(8,128)(2,1)}, bf16[384,768]{1,0:T(8,128)(2,1)}, u32[]{:S(2)}, u32[]{:S(2)}) collective-permute-start(bf16[384,768]{1,0:T(8,128)(2,1)} %slice.1019), channel_id=1, source_target_pairs={{0,2},{1,3},{2,0},{3,1},{4,6},{5,7},{6,4},{7,5},{8,10},{9,11},{10,... | collective-permute-start | bytes 1769480 | tf_op jit(solution)/shard_map/ppermute | solution.py:536
  (215 other events, 2878.8 us)
Sparse Core Ops, SparseCore 0:
  450.2 31.1 all-gather.2

commit v4 on v3

--- a/solution.py
+++ b/solution.py
@@ -47,16 +47,11 @@
     return mm(parts.astype(BF16), spread)
 
 
-def shifted_back(joined, offset):
-    return joined[TAIL - offset : TAIL - offset + CHUNK]
-
-
-def conv_pre(joined, taps, bias_row, aux):
-    summed = bias_row + taps[0:1] * joined[TAIL:]
+def conv_pre(joined_ref, at, taps, bias_row, aux):
+    summed = bias_row + taps[0:1] * joined_ref[TAIL:, at]
     for offset in range(1, 4):
-        summed = summed + taps[offset : offset + 1] * (
-            shifted_back(joined, offset) * aux[:, offset : offset + 1]
-        )
+        moved = joined_ref[TAIL - offset : TAIL - offset + CHUNK, at]
+        summed = summed + taps[offset : offset + 1] * (moved * aux[:, offset : offset + 1])
     return summed
 
 
@@ -67,13 +62,27 @@
     )
 
 
+def parts_of(values, count):
+    parts = []
+    for _ in range(count):
+        low = values.astype(BF16)
+        parts.append(low)
+        values = values - low.astype(F32)
+    return jnp.concatenate(parts, 0)
+
+
+def order_masks():
+    row = iota((CHUNK, CHUNK), 0)
+    col = iota((CHUNK, CHUNK), 1)
+    return row, col
+
+
 def step_values(dt_ref, head_ref):
     raw = dt_ref + head_ref[0:1]
     dt = jnp.maximum(raw, 0.0) + jnp.log1p(jnp.exp(-jnp.abs(raw)))
-    row = iota((CHUNK, CHUNK), 0)
-    col = iota((CHUNK, CHUNK), 1)
-    lower = (row >= col).astype(F32)
-    log_decay = mm(lower, dt * head_ref[1:2], PRECISE)
+    row, col = order_masks()
+    lower = (row >= col).astype(BF16)
+    log_decay = mm(jnp.concatenate([lower] * 3, 1), parts_of(dt * head_ref[1:2], 3))
     return raw, dt, log_decay, row, col
 
 
@@ -99,6 +108,7 @@
     state,
     tail_x,
     tail_bc,
+    ending_ref,
 ):
     width = x_ref.shape[1]
 
@@ -110,9 +120,9 @@
 
     aux = aux_ref[...]
     bc_now = bcdt_ref[:, : 2 * STATE]
-    joined_bc = jnp.concatenate([tail_bc[...], bc_now], 0)
-    tail_bc[...] = bc_now[CHUNK - TAIL :]
-    bc_pre = conv_pre(joined_bc, bc_taps_ref[...], bc_bias_ref[...], aux)
+    tail_bc[:TAIL] = tail_bc[CHUNK:]
+    tail_bc[TAIL:] = bc_now
+    bc_pre = conv_pre(tail_bc, slice(None), bc_taps_ref[...], bc_bias_ref[...], aux)
     bc = bc_pre * jax.nn.sigmoid(bc_pre)
     b_low = bc[:, :STATE].astype(BF16)
     c_low = bc[:, STATE:].astype(BF16)
@@ -132,10 +142,9 @@
     squares = jnp.zeros((CHUNK, LANES), F32)
     for pair in range(width // LANES):
         at = slice(pair * LANES, (pair + 1) * LANES)
-        now = x_ref[:, at]
-        joined = jnp.concatenate([tail_x[:, at], now], 0)
-        tail_x[:, at] = now[CHUNK - TAIL :]
-        pre = conv_pre(joined, taps_ref[:, at], bias_ref[:, at], aux)
+        tail_x[:TAIL, at] = tail_x[CHUNK:, at]
+        tail_x[TAIL:, at] = x_ref[:, at]
+        pre = conv_pre(tail_x, at, taps_ref[:, at], bias_ref[:, at], aux)
         x_conv = pre * jax.nn.sigmoid(pre)
         inputs = x_conv * dt_wide[:, at]
         mats = []
@@ -145,13 +154,13 @@
         local = mm(jnp.concatenate(mats, 1), halves_rows(inputs.astype(BF16), low_lanes))
         y = local + carried[:, at] * reach[:, at] + skip_ref[:, at] * x_conv
         y_ref[:, at] = y.astype(y_ref.dtype)
-        ending = (inputs * to_end[:, at]).astype(BF16)
-        state[:, at] = state[:, at] * reach[CHUNK - 1 :, at] + mm(b_turned, ending)
+        ending_ref[:, at] = (inputs * to_end[:, at]).astype(BF16)
         gate = gate_ref[:, at].astype(F32)
         gated = y * (gate * jax.nn.sigmoid(gate))
         grown = gated * gain_ref[:, at]
         u_ref[:, at] = grown.astype(BF16)
         squares = squares + gated * gated
+    state[...] = state[...] * reach[CHUNK - 1 :] + mm(b_turned, ending_ref[...])
     ones = jnp.ones((8, LANES), F32)
     sums = lax.dot_general(
         ones, squares, (((1,), (1,)), ((), ())), precision=PRECISE, preferred_element_type=F32
@@ -196,8 +205,9 @@
             ],
             scratch_shapes=[
                 pltpu.VMEM((STATE, width), F32),
-                pltpu.VMEM((TAIL, width), F32),
-                pltpu.VMEM((TAIL, 2 * STATE), F32),
+                pltpu.VMEM((TAIL + CHUNK, width), F32),
+                pltpu.VMEM((TAIL + CHUNK, 2 * STATE), F32),
+                pltpu.VMEM((CHUNK, width), BF16),
             ],
         ),
         out_shape=[
@@ -270,14 +280,15 @@
     )(me, gs, y, gate_pre, columns, gain)
 
 
-def conv_bwd(joined, joined_grad, grad, taps, aux, acc_ref, at):
+def conv_bwd(joined_ref, later_ref, grad, taps, aux, acc_ref, at):
     acc_ref[4:5, at] += jnp.sum(grad, 0, keepdims=True)
-    acc_ref[0:1, at] += jnp.sum(grad * joined[TAIL:], 0, keepdims=True)
+    acc_ref[0:1, at] += jnp.sum(grad * joined_ref[TAIL:, at], 0, keepdims=True)
     result = taps[0:1] * grad
     for offset in range(1, 4):
-        moved = shifted_back(joined, offset) * aux[:, offset : offset + 1]
+        moved = joined_ref[TAIL - offset : TAIL - offset + CHUNK, at]
+        moved = moved * aux[:, offset : offset + 1]
         acc_ref[offset : offset + 1, at] += jnp.sum(grad * moved, 0, keepdims=True)
-        later = joined_grad[offset : offset + CHUNK] * aux[:, 5 + offset : 6 + offset]
+        later = later_ref[offset : offset + CHUNK, at] * aux[:, 5 + offset : 6 + offset]
         result = result + taps[offset : offset + 1] * later
     return result
 
@@ -308,6 +319,14 @@
     grad_state,
     next_x,
     next_bc,
+    joined_x,
+    joined_bc,
+    conv_ref,
+    slope_ref,
+    inputs_ref,
+    coming_ref,
+    ending_ref,
+    sums_ref,
 ):
     width = x_ref.shape[1]
 
@@ -320,8 +339,9 @@
         accbc_ref[...] = jnp.zeros_like(accbc_ref)
 
     aux = aux_ref[...]
-    joined_bc = jnp.concatenate([bc_tail_ref[:, : 2 * STATE], bcdt_ref[:, : 2 * STATE]], 0)
-    bc_pre = conv_pre(joined_bc, bc_taps_ref[...], bc_bias_ref[...], aux)
+    joined_bc[:TAIL] = bc_tail_ref[:, : 2 * STATE]
+    joined_bc[TAIL:] = bcdt_ref[:, : 2 * STATE]
+    bc_pre = conv_pre(joined_bc, slice(None), bc_taps_ref[...], bc_bias_ref[...], aux)
     bc_sig = jax.nn.sigmoid(bc_pre)
     bc = bc_pre * bc_sig
     b_low = bc[:, :STATE].astype(BF16)
@@ -337,24 +357,39 @@
     to_end = expand(jnp.exp(log_decay[CHUNK - 1 :] - log_decay) * aux[:, 5:6], spread)
     low_lanes = iota((CHUNK, LANES), 1) < HEAD_DIM
     lane = iota((CHUNK, LANES), 1)
+    for pair in range(width // LANES):
+        at = slice(pair * LANES, (pair + 1) * LANES)
+        joined_x[:TAIL, at] = x_tail_ref[:, at]
+        joined_x[TAIL:, at] = x_ref[:, at]
+        pre = conv_pre(joined_x, at, taps_ref[:, at], bias_ref[:, at], aux)
+        sig = jax.nn.sigmoid(pre)
+        x_conv = pre * sig
+        inputs = x_conv * dt_wide[:, at]
+        conv_ref[:, at] = x_conv
+        slope_ref[:, at] = sig * (1.0 + pre * (1.0 - sig))
+        inputs_ref[:, at] = inputs.astype(BF16)
+        ending_ref[:, at] = (inputs * to_end[:, at]).astype(BF16)
+        coming_ref[:, at] = (g_ref[:, at].astype(F32) * reach[:, at]).astype(BF16)
+    state_low = kept_ref[0]
+    grad_state_low = grad_state[...].astype(BF16)
+    coming_low = coming_ref[...]
+    ending_low = ending_ref[...]
+    carried = mm(c_low, state_low)
+    leaving = mm(b_low, grad_state_low)
+    grad_c = mm_t(coming_low, state_low)
+    grad_b = mm_t(ending_low, grad_state_low)
+    last = reach[CHUNK - 1 :]
+    passed = jnp.sum(grad_state[...] * state_low.astype(F32), 0, keepdims=True) * last
+    through = mm_t(jnp.broadcast_to(passed, (8, width)).astype(BF16), spread)
+    grad_state[...] = grad_state[...] * last + mm(c_turned, coming_low)
     grad_meet = jnp.zeros((CHUNK, CHUNK), F32)
-    grad_b = jnp.zeros((CHUNK, STATE), F32)
-    grad_c = jnp.zeros((CHUNK, STATE), F32)
     col_sums = jnp.zeros((CHUNK, LANES), F32)
     row_sums = jnp.zeros((LANES, CHUNK), F32)
-    head_sums = jnp.zeros((3 * CHUNK, LANES), F32)
-    through = jnp.zeros((8, LANES), F32)
     head_row = iota((LANES, CHUNK), 0)
     for pair in range(width // LANES):
         at = slice(pair * LANES, (pair + 1) * LANES)
-        joined = jnp.concatenate([x_tail_ref[:, at], x_ref[:, at]], 0)
-        pre = conv_pre(joined, taps_ref[:, at], bias_ref[:, at], aux)
-        sig = jax.nn.sigmoid(pre)
-        x_conv = pre * sig
-        inputs = x_conv * dt_wide[:, at]
         g_low = g_ref[:, at]
-        g = g_low.astype(F32)
-        grad_mats = mm_t(halves_rows(inputs.astype(BF16), low_lanes), g_low)
+        grad_mats = mm_t(halves_rows(inputs_ref[:, at], low_lanes), g_low)
         mats = []
         for member in range(2):
             head = 2 * pair + member
@@ -367,43 +402,36 @@
             col_sums = jnp.where(lane == head, jnp.sum(product, 1, keepdims=True), col_sums)
             row_sums = jnp.where(head_row == head, jnp.sum(product, 0, keepdims=True), row_sums)
         local = mm(jnp.concatenate(mats, 1), halves_rows(g_low, low_lanes))
-        reach_now = reach[:, at]
-        to_end_now = to_end[:, at]
-        state_low = kept_ref[0, :, at]
-        coming = g * reach_now
-        coming_low = coming.astype(BF16)
-        carried = mm(c_low, state_low)
-        grad_c = grad_c + mm_t(coming_low, state_low)
-        grad_state_now = grad_state[:, at]
-        grad_state_low = grad_state_now.astype(BF16)
-        leaving = mm(b_low, grad_state_low)
-        ending = inputs * to_end_now
-        grad_b = grad_b + mm_t(ending.astype(BF16), grad_state_low)
-        last = reach_now[CHUNK - 1 :]
-        passed = jnp.sum(grad_state_now * state_low.astype(F32), 0, keepdims=True) * last
-        through = through + mm_t(
-            jnp.broadcast_to(passed, (8, LANES)).astype(BF16), spread[:, at]
-        )
-        grad_state[:, at] = grad_state_now * last + mm(c_turned, coming_low)
-        grad_inputs = local + leaving * to_end_now
-        stacked = jnp.concatenate([coming * carried, ending * leaving, grad_inputs * x_conv], 0)
-        head_sums = head_sums + mm_t(stacked.astype(BF16), spread[:, at])
+        g = g_low.astype(F32)
+        x_conv = conv_ref[:, at]
+        leaving_now = leaving[:, at]
+        grad_inputs = local + leaving_now * to_end[:, at]
+        sums_ref[:CHUNK, at] = (coming_ref[:, at].astype(F32) * carried[:, at]).astype(BF16)
+        sums_ref[CHUNK : 2 * CHUNK, at] = (
+            ending_ref[:, at].astype(F32) * leaving_now
+        ).astype(BF16)
+        sums_ref[2 * CHUNK :, at] = (grad_inputs * x_conv).astype(BF16)
         accx_ref[5:6, at] += jnp.sum(g * x_conv, 0, keepdims=True)
-        grad_conv = (grad_inputs * dt_wide[:, at] + g * skip_ref[:, at]) * (
-            sig * (1.0 + pre * (1.0 - sig))
-        )
-        joined_grad = jnp.concatenate([grad_conv, next_x[:, at]], 0)
-        next_x[:, at] = grad_conv[:TAIL]
+        grad_conv = (grad_inputs * dt_wide[:, at] + g * skip_ref[:, at]) * slope_ref[:, at]
+        next_x[CHUNK:, at] = next_x[:TAIL, at]
+        next_x[:CHUNK, at] = grad_conv
         gx_ref[:, at] = conv_bwd(
-            joined, joined_grad, grad_conv, taps_ref[:, at], aux, accx_ref, at
+            joined_x, next_x, grad_conv, taps_ref[:, at], aux, accx_ref, at
         ).astype(BF16)
-    upper = (row <= col).astype(F32)
-    strict = (row > col).astype(F32)
-    straddle = (
-        mm(upper, row_sums.T - col_sums + head_sums[:CHUNK], PRECISE)
-        + mm(strict, head_sums[CHUNK : 2 * CHUNK], PRECISE)
-        + through[0:1]
-    )
+    head_sums = mm_t(sums_ref[...], spread)
+    upper = (row <= col).astype(BF16)
+    strict = (row > col).astype(BF16)
+    straddle = mm(
+        jnp.concatenate([upper] * 3 + [strict] * 2, 1),
+        jnp.concatenate(
+            [
+                parts_of(row_sums.T - col_sums + head_sums[:CHUNK], 3),
+                parts_of(head_sums[CHUNK : 2 * CHUNK], 2),
+            ],
+            0,
+        ),
+    )
+    straddle = straddle + through[0:1]
     grad_dt = head_sums[2 * CHUNK :] + head_ref[1:2] * straddle
     grad_raw = jnp.where(lane < GROUP, grad_dt * jax.nn.sigmoid(raw), 0.0)
     gdt_ref[...] = grad_raw.astype(BF16)
@@ -413,10 +441,10 @@
     grad_b = grad_b + mm(grad_meet_low, c_low)
     grad_c = grad_c + t_mm(grad_meet_low, b_low)
     grad_bc = jnp.concatenate([grad_b, grad_c], 1) * (bc_sig * (1.0 + bc_pre * (1.0 - bc_sig)))
-    joined_grad = jnp.concatenate([grad_bc, next_bc[...]], 0)
-    next_bc[...] = grad_bc[:TAIL]
+    next_bc[CHUNK:] = next_bc[:TAIL]
+    next_bc[:CHUNK] = grad_bc
     gbc_ref[...] = conv_bwd(
-        joined_bc, joined_grad, grad_bc, bc_taps_ref[...], aux, accbc_ref, slice(None)
+        joined_bc, next_bc, grad_bc, bc_taps_ref[...], aux, accbc_ref, slice(None)
     ).astype(BF16)
 
 
@@ -459,8 +487,16 @@
             ],
             scratch_shapes=[
                 pltpu.VMEM((STATE, width), F32),
-                pltpu.VMEM((TAIL, width), F32),
-                pltpu.VMEM((TAIL, 2 * STATE), F32),
+                pltpu.VMEM((TAIL + CHUNK, width), F32),
+                pltpu.VMEM((TAIL + CHUNK, 2 * STATE), F32),
+                pltpu.VMEM((TAIL + CHUNK, width), F32),
+                pltpu.VMEM((TAIL + CHUNK, 2 * STATE), F32),
+                pltpu.VMEM((CHUNK, width), F32),
+                pltpu.VMEM((CHUNK, width), F32),
+                pltpu.VMEM((CHUNK, width), BF16),
+                pltpu.VMEM((CHUNK, width), BF16),
+                pltpu.VMEM((CHUNK, width), BF16),
+                pltpu.VMEM((3 * CHUNK, width), BF16),
             ],
         ),
         out_shape=[
@@ -704,15 +740,15 @@
     small = Rows(w_small)
     near_mask, side_mask = masks[-2:]
     x0_far = x0.begin(masks)
+    small_far = small.begin(masks)
     out1_side = out1.stage(side_mask)
-    x0_near = x0.stage(near_mask)
-    small_far = small.begin(masks, x0_far)
-    z0_far = z0.begin(masks, x0_near, small_far)
-    small_near = small.stage(near_mask, x0_near)
+    x0_near = x0.stage(near_mask, small_far)
+    small_near = small.stage(near_mask, x0_far)
+    z0_far = z0.begin(masks, x0_far, small_far)
+    small.stage(side_mask)
     x0.stage(side_mask)
-    out0_far = out0.begin(masks, small_near, z0_far)
-    z0_near = z0.stage(near_mask, small_near)
-    small.stage(side_mask)
+    out0_far = out0.begin(masks, x0_near, small_near, z0_far)
+    z0_near = z0.stage(near_mask, x0_near, small_near)
     x1_far = x1.begin(masks, z0_near, out0_far)
     out0_near = out0.stage(near_mask, z0_near)
     z0.stage(side_mask)
@@ -771,9 +807,9 @@
     ]
     order, side, weights = lax.optimization_barrier((order, side, weights))
     hidden_rows = reordered(after(hidden, x0_far), me)
-    hidden_low = dot(after(hidden_rows, x0_near, small_far, out1_side), order).astype(BF16)
+    hidden_low = dot(after(hidden_rows, x0_near, small_near, out1_side), order).astype(BF16)
     cotangent_rows = reordered(after(cotangent, x0_far), me)
-    cotangent_low = dot(after(cotangent_rows, small_near, z0_far), order).astype(BF16)
+    cotangent_low = dot(after(cotangent_rows, hidden_low, z0_near), order).astype(BF16)
     gains = mm(after(norm_gain, small_near), order.astype(F32), PRECISE)
     hidden_low, cotangent_low, gains = lax.optimization_barrier(
         (hidden_low, cotangent_low, gains)
@@ -939,9 +975,7 @@
     x_far = swap(x_next, "dp", masks[-3])
     out_kept0, out_next0 = scatter_first(out_kept0, out_near0)
     out_far0 = swap(out_next0, "dp", masks[-3])
-    got, mine, x_got0, z_near0, out_next0 = lax.optimization_barrier(
-        (got, mine, x_got0, z_near0, out_next0)
-    )
+    got, mine, out_next0 = lax.optimization_barrier((got, mine, out_next0))
     total = mine[:quarter] + got.astype(F32)
     rms = rms_of(stream0)
     normal = stream0 * rms
@@ -950,14 +984,20 @@
         grown - normal * jnp.mean(grown * normal, -1, keepdims=True)
     )
     d_hidden = dot_t(grad_stream.astype(BF16), order).astype(BF16)
+    x_got0, z_near0, _ = lax.optimization_barrier((x_got0, z_near0, d_hidden))
     x_kept0, x_next0 = scatter_first(x_kept_half0, x_got0)
     x_near0 = swap(x_next0, "dp", near_mask)
+    x_next0_first = x_next0
     z_kept0, z_next0 = scatter_first(z_kept0, z_near0)
     z_far0 = swap(z_next0, "dp", masks[-3])
-    total_now = after(total, d_hidden)
+    total_now = after(total, d_hidden, z_next0)
     d_norm0 = jnp.sum(total_now * normal, 0)
     d_hidden = jnp.concatenate([d_hidden, swap(d_hidden, "tensor", 2)], 0)
+    d_half = d_hidden
     d_hidden = jnp.concatenate([d_hidden, swap(d_hidden, "tensor", 1)], 0)
+    out_kept, x_kept, z_kept, out_kept0, z_kept0, _ = lax.optimization_barrier(
+        (out_kept, x_kept, z_kept, out_kept0, z_kept0, d_half)
+    )
     d_hidden = restored(d_hidden, me).astype(F32)
 
     def finished(kept, sent):
@@ -975,6 +1015,7 @@
     d_x0 = finished(x_kept0, swap(x_next0, "dp", masks[-3]))
 
     near_cols = jnp.concatenate([columns_of(v, far) for v in (g_bc0, g_bc1)], 1)
+    near_cols = after(near_cols, x_next0_first)
     away_cols = jnp.concatenate([away0, away1], 1)
     bc_sum = near_cols.astype(F32) + turned_over(away_cols, quarter).astype(F32)
     across_sum = swap(bc_sum.astype(BF16), "tensor", 1)

time: 622 us -> 604 us (0.971)
  matrix products: 144 us -> 132 us
  local copies, waits for them, and re-layouts: 37.5 us -> 48.2 us
  other arithmetic: 73.7 us -> 63.2 us
    dot_general x18, matrix products: 58.3 us -> 50.3 us  [dot_t(): lax.dot_general(lhs, rhs, (((1,), (1,)), ((), ())), preferred_element_typ...]
    unnamed x365 -> x335, local copies, waits for them, and re-layouts: 15.8 us -> 20.6 us
  transfers between devices with their start and end apart: 73 -> 73, of which waited for: 31 -> 34; matrix products, arithmetic and copies ran while one was open for 33% -> 30% of each run, Pallas kernels for 12% -> 11%
where the time goes in v4:
time: 604 us; the launch traced here: 595 us
  waiting for transfers between devices  172 us (28%)
  matrix products  132 us (22%)
  Pallas kernels  84.2 us (14%)
  starting transfers between devices  78.2 us (13%)
  other arithmetic  63.2 us (10%)
  local copies, waits for them, and re-layouts  48.2 us (8%)
  between operations  17.5 us (3%)
    ppermute x72, waiting for transfers between devices, swap(): return lax.ppermute(values, axis, partners(lax.axis_size(axis), step))  172 us
    ppermute x72, starting transfers between devices, swap(): return lax.ppermute(values, axis, partners(lax.axis_size(axis), step))  78.2 us
    dot_general x18, matrix products, dot_t(): lax.dot_general(lhs, rhs, (((1,), (1,)), ((), ())), preferred_element_typ...  50.3 us
    pallas_call x2, Pallas kernels, scan_bwd(): pl.pallas_call(scan_bwd_kernel, grid_spec=pltpu.PrefetchScalarGridSpec(nu...  49.8 us
    dot_general x10, matrix products, dot(): lax.dot_general(lhs, rhs, (((1,), (0,)), ((), ())), preferred_element_typ...  49.7 us
    dot_general x16, matrix products, grad_half(): return lax.dot_general(taken, grads, dims, preferred_element_type=F32)  30.2 us
    pallas_call x2, Pallas kernels, scan_fwd(): pl.pallas_call(scan_fwd_kernel, grid_spec=pltpu.PrefetchScalarGridSpec(nu...  24.8 us
    unnamed x335, local copies, waits for them, and re-layouts  20.6 us
  transfers between devices with their start and end apart: 73, of which 34 were waited for; matrix products, arithmetic and copies ran while one was open for 30% of the time, Pallas kernels for 11%

profile of v4, /device:TPU:0, one launch (start us, length us, event | category | flops | bytes accessed | tf_op | source)
XLA Modules:
  0.0 595.1 jit_solution(17205882406850394302)
XLA Ops:
  20.9 6.1 %collective-permute-done.1 = bf16[192,256]{0,1:T(8,128)(2,1)S(1)} collective-permute-done((bf16[192,256]{0,1:T(8,128)(2,1)S(1)}, bf16[192,256]{0,1:T(8,128)(2,1)S(1)}, u32[]{:S(2)}, u32[]{:S(2)}) %collective-permute-start.1) | collective-permute-done | bytes 98336 | tf_op jit(solution)/shard_map/ppermute | solution.py:572
  27.8 4.7 collective-permute-done
  53.5 5.0 collective-permute-done.2
  63.4 6.4 %convolution_convert_fusion.1 = bf16[1024,1536]{1,0:T(8,128)(2,1)} fusion(bf16[1024,1536]{1,0:T(8,128)(2,1)S(1)} %pad_maximum_fusion, bf16[1536,1536]{1,0:T(8,128)(2,1)S(1)} %fusion), kind=kOutput, calls=%fused_computation.10 | convolution fusion | flops 4833411072 | bytes 11010048 | tf_op jit(solution)/shard_map/dot_general | solution.py:676
  84.5 8.6 %convolution_convert_fusion = bf16[1024,1536]{1,0:T(8,128)(2,1)} fusion(bf16[1024,1536]{1,0:T(8,128)(2,1)} %pad_maximum_fusion.1, bf16[1536,1536]{1,0:T(8,128)(2,1)S(1)} %copy-done.37), kind=kOutput, calls=%fused_computation.9 | convolution fusion | flops 4833411072 | bytes 11010048 | tf_op jit(solution)/shard_map/dot_general | solution.py:676
  99.3 4.8 collective-permute-done.9
  108.9 5.7 fusion.154.x_ref.x_tail_ref
  120.3 7.8 %collective-permute-done.19 = bf16[768,768]{1,0:T(8,128)(2,1)S(1)} collective-permute-done((bf16[768,768]{1,0:T(8,128)(2,1)S(1)}, bf16[768,768]{1,0:T(8,128)(2,1)S(1)}, u32[]{:S(2)}, u32[]{:S(2)}) %collective-permute-start.19) | collective-permute-done | bytes 1179680 | tf_op jit(solution)/shard_map/ppermute | solution.py:572
  128.1 5.3 convolution_convert_fusion.7.gate_ref
  133.5 12.6 %scan_fwd.2 = (bf16[1024,768]{1,0:T(8,128)(2,1)S(1)}, bf16[1024,768]{1,0:T(8,128)(2,1)S(1)}, f32[8,1024]{1,0:T(8,128)S(1)}, bf16[8,128,768]{2,1,0:T(8,128)(2,1)S(1)}) custom-call(s32[1]{0:T(128)} %bitcast.me_ref, f32[1024,768]{1,0:T(8,128)} %fusion.154.x_ref.x_tail_ref, f32[1024,384]{1,0:T(8,128)} %fusion.170.bcdt_ref.bc_tail_ref, ...), custom_call_target="tpu_custom_call" | custom-call | flops 14092861440 | bytes 15728640 | tf_op jit(solution)/shard_map/scan_fwd/pallas_call | solution.py:194
  146.1 4.8 collective-permute-done.22
  169.5 19.2 %collective-permute-done.12 = bf16[384,768]{1,0:T(8,128)(2,1)S(1)} collective-permute-done((bf16[384,768]{1,0:T(8,128)(2,1)S(1)}, bf16[384,768]{1,0:T(8,128)(2,1)S(1)}, u32[]{:S(2)}, u32[]{:S(2)}) %collective-permute-start.12) | collective-permute-done | bytes 589856 | tf_op jit(solution)/shard_map/ppermute | solution.py:572
  194.1 18.3 %collective-permute-done.26 = bf16[256,1536]{1,0:T(8,128)(2,1)S(1)} collective-permute-done((bf16[256,1536]{1,0:T(8,128)(2,1)S(1)}, bf16[256,1536]{1,0:T(8,128)(2,1)S(1)}, u32[]{:S(2)}, u32[]{:S(2)}) %collective-permute-start.26) | collective-permute-done | bytes 786464 | tf_op jit(solution)/shard_map/ppermute | solution.py:572
  212.5 4.4 collective-permute-done.27
  227.2 4.3 fusion.152.x_ref.x_tail_ref
  231.5 12.3 %scan_fwd.3 = (bf16[1024,768]{1,0:T(8,128)(2,1)S(1)}, bf16[1024,768]{1,0:T(8,128)(2,1)S(1)}, f32[8,1024]{1,0:T(8,128)S(1)}, bf16[8,128,768]{2,1,0:T(8,128)(2,1)S(1)}) custom-call(s32[1]{0:T(128)} %bitcast.me_ref, f32[1024,768]{1,0:T(8,128)} %fusion.152.x_ref.x_tail_ref, f32[1024,384]{1,0:T(8,128)} %fusion.171.bcdt_ref.bc_tail_ref, ...), custom_call_target="tpu_custom_call" | custom-call | flops 14092861440 | bytes 15728640 | tf_op jit(solution)/shard_map/scan_fwd/pallas_call | solution.py:194
  247.4 4.4 fusion.10
  261.9 4.8 gate_bwd.2
  270.3 24.8 %scan_bwd.2 = (bf16[1024,768]{1,0:T(8,128)(2,1)S(1)}, bf16[1024,256]{1,0:T(8,128)(2,1)S(1)}, bf16[1024,128]{1,0:T(8,128)(2,1)S(1)}, f32[8,768]{1,0:T(8,128)S(1)}, f32[8,256]{1,0:T(8,128)S(1)}) custom-call(s32[1]{0:T(128)} %bitcast.me_ref, bf16[1024,768]{1,0:T(8,128)(2,1)S(1)} %get-tuple-element.205.g_ref, f32[1024,768]{1,0:T(8,128)} %fusion.152.x_ref.x_tail_ref, ...), custom_call_target="tpu_custom_call" | custom-call | flops 28185722880 | bytes 15728640 | tf_op jit(solution)/shard_map/scan_bwd/pallas_call | solution.py:475
  303.4 5.0 fusion.13
  317.1 5.5 fusion.6
  339.8 5.7 collective-permute-done.35
  353.9 12.6 %collective-permute-done.39 = f32[256]{0:T(256)S(1)} collective-permute-done((f32[256]{0:T(256)S(1)}, f32[256]{0:T(256)S(1)}, u32[]{:S(2)}, u32[]{:S(2)}) %collective-permute-start.39) | collective-permute-done | bytes 1056 | tf_op jit(solution)/shard_map/ppermute | solution.py:572
  386.3 5.4 fusion.153.gs_ref
  391.6 4.8 gate_bwd.3
  404.8 25.0 %scan_bwd.3 = (bf16[1024,768]{1,0:T(8,128)(2,1)S(1)}, bf16[1024,256]{1,0:T(8,128)(2,1)S(1)}, bf16[1024,128]{1,0:T(8,128)(2,1)S(1)}, f32[8,768]{1,0:T(8,128)S(1)}, f32[8,256]{1,0:T(8,128)S(1)}) custom-call(s32[1]{0:T(128)} %bitcast.me_ref, bf16[1024,768]{1,0:T(8,128)(2,1)S(1)} %get-tuple-element.236.g_ref, f32[1024,768]{1,0:T(8,128)} %fusion.154.x_ref.x_tail_ref, ...), custom_call_target="tpu_custom_call" | custom-call | flops 28185722880 | bytes 15728640 | tf_op jit(solution)/shard_map/scan_bwd/pallas_call | solution.py:475
  449.3 4.1 fusion.80
  458.6 10.4 %collective-permute-done.51 = bf16[768,768]{1,0:T(8,128)(2,1)} collective-permute-done((bf16[768,768]{1,0:T(8,128)(2,1)S(1)}, bf16[768,768]{1,0:T(8,128)(2,1)}, u32[]{:S(2)}, u32[]{:S(2)}) %collective-permute-start.51) | collective-permute-done | bytes 1179680 | tf_op jit(solution)/shard_map/ppermute | solution.py:572
  486.0 7.8 %collective-permute-done.56 = bf16[768,768]{1,0:T(8,128)(2,1)S(1)} collective-permute-done((bf16[768,768]{1,0:T(8,128)(2,1)S(1)}, bf16[768,768]{1,0:T(8,128)(2,1)S(1)}, u32[]{:S(2)}, u32[]{:S(2)}) %collective-permute-start.56) | collective-permute-done | bytes 1179680 | tf_op jit(solution)/shard_map/ppermute | solution.py:572
  520.8 9.0 %collective-permute-done.62 = f32[30,768]{1,0:T(8,128)S(1)} collective-permute-done((f32[30,768]{1,0:T(8,128)S(1)}, f32[30,768]{1,0:T(8,128)S(1)}, u32[]{:S(2)}, u32[]{:S(2)}) %collective-permute-start.62) | collective-permute-done | bytes 92192 | tf_op jit(solution)/shard_map/ppermute | solution.py:572
  554.6 4.7 collective-permute-done.63
  571.8 7.0 %collective-permute-done.70 = bf16[192,256]{0,1:T(8,128)(2,1)S(1)} collective-permute-done((bf16[192,256]{0,1:T(8,128)(2,1)S(1)}, bf16[192,256]{0,1:T(8,128)(2,1)S(1)}, u32[]{:S(2)}, u32[]{:S(2)}) %collective-permute-start.70) | collective-permute-done | bytes 98336 | tf_op jit(solution)/shard_map/ppermute | solution.py:572
  (730 shorter events, 306.5 us)
Async XLA Ops:
  7.3 564.5 %all-gather.3.cloned.1.call-start = ((), (), s32[]{:S(2)}) async-start(), calls=%async_computation | async-start | bytes 3932160 | tf_op jit(solution)/shard_map/all_gather | solution.py:947
  17.3 46.1 %collective-permute-start.4 = (bf16[192,768]{1,0:T(8,128)(2,1)S(1)}, bf16[192,768]{1,0:T(8,128)(2,1)S(1)}, u32[]{:S(2)}, u32[]{:S(2)}) collective-permute-start(bf16[192,768]{1,0:T(8,128)(2,1)S(1)} %get-tuple-element.392), channel_id=1, source_target_pairs={{0,1},{1,0},{2,3},{3,2},{4,5},{5,4},{6,7},{7,6},{8,9},{9,8},{10,11... | collective-permute-start | bytes 884744 | tf_op jit(solution)/shard_map/ppermute | solution.py:572
  58.5 22.5 %collective-permute-start.6 = (bf16[384,768]{1,0:T(8,128)(2,1)}, bf16[384,768]{1,0:T(8,128)(2,1)}, u32[]{:S(2)}, u32[]{:S(2)}) collective-permute-start(bf16[384,768]{1,0:T(8,128)(2,1)} %pad_maximum_fusion.23), channel_id=1, source_target_pairs={{0,2},{1,3},{2,0},{3,1},{4,6},{5,7},{6,4},{7,5},{8,10},{9,11},{10,... | collective-permute-start | bytes 1769480 | tf_op jit(solution)/shard_map/ppermute | solution.py:572
  74.0 34.8 %collective-permute-start.15 = (bf16[768,768]{1,0:T(8,128)(2,1)S(1)}, bf16[768,768]{1,0:T(8,128)(2,1)S(1)}, u32[]{:S(2)}, u32[]{:S(2)}) collective-permute-start(bf16[768,768]{1,0:T(8,128)(2,1)S(1)} %pad_maximum_fusion.13), channel_id=1, source_target_pairs={{0,1},{1,0},{2,3},{3,2},{4,5},{5,4},{6,7},{7,6},{8,9},{9,8},{10,11... | collective-permute-start | bytes 3538952 | tf_op jit(solution)/shard_map/ppermute | solution.py:572
  95.1 33.0 %collective-permute-start.19 = (bf16[768,768]{1,0:T(8,128)(2,1)S(1)}, bf16[768,768]{1,0:T(8,128)(2,1)S(1)}, u32[]{:S(2)}, u32[]{:S(2)}) collective-permute-start(bf16[768,768]{1,0:T(8,128)(2,1)S(1)} %pad_maximum_fusion.14), channel_id=1, source_target_pairs={{0,1},{1,0},{2,3},{3,2},{4,5},{5,4},{6,7},{7,6},{8,9},{9,8},{10,11... | collective-permute-start | bytes 3538952 | tf_op jit(solution)/shard_map/ppermute | solution.py:572
  104.0 42.1 %collective-permute-start.10 = (bf16[384,768]{1,0:T(8,128)(2,1)S(1)}, bf16[384,768]{1,0:T(8,128)(2,1)S(1)}, u32[]{:S(2)}, u32[]{:S(2)}) collective-permute-start(bf16[384,768]{1,0:T(8,128)(2,1)S(1)} %pad_maximum_fusion.25), channel_id=1, source_target_pairs={{0,2},{1,3},{2,0},{3,1},{4,6},{5,7},{6,4},{7,5},{8,10},{9,11},{10,... | collective-permute-start | bytes 1769480 | tf_op jit(solution)/shard_map/ppermute | solution.py:572
  105.4 40.7 %collective-permute-start.11 = (bf16[192,768]{1,0:T(8,128)(2,1)S(1)}, bf16[192,768]{1,0:T(8,128)(2,1)S(1)}, u32[]{:S(2)}, u32[]{:S(2)}) collective-permute-start(bf16[192,768]{1,0:T(8,128)(2,1)S(1)} %copy-done.77), channel_id=1, source_target_pairs={{0,4},{1,5},{2,6},{3,7},{4,0},{5,1},{6,2},{7,3},{8,12},{9,13},{10,... | collective-permute-start | bytes 884744 | tf_op jit(solution)/shard_map/ppermute | solution.py:572
  118.8 32.2 %collective-permute-start.22 = (bf16[768,768]{1,0:T(8,128)(2,1)S(1)}, bf16[768,768]{1,0:T(8,128)(2,1)S(1)}, u32[]{:S(2)}, u32[]{:S(2)}) collective-permute-start(bf16[768,768]{1,0:T(8,128)(2,1)S(1)} %pad_maximum_fusion.15), channel_id=1, source_target_pairs={{0,1},{1,0},{2,3},{3,2},{4,5},{5,4},{6,7},{7,6},{8,9},{9,8},{10,11... | collective-permute-start | bytes 3538952 | tf_op jit(solution)/shard_map/ppermute | solution.py:572
  159.7 29.0 %collective-permute-start.12 = (bf16[384,768]{1,0:T(8,128)(2,1)S(1)}, bf16[384,768]{1,0:T(8,128)(2,1)S(1)}, u32[]{:S(2)}, u32[]{:S(2)}) collective-permute-start(bf16[384,768]{1,0:T(8,128)(2,1)S(1)} %pad_maximum_fusion.24), channel_id=1, source_target_pairs={{0,4},{1,5},{2,6},{3,7},{4,0},{5,1},{6,2},{7,3},{8,12},{9,13},{10,... | collective-permute-start | bytes 1769480 | tf_op jit(solution)/shard_map/ppermute | solution.py:572
  160.1 28.7 %collective-permute-start.13 = (bf16[384,768]{1,0:T(8,128)(2,1)S(1)}, bf16[384,768]{1,0:T(8,128)(2,1)S(1)}, u32[]{:S(2)}, u32[]{:S(2)}) collective-permute-start(bf16[384,768]{1,0:T(8,128)(2,1)S(1)} %pad_maximum_fusion.27), channel_id=1, source_target_pairs={{0,2},{1,3},{2,0},{3,1},{4,6},{5,7},{6,4},{7,5},{8,10},{9,11},{10,... | collective-permute-start | bytes 1769480 | tf_op jit(solution)/shard_map/ppermute | solution.py:572
  161.8 28.7 %collective-permute-start.25 = (bf16[768,768]{1,0:T(8,128)(2,1)S(1)}, bf16[768,768]{1,0:T(8,128)(2,1)S(1)}, u32[]{:S(2)}, u32[]{:S(2)}) collective-permute-start(bf16[768,768]{1,0:T(8,128)(2,1)S(1)} %pad_maximum_fusion.16), channel_id=1, source_target_pairs={{0,1},{1,0},{2,3},{3,2},{4,5},{5,4},{6,7},{7,6},{8,9},{9,8},{10,11... | collective-permute-start | bytes 3538952 | tf_op jit(solution)/shard_map/ppermute | solution.py:572
  167.8 22.8 %collective-permute-start.24 = (bf16[256,1536]{1,0:T(8,128)(2,1)S(1)}, bf16[256,1536]{1,0:T(8,128)(2,1)S(1)}, u32[]{:S(2)}, u32[]{:S(2)}) collective-permute-start(bf16[256,1536]{1,0:T(8,128)(2,1)S(1)} %slice.1003), channel_id=1, source_target_pairs={{0,16},{8,24},{16,0},{24,8},{1,17},{9,25},{17,1},{25,9},{2,18},{10... | collective-permute-start | bytes 2359304 | tf_op jit(solution)/shard_map/ppermute | solution.py:572
  188.8 28.1 %collective-permute-start.14 = (bf16[768,768]{1,0:T(8,128)(2,1)S(1)}, bf16[768,768]{1,0:T(8,128)(2,1)S(1)}, u32[]{:S(2)}, u32[]{:S(2)}) collective-permute-start(bf16[768,768]{1,0:T(8,128)(2,1)S(1)} %pad_maximum_fusion.12), channel_id=1, source_target_pairs={{0,2},{1,3},{2,0},{3,1},{4,6},{5,7},{6,4},{7,5},{8,10},{9,11},{10,... | collective-permute-start | bytes 3538952 | tf_op jit(solution)/shard_map/ppermute | solution.py:572
  189.0 27.9 %collective-permute-start.27 = (bf16[768,768]{1,0:T(8,128)(2,1)S(1)}, bf16[768,768]{1,0:T(8,128)(2,1)S(1)}, u32[]{:S(2)}, u32[]{:S(2)}) collective-permute-start(bf16[768,768]{1,0:T(8,128)(2,1)S(1)} %pad_maximum_fusion.17), channel_id=1, source_target_pairs={{0,1},{1,0},{2,3},{3,2},{4,5},{5,4},{6,7},{7,6},{8,9},{9,8},{10,11... | collective-permute-start | bytes 3538952 | tf_op jit(solution)/shard_map/ppermute | solution.py:572
  268.2 32.5 %collective-permute-start.32 = (bf16[768,768]{1,0:T(8,128)(2,1)S(1)}, bf16[768,768]{1,0:T(8,128)(2,1)S(1)}, u32[]{:S(2)}, u32[]{:S(2)}) collective-permute-start(bf16[768,768]{1,0:T(8,128)(2,1)S(1)} %convolution_convert_fusion.10), channel_id=1, source_target_pairs={{0,1},{1,0},{2,3},{3,2},{4,5},{5,4},{6,7},{7,6},{8,9},{9,8},{10,11... | collective-permute-start | bytes 3538952 | tf_op jit(solution)/shard_map/ppermute | solution.py:572
  269.8 30.9 %collective-permute-start.33 = (bf16[256,1536]{1,0:T(8,128)(2,1)S(1)}, bf16[256,1536]{1,0:T(8,128)(2,1)S(1)}, u32[]{:S(2)}, u32[]{:S(2)}) collective-permute-start(bf16[256,1536]{1,0:T(8,128)(2,1)S(1)} %copy-done.102), channel_id=1, source_target_pairs={{0,16},{8,24},{16,0},{24,8},{1,17},{9,25},{17,1},{25,9},{2,18},{10... | collective-permute-start | bytes 2359304 | tf_op jit(solution)/shard_map/ppermute | solution.py:572
  311.1 28.7 %collective-permute-start.36 = (bf16[768,768]{1,0:T(8,128)(2,1)}, bf16[768,768]{1,0:T(8,128)(2,1)}, u32[]{:S(2)}, u32[]{:S(2)}) collective-permute-start(bf16[768,768]{1,0:T(8,128)(2,1)} %fusion.53), channel_id=1, source_target_pairs={{0,1},{1,0},{2,3},{3,2},{4,5},{5,4},{6,7},{7,6},{8,9},{9,8},{10,11... | collective-permute-start | bytes 3538952 | tf_op jit(solution)/shard_map/ppermute | solution.py:572
  373.1 29.1 %collective-permute-start.44 = (bf16[768,768]{1,0:T(8,128)(2,1)}, bf16[768,768]{1,0:T(8,128)(2,1)}, u32[]{:S(2)}, u32[]{:S(2)}) collective-permute-start(bf16[768,768]{1,0:T(8,128)(2,1)} %fusion.56), channel_id=1, source_target_pairs={{0,1},{1,0},{2,3},{3,2},{4,5},{5,4},{6,7},{7,6},{8,9},{9,8},{10,11... | collective-permute-start | bytes 3538952 | tf_op jit(solution)/shard_map/ppermute | solution.py:572
  385.2 46.9 %collective-permute-start.48 = (bf16[768,768]{1,0:T(8,128)(2,1)}, bf16[768,768]{1,0:T(8,128)(2,1)}, u32[]{:S(2)}, u32[]{:S(2)}) collective-permute-start(bf16[768,768]{1,0:T(8,128)(2,1)} %fusion.59), channel_id=1, source_target_pairs={{0,1},{1,0},{2,3},{3,2},{4,5},{5,4},{6,7},{7,6},{8,9},{9,8},{10,11... | collective-permute-start | bytes 3538952 | tf_op jit(solution)/shard_map/ppermute | solution.py:572
  385.8 46.3 %collective-permute-start.46 = (bf16[1024,128]{1,0:T(8,128)(2,1)}, bf16[1024,128]{1,0:T(8,128)(2,1)S(1)}, u32[]{:S(2)}, u32[]{:S(2)}) collective-permute-start(bf16[1024,128]{1,0:T(8,128)(2,1)} %get-tuple-element.239), channel_id=1, source_target_pairs={{0,16},{8,24},{16,0},{24,8},{1,17},{9,25},{17,1},{25,9},{2,18},{10... | collective-permute-start | bytes 786440 | tf_op jit(solution)/shard_map/ppermute | solution.py:572
  404.7 27.4 %collective-permute-start.47 = (bf16[384,768]{1,0:T(8,128)(2,1)}, bf16[384,768]{1,0:T(8,128)(2,1)}, u32[]{:S(2)}, u32[]{:S(2)}) collective-permute-start(bf16[384,768]{1,0:T(8,128)(2,1)} %slice.1007), channel_id=1, source_target_pairs={{0,2},{1,3},{2,0},{3,1},{4,6},{5,7},{6,4},{7,5},{8,10},{9,11},{10,... | collective-permute-start | bytes 1769480 | tf_op jit(solution)/shard_map/ppermute | solution.py:572
  440.1 28.9 %collective-permute-start.51 = (bf16[768,768]{1,0:T(8,128)(2,1)S(1)}, bf16[768,768]{1,0:T(8,128)(2,1)}, u32[]{:S(2)}, u32[]{:S(2)}) collective-permute-start(bf16[768,768]{1,0:T(8,128)(2,1)S(1)} %copy-done.151), channel_id=1, source_target_pairs={{0,1},{1,0},{2,3},{3,2},{4,5},{5,4},{6,7},{7,6},{8,9},{9,8},{10,11... | collective-permute-start | bytes 3538952 | tf_op jit(solution)/shard_map/ppermute | solution.py:572
  446.7 32.3 %collective-permute-start.53 = (bf16[384,768]{1,0:T(8,128)(2,1)S(1)}, bf16[384,768]{1,0:T(8,128)(2,1)S(1)}, u32[]{:S(2)}, u32[]{:S(2)}) collective-permute-start(bf16[384,768]{1,0:T(8,128)(2,1)S(1)} %slice.1006), channel_id=1, source_target_pairs={{0,2},{1,3},{2,0},{3,1},{4,6},{5,7},{6,4},{7,5},{8,10},{9,11},{10,... | collective-permute-start | bytes 1769480 | tf_op jit(solution)/shard_map/ppermute | solution.py:572
  448.8 44.9 %collective-permute-start.56 = (bf16[768,768]{1,0:T(8,128)(2,1)S(1)}, bf16[768,768]{1,0:T(8,128)(2,1)S(1)}, u32[]{:S(2)}, u32[]{:S(2)}) collective-permute-start(bf16[768,768]{1,0:T(8,128)(2,1)S(1)} %convolution_convert_fusion.8), channel_id=1, source_target_pairs={{0,1},{1,0},{2,3},{3,2},{4,5},{5,4},{6,7},{7,6},{8,9},{9,8},{10,11... | collective-permute-start | bytes 3538952 | tf_op jit(solution)/shard_map/ppermute | solution.py:572
  457.4 22.5 %collective-permute-start.50 = (bf16[256,1536]{1,0:T(8,128)(2,1)S(1)}, bf16[256,1536]{1,0:T(8,128)(2,1)S(1)}, u32[]{:S(2)}, u32[]{:S(2)}) collective-permute-start(bf16[256,1536]{1,0:T(8,128)(2,1)S(1)} %slice.1000), channel_id=1, source_target_pairs={{0,16},{8,24},{16,0},{24,8},{1,17},{9,25},{17,1},{25,9},{2,18},{10... | collective-permute-start | bytes 2359304 | tf_op jit(solution)/shard_map/ppermute | solution.py:572
  471.9 21.9 %collective-permute-start.57 = (bf16[384,768]{1,0:T(8,128)(2,1)S(1)}, bf16[384,768]{1,0:T(8,128)(2,1)S(1)}, u32[]{:S(2)}, u32[]{:S(2)}) collective-permute-start(bf16[384,768]{1,0:T(8,128)(2,1)S(1)} %slice.1005), channel_id=1, source_target_pairs={{0,2},{1,3},{2,0},{3,1},{4,6},{5,7},{6,4},{7,5},{8,10},{9,11},{10,... | collective-permute-start | bytes 1769480 | tf_op jit(solution)/shard_map/ppermute | solution.py:572
  498.6 52.6 %collective-permute-start.71 = (bf16[192,768]{1,0:T(8,128)(2,1)}, bf16[192,768]{1,0:T(8,128)(2,1)}, u32[]{:S(2)}, u32[]{:S(2)}) collective-permute-start(bf16[192,768]{1,0:T(8,128)(2,1)} %slice.1012), channel_id=1, source_target_pairs={{0,4},{1,5},{2,6},{3,7},{4,0},{5,1},{6,2},{7,3},{8,12},{9,13},{10,... | collective-permute-start | bytes 884744 | tf_op jit(solution)/shard_map/ppermute | solution.py:572
  504.4 49.2 %collective-permute-start.66 = (bf16[192,768]{1,0:T(8,128)(2,1)}, bf16[192,768]{1,0:T(8,128)(2,1)}, u32[]{:S(2)}, u32[]{:S(2)}) collective-permute-start(bf16[192,768]{1,0:T(8,128)(2,1)} %slice.1013), channel_id=1, source_target_pairs={{0,4},{1,5},{2,6},{3,7},{4,0},{5,1},{6,2},{7,3},{8,12},{9,13},{10,... | collective-permute-start | bytes 884744 | tf_op jit(solution)/shard_map/ppermute | solution.py:572
  505.8 42.6 %collective-permute-start.54 = (bf16[256,1536]{1,0:T(8,128)(2,1)}, bf16[256,1536]{1,0:T(8,128)(2,1)}, u32[]{:S(2)}, u32[]{:S(2)}) collective-permute-start(bf16[256,1536]{1,0:T(8,128)(2,1)} %convolution_convert_fusion.4), channel_id=1, source_target_pairs={{0,16},{8,24},{16,0},{24,8},{1,17},{9,25},{17,1},{25,9},{2,18},{10... | collective-permute-start | bytes 2359304 | tf_op jit(solution)/shard_map/ppermute | solution.py:572
  511.8 33.8 %collective-permute-start.64 = (bf16[384,768]{1,0:T(8,128)(2,1)}, bf16[384,768]{1,0:T(8,128)(2,1)}, u32[]{:S(2)}, u32[]{:S(2)}) collective-permute-start(bf16[384,768]{1,0:T(8,128)(2,1)} %slice.1004), channel_id=1, source_target_pairs={{0,2},{1,3},{2,0},{3,1},{4,6},{5,7},{6,4},{7,5},{8,10},{9,11},{10,... | collective-permute-start | bytes 1769480 | tf_op jit(solution)/shard_map/ppermute | solution.py:572
  535.3 23.9 %collective-permute-start.63 = (bf16[192,768]{1,0:T(8,128)(2,1)}, bf16[192,768]{1,0:T(8,128)(2,1)}, u32[]{:S(2)}, u32[]{:S(2)}) collective-permute-start(bf16[192,768]{1,0:T(8,128)(2,1)} %slice.1011), channel_id=1, source_target_pairs={{0,4},{1,5},{2,6},{3,7},{4,0},{5,1},{6,2},{7,3},{8,12},{9,13},{10,... | collective-permute-start | bytes 884744 | tf_op jit(solution)/shard_map/ppermute | solution.py:572
  551.2 29.0 %collective-permute-start.55 = (bf16[512,1536]{1,0:T(8,128)(2,1)S(1)}, bf16[512,1536]{1,0:T(8,128)(2,1)}, u32[]{:S(2)}, u32[]{:S(2)}) collective-permute-start(bf16[512,1536]{1,0:T(8,128)(2,1)S(1)} %pad_maximum_fusion.11), channel_id=1, source_target_pairs={{0,8},{8,0},{16,24},{24,16},{1,9},{9,1},{17,25},{25,17},{2,10},{10... | collective-permute-start | bytes 4718600 | tf_op jit(solution)/shard_map/ppermute | solution.py:572
  (205 other events, 2721.2 us)
Sparse Core Ops, SparseCore 0:
  496.5 44.0 all-gather.2

commit v5 on v4

--- a/solution.py
+++ b/solution.py
@@ -990,10 +990,9 @@
     x_next0_first = x_next0
     z_kept0, z_next0 = scatter_first(z_kept0, z_near0)
     z_far0 = swap(z_next0, "dp", masks[-3])
-    total_now = after(total, d_hidden, z_next0)
-    d_norm0 = jnp.sum(total_now * normal, 0)
     d_hidden = jnp.concatenate([d_hidden, swap(d_hidden, "tensor", 2)], 0)
     d_half = d_hidden
+    d_norm0 = jnp.sum(after(total, d_half) * normal, 0)
     d_hidden = jnp.concatenate([d_hidden, swap(d_hidden, "tensor", 1)], 0)
     out_kept, x_kept, z_kept, out_kept0, z_kept0, _ = lax.optimization_barrier(
         (out_kept, x_kept, z_kept, out_kept0, z_kept0, d_half)

time: 604 us -> 592 us (0.980)
  waiting for transfers between devices: 172 us -> 160 us
  starting transfers between devices: 78.2 us -> 71.9 us
    ppermute x72, waiting for transfers between devices: 172 us -> 160 us  [swap(): return lax.ppermute(values, axis, partners(lax.axis_size(axis), step))]
    ppermute x72, starting transfers between devices: 78.2 us -> 71.9 us  [swap(): return lax.ppermute(values, axis, partners(lax.axis_size(axis), step))]
    unnamed x335 -> x319, local copies, waits for them, and re-layouts: 20.6 us -> 18.4 us
  transfers between devices with their start and end apart: 73 -> 73, of which waited for: 34 -> 33; matrix products, arithmetic and copies ran while one was open for 30% -> 33% of each run, Pallas kernels for 11% -> 11%
where the time goes in v5:
time: 592 us; the launch traced here: 583 us
  waiting for transfers between devices  160 us (27%)
  matrix products  138 us (23%)
  Pallas kernels  84.1 us (14%)
  starting transfers between devices  71.9 us (12%)
  other arithmetic  65.2 us (11%)
  local copies, waits for them, and re-layouts  46.8 us (8%)
  between operations  17.4 us (3%)
    ppermute x72, waiting for transfers between devices, swap(): return lax.ppermute(values, axis, partners(lax.axis_size(axis), step))  160 us
    ppermute x72, starting transfers between devices, swap(): return lax.ppermute(values, axis, partners(lax.axis_size(axis), step))  71.9 us
    dot_general x10, matrix products, dot(): lax.dot_general(lhs, rhs, (((1,), (0,)), ((), ())), preferred_element_typ...  52.8 us
    dot_general x18, matrix products, dot_t(): lax.dot_general(lhs, rhs, (((1,), (1,)), ((), ())), preferred_element_typ...  50.7 us
    pallas_call x2, Pallas kernels, scan_bwd(): pl.pallas_call(scan_bwd_kernel, grid_spec=pltpu.PrefetchScalarGridSpec(nu...  49.5 us
    dot_general x16, matrix products, grad_half(): return lax.dot_general(taken, grads, dims, preferred_element_type=F32)  32.5 us
    pallas_call x2, Pallas kernels, scan_fwd(): pl.pallas_call(scan_fwd_kernel, grid_spec=pltpu.PrefetchScalarGridSpec(nu...  25 us
    unnamed x319, local copies, waits for them, and re-layouts  18.4 us
  transfers between devices with their start and end apart: 73, of which 33 were waited for; matrix products, arithmetic and copies ran while one was open for 33% of the time, Pallas kernels for 11%

profile of v5, /device:TPU:0, one launch (start us, length us, event | category | flops | bytes accessed | tf_op | source)
XLA Modules:
  0.0 583.0 jit_solution(187339404419315207)
XLA Ops:
  9.3 4.1 collective-permute-start.1
  18.8 8.1 %collective-permute-done.1 = bf16[192,256]{0,1:T(8,128)(2,1)S(1)} collective-permute-done((bf16[192,256]{0,1:T(8,128)(2,1)S(1)}, bf16[192,256]{0,1:T(8,128)(2,1)S(1)}, u32[]{:S(2)}, u32[]{:S(2)}) %collective-permute-start.1) | collective-permute-done | bytes 98336 | tf_op jit(solution)/shard_map/ppermute | solution.py:572
  27.7 4.7 collective-permute-done
  42.6 4.0 constant_dynamic-slice_fusion.20
  63.3 6.4 %convolution_convert_fusion.1 = bf16[1024,1536]{1,0:T(8,128)(2,1)} fusion(bf16[1024,1536]{1,0:T(8,128)(2,1)S(1)} %pad_maximum_fusion, bf16[1536,1536]{1,0:T(8,128)(2,1)S(1)} %fusion), kind=kOutput, calls=%fused_computation.10 | convolution fusion | flops 4833411072 | bytes 11010048 | tf_op jit(solution)/shard_map/dot_general | solution.py:676
  84.4 8.5 %convolution_convert_fusion = bf16[1024,1536]{1,0:T(8,128)(2,1)} fusion(bf16[1024,1536]{1,0:T(8,128)(2,1)} %pad_maximum_fusion.1, bf16[1536,1536]{1,0:T(8,128)(2,1)S(1)} %copy-done.36), kind=kOutput, calls=%fused_computation.9 | convolution fusion | flops 4833411072 | bytes 11010048 | tf_op jit(solution)/shard_map/dot_general | solution.py:676
  99.6 4.3 collective-permute-done.9
  108.6 5.7 fusion.154.x_ref.x_tail_ref
  120.9 7.4 %collective-permute-done.19 = bf16[768,768]{1,0:T(8,128)(2,1)S(1)} collective-permute-done((bf16[768,768]{1,0:T(8,128)(2,1)S(1)}, bf16[768,768]{1,0:T(8,128)(2,1)S(1)}, u32[]{:S(2)}, u32[]{:S(2)}) %collective-permute-start.19) | collective-permute-done | bytes 1179680 | tf_op jit(solution)/shard_map/ppermute | solution.py:572
  128.3 5.3 convolution_convert_fusion.7.gate_ref
  133.7 12.6 %scan_fwd.2 = (bf16[1024,768]{1,0:T(8,128)(2,1)S(1)}, bf16[1024,768]{1,0:T(8,128)(2,1)S(1)}, f32[8,1024]{1,0:T(8,128)S(1)}, bf16[8,128,768]{2,1,0:T(8,128)(2,1)S(1)}) custom-call(s32[1]{0:T(128)} %bitcast.me_ref, f32[1024,768]{1,0:T(8,128)} %fusion.154.x_ref.x_tail_ref, f32[1024,384]{1,0:T(8,128)} %fusion.170.bcdt_ref.bc_tail_ref, ...), custom_call_target="tpu_custom_call" | custom-call | flops 14092861440 | bytes 15728640 | tf_op jit(solution)/shard_map/scan_fwd/pallas_call | solution.py:194
  146.4 4.7 collective-permute-done.22
  164.5 19.1 %collective-permute-done.12 = bf16[384,768]{1,0:T(8,128)(2,1)S(1)} collective-permute-done((bf16[384,768]{1,0:T(8,128)(2,1)S(1)}, bf16[384,768]{1,0:T(8,128)(2,1)S(1)}, u32[]{:S(2)}, u32[]{:S(2)}) %collective-permute-start.12) | collective-permute-done | bytes 589856 | tf_op jit(solution)/shard_map/ppermute | solution.py:572
  188.8 17.2 %collective-permute-done.26 = bf16[256,1536]{1,0:T(8,128)(2,1)S(1)} collective-permute-done((bf16[256,1536]{1,0:T(8,128)(2,1)S(1)}, bf16[256,1536]{1,0:T(8,128)(2,1)S(1)}, u32[]{:S(2)}, u32[]{:S(2)}) %collective-permute-start.26) | collective-permute-done | bytes 786464 | tf_op jit(solution)/shard_map/ppermute | solution.py:572
  206.1 5.8 collective-permute-done.27
  222.1 4.3 fusion.152.x_ref.x_tail_ref
  226.4 12.4 %scan_fwd.3 = (bf16[1024,768]{1,0:T(8,128)(2,1)S(1)}, bf16[1024,768]{1,0:T(8,128)(2,1)S(1)}, f32[8,1024]{1,0:T(8,128)S(1)}, bf16[8,128,768]{2,1,0:T(8,128)(2,1)S(1)}) custom-call(s32[1]{0:T(128)} %bitcast.me_ref, f32[1024,768]{1,0:T(8,128)} %fusion.152.x_ref.x_tail_ref, f32[1024,384]{1,0:T(8,128)} %fusion.171.bcdt_ref.bc_tail_ref, ...), custom_call_target="tpu_custom_call" | custom-call | flops 14092861440 | bytes 15728640 | tf_op jit(solution)/shard_map/scan_fwd/pallas_call | solution.py:194
  241.7 7.1 %fusion.10 = (f32[1024]{0:T(1024)S(1)}, f32[1024,768]{1,0:T(8,128)}) fusion(bf16[1024,768]{1,0:T(8,128)(2,1)S(1)} %get-tuple-element.201, bf16[1024,1536]{1,0:T(8,128)(2,1)} %convolution_convert_fusion, bf16[1536,768]{1,0:T(8,128)(2,1)} %copy-done.123), kind=kOutput, calls=%fused_computation.23 | convolution fusion | flops 2418277376 | bytes 10227712 | tf_op jit(solution)/shard_map/dot_general | solution.py:676
  260.4 4.8 gate_bwd.2
  268.9 24.6 %scan_bwd.2 = (bf16[1024,768]{1,0:T(8,128)(2,1)S(1)}, bf16[1024,256]{1,0:T(8,128)(2,1)S(1)}, bf16[1024,128]{1,0:T(8,128)(2,1)S(1)}, f32[8,768]{1,0:T(8,128)S(1)}, f32[8,256]{1,0:T(8,128)S(1)}) custom-call(s32[1]{0:T(128)} %bitcast.me_ref, bf16[1024,768]{1,0:T(8,128)(2,1)S(1)} %get-tuple-element.205.g_ref, f32[1024,768]{1,0:T(8,128)} %fusion.152.x_ref.x_tail_ref, ...), custom_call_target="tpu_custom_call" | custom-call | flops 28185722880 | bytes 15728640 | tf_op jit(solution)/shard_map/scan_bwd/pallas_call | solution.py:475
  302.2 5.0 fusion.13
  316.0 5.5 fusion.6
  334.7 3.9 collective-permute-done.36
  338.7 5.5 collective-permute-done.35
  352.1 13.0 %collective-permute-done.39 = f32[256]{0:T(256)S(1)} collective-permute-done((f32[256]{0:T(256)S(1)}, f32[256]{0:T(256)S(1)}, u32[]{:S(2)}, u32[]{:S(2)}) %collective-permute-start.39) | collective-permute-done | bytes 1056 | tf_op jit(solution)/shard_map/ppermute | solution.py:572
  383.8 5.6 fusion.153.gs_ref
  389.4 4.8 gate_bwd.3
  403.5 24.8 %scan_bwd.3 = (bf16[1024,768]{1,0:T(8,128)(2,1)S(1)}, bf16[1024,256]{1,0:T(8,128)(2,1)S(1)}, bf16[1024,128]{1,0:T(8,128)(2,1)S(1)}, f32[8,768]{1,0:T(8,128)S(1)}, f32[8,256]{1,0:T(8,128)S(1)}) custom-call(s32[1]{0:T(128)} %bitcast.me_ref, bf16[1024,768]{1,0:T(8,128)(2,1)S(1)} %get-tuple-element.236.g_ref, f32[1024,768]{1,0:T(8,128)} %fusion.154.x_ref.x_tail_ref, ...), custom_call_target="tpu_custom_call" | custom-call | flops 28185722880 | bytes 15728640 | tf_op jit(solution)/shard_map/scan_bwd/pallas_call | solution.py:475
  466.2 6.9 %collective-permute-done.50 = bf16[256,1536]{1,0:T(8,128)(2,1)} collective-permute-done((bf16[256,1536]{1,0:T(8,128)(2,1)}, bf16[256,1536]{1,0:T(8,128)(2,1)}, u32[]{:S(2)}, u32[]{:S(2)}) %collective-permute-start.50) | collective-permute-done | bytes 786464 | tf_op jit(solution)/shard_map/ppermute | solution.py:572
  475.6 6.2 %convolution_convert_fusion.4 = bf16[256,1536]{1,0:T(8,128)(2,1)} fusion(bf16[1536,1536]{1,0:T(8,128)(2,1)} %copy-done.35, f32[256,1536]{1,0:T(8,128)S(1)} %get-tuple-element.261, f32[256]{0:T(256)S(1)} %broadcast_multiply_fusion, f32[1536]{0:T(1024)S(1)} %copy-done.122, f32[256]{0:T(256)S(1)} %add_rsqrt_fusion.3, ...), kind=kOutput, calls=%fused_computation.35 | convolution fusion | flops 1214251008 | bytes 11812864 | tf_op jit(solution)/shard_map/dot_general | solution.py:680
  502.9 16.1 %collective-permute-done.64 = bf16[384,768]{1,0:T(8,128)(2,1)} collective-permute-done((bf16[384,768]{1,0:T(8,128)(2,1)}, bf16[384,768]{1,0:T(8,128)(2,1)}, u32[]{:S(2)}, u32[]{:S(2)}) %collective-permute-start.64) | collective-permute-done | bytes 589856 | tf_op jit(solution)/shard_map/ppermute | solution.py:572
  555.1 6.1 %collective-permute-done.60 = f32[30,768]{1,0:T(8,128)S(1)} collective-permute-done((f32[30,768]{1,0:T(8,128)S(1)}, f32[30,768]{1,0:T(8,128)S(1)}, u32[]{:S(2)}, u32[]{:S(2)}) %collective-permute-start.60) | collective-permute-done | bytes 92192 | tf_op jit(solution)/shard_map/ppermute | solution.py:572
  (712 shorter events, 291.0 us)
Async XLA Ops:
  7.3 559.5 %all-gather.3.cloned.1.call-start = ((), (), s32[]{:S(2)}) async-start(), calls=%async_computation | async-start | bytes 3932160 | tf_op jit(solution)/shard_map/all_gather | solution.py:947
  15.8 47.5 %collective-permute-start.4 = (bf16[192,768]{1,0:T(8,128)(2,1)S(1)}, bf16[192,768]{1,0:T(8,128)(2,1)S(1)}, u32[]{:S(2)}, u32[]{:S(2)}) collective-permute-start(bf16[192,768]{1,0:T(8,128)(2,1)S(1)} %get-tuple-element.392), channel_id=1, source_target_pairs={{0,1},{1,0},{2,3},{3,2},{4,5},{5,4},{6,7},{7,6},{8,9},{9,8},{10,11... | collective-permute-start | bytes 884744 | tf_op jit(solution)/shard_map/ppermute | solution.py:572
  58.4 22.5 %collective-permute-start.6 = (bf16[384,768]{1,0:T(8,128)(2,1)}, bf16[384,768]{1,0:T(8,128)(2,1)}, u32[]{:S(2)}, u32[]{:S(2)}) collective-permute-start(bf16[384,768]{1,0:T(8,128)(2,1)} %pad_maximum_fusion.23), channel_id=1, source_target_pairs={{0,2},{1,3},{2,0},{3,1},{4,6},{5,7},{6,4},{7,5},{8,10},{9,11},{10,... | collective-permute-start | bytes 1769480 | tf_op jit(solution)/shard_map/ppermute | solution.py:572
  74.0 34.5 %collective-permute-start.15 = (bf16[768,768]{1,0:T(8,128)(2,1)S(1)}, bf16[768,768]{1,0:T(8,128)(2,1)S(1)}, u32[]{:S(2)}, u32[]{:S(2)}) collective-permute-start(bf16[768,768]{1,0:T(8,128)(2,1)S(1)} %pad_maximum_fusion.13), channel_id=1, source_target_pairs={{0,1},{1,0},{2,3},{3,2},{4,5},{5,4},{6,7},{7,6},{8,9},{9,8},{10,11... | collective-permute-start | bytes 3538952 | tf_op jit(solution)/shard_map/ppermute | solution.py:572
  94.9 33.4 %collective-permute-start.19 = (bf16[768,768]{1,0:T(8,128)(2,1)S(1)}, bf16[768,768]{1,0:T(8,128)(2,1)S(1)}, u32[]{:S(2)}, u32[]{:S(2)}) collective-permute-start(bf16[768,768]{1,0:T(8,128)(2,1)S(1)} %pad_maximum_fusion.14), channel_id=1, source_target_pairs={{0,1},{1,0},{2,3},{3,2},{4,5},{5,4},{6,7},{7,6},{8,9},{9,8},{10,11... | collective-permute-start | bytes 3538952 | tf_op jit(solution)/shard_map/ppermute | solution.py:572
  103.9 42.4 %collective-permute-start.10 = (bf16[384,768]{1,0:T(8,128)(2,1)}, bf16[384,768]{1,0:T(8,128)(2,1)S(1)}, u32[]{:S(2)}, u32[]{:S(2)}) collective-permute-start(bf16[384,768]{1,0:T(8,128)(2,1)} %pad_maximum_fusion.25), channel_id=1, source_target_pairs={{0,2},{1,3},{2,0},{3,1},{4,6},{5,7},{6,4},{7,5},{8,10},{9,11},{10,... | collective-permute-start | bytes 1769480 | tf_op jit(solution)/shard_map/ppermute | solution.py:572
  105.1 41.2 %collective-permute-start.11 = (bf16[192,768]{1,0:T(8,128)(2,1)S(1)}, bf16[192,768]{1,0:T(8,128)(2,1)S(1)}, u32[]{:S(2)}, u32[]{:S(2)}) collective-permute-start(bf16[192,768]{1,0:T(8,128)(2,1)S(1)} %get-tuple-element.164), channel_id=1, source_target_pairs={{0,4},{1,5},{2,6},{3,7},{4,0},{5,1},{6,2},{7,3},{8,12},{9,13},{10,... | collective-permute-start | bytes 884744 | tf_op jit(solution)/shard_map/ppermute | solution.py:572
  119.4 31.6 %collective-permute-start.22 = (bf16[768,768]{1,0:T(8,128)(2,1)}, bf16[768,768]{1,0:T(8,128)(2,1)}, u32[]{:S(2)}, u32[]{:S(2)}) collective-permute-start(bf16[768,768]{1,0:T(8,128)(2,1)} %pad_maximum_fusion.15), channel_id=1, source_target_pairs={{0,1},{1,0},{2,3},{3,2},{4,5},{5,4},{6,7},{7,6},{8,9},{9,8},{10,11... | collective-permute-start | bytes 3538952 | tf_op jit(solution)/shard_map/ppermute | solution.py:572
  154.7 28.9 %collective-permute-start.12 = (bf16[384,768]{1,0:T(8,128)(2,1)S(1)}, bf16[384,768]{1,0:T(8,128)(2,1)S(1)}, u32[]{:S(2)}, u32[]{:S(2)}) collective-permute-start(bf16[384,768]{1,0:T(8,128)(2,1)S(1)} %pad_maximum_fusion.24), channel_id=1, source_target_pairs={{0,4},{1,5},{2,6},{3,7},{4,0},{5,1},{6,2},{7,3},{8,12},{9,13},{10,... | collective-permute-start | bytes 1769480 | tf_op jit(solution)/shard_map/ppermute | solution.py:572
  155.1 28.6 %collective-permute-start.13 = (bf16[384,768]{1,0:T(8,128)(2,1)S(1)}, bf16[384,768]{1,0:T(8,128)(2,1)S(1)}, u32[]{:S(2)}, u32[]{:S(2)}) collective-permute-start(bf16[384,768]{1,0:T(8,128)(2,1)S(1)} %pad_maximum_fusion.27), channel_id=1, source_target_pairs={{0,2},{1,3},{2,0},{3,1},{4,6},{5,7},{6,4},{7,5},{8,10},{9,11},{10,... | collective-permute-start | bytes 1769480 | tf_op jit(solution)/shard_map/ppermute | solution.py:572
  157.9 27.8 %collective-permute-start.25 = (bf16[768,768]{1,0:T(8,128)(2,1)S(1)}, bf16[768,768]{1,0:T(8,128)(2,1)S(1)}, u32[]{:S(2)}, u32[]{:S(2)}) collective-permute-start(bf16[768,768]{1,0:T(8,128)(2,1)S(1)} %pad_maximum_fusion.16), channel_id=1, source_target_pairs={{0,1},{1,0},{2,3},{3,2},{4,5},{5,4},{6,7},{7,6},{8,9},{9,8},{10,11... | collective-permute-start | bytes 3538952 | tf_op jit(solution)/shard_map/ppermute | solution.py:572
  183.7 28.1 %collective-permute-start.14 = (bf16[768,768]{1,0:T(8,128)(2,1)S(1)}, bf16[768,768]{1,0:T(8,128)(2,1)S(1)}, u32[]{:S(2)}, u32[]{:S(2)}) collective-permute-start(bf16[768,768]{1,0:T(8,128)(2,1)S(1)} %pad_maximum_fusion.12), channel_id=1, source_target_pairs={{0,2},{1,3},{2,0},{3,1},{4,6},{5,7},{6,4},{7,5},{8,10},{9,11},{10,... | collective-permute-start | bytes 3538952 | tf_op jit(solution)/shard_map/ppermute | solution.py:572
  183.9 27.9 %collective-permute-start.27 = (bf16[768,768]{1,0:T(8,128)(2,1)S(1)}, bf16[768,768]{1,0:T(8,128)(2,1)S(1)}, u32[]{:S(2)}, u32[]{:S(2)}) collective-permute-start(bf16[768,768]{1,0:T(8,128)(2,1)S(1)} %pad_maximum_fusion.17), channel_id=1, source_target_pairs={{0,1},{1,0},{2,3},{3,2},{4,5},{5,4},{6,7},{7,6},{8,9},{9,8},{10,11... | collective-permute-start | bytes 3538952 | tf_op jit(solution)/shard_map/ppermute | solution.py:572
  266.7 32.6 %collective-permute-start.32 = (bf16[768,768]{1,0:T(8,128)(2,1)S(1)}, bf16[768,768]{1,0:T(8,128)(2,1)S(1)}, u32[]{:S(2)}, u32[]{:S(2)}) collective-permute-start(bf16[768,768]{1,0:T(8,128)(2,1)S(1)} %convolution_convert_fusion.10), channel_id=1, source_target_pairs={{0,1},{1,0},{2,3},{3,2},{4,5},{5,4},{6,7},{7,6},{8,9},{9,8},{10,11... | collective-permute-start | bytes 3538952 | tf_op jit(solution)/shard_map/ppermute | solution.py:572
  268.2 31.0 %collective-permute-start.33 = (bf16[256,1536]{1,0:T(8,128)(2,1)S(1)}, bf16[256,1536]{1,0:T(8,128)(2,1)S(1)}, u32[]{:S(2)}, u32[]{:S(2)}) collective-permute-start(bf16[256,1536]{1,0:T(8,128)(2,1)S(1)} %copy-done.99), channel_id=1, source_target_pairs={{0,16},{8,24},{16,0},{24,8},{1,17},{9,25},{17,1},{25,9},{2,18},{10... | collective-permute-start | bytes 2359304 | tf_op jit(solution)/shard_map/ppermute | solution.py:572
  309.9 28.7 %collective-permute-start.36 = (bf16[768,768]{1,0:T(8,128)(2,1)}, bf16[768,768]{1,0:T(8,128)(2,1)}, u32[]{:S(2)}, u32[]{:S(2)}) collective-permute-start(bf16[768,768]{1,0:T(8,128)(2,1)} %fusion.53), channel_id=1, source_target_pairs={{0,1},{1,0},{2,3},{3,2},{4,5},{5,4},{6,7},{7,6},{8,9},{9,8},{10,11... | collective-permute-start | bytes 3538952 | tf_op jit(solution)/shard_map/ppermute | solution.py:572
  372.5 29.1 %collective-permute-start.44 = (bf16[768,768]{1,0:T(8,128)(2,1)}, bf16[768,768]{1,0:T(8,128)(2,1)}, u32[]{:S(2)}, u32[]{:S(2)}) collective-permute-start(bf16[768,768]{1,0:T(8,128)(2,1)} %fusion.56), channel_id=1, source_target_pairs={{0,1},{1,0},{2,3},{3,2},{4,5},{5,4},{6,7},{7,6},{8,9},{9,8},{10,11... | collective-permute-start | bytes 3538952 | tf_op jit(solution)/shard_map/ppermute | solution.py:572
  374.9 23.3 %collective-permute-start.45 = (bf16[192,768]{1,0:T(8,128)(2,1)}, bf16[192,768]{1,0:T(8,128)(2,1)}, u32[]{:S(2)}, u32[]{:S(2)}) collective-permute-start(bf16[192,768]{1,0:T(8,128)(2,1)} %slice.1014), channel_id=1, source_target_pairs={{0,4},{1,5},{2,6},{3,7},{4,0},{5,1},{6,2},{7,3},{8,12},{9,13},{10,... | collective-permute-start | bytes 884744 | tf_op jit(solution)/shard_map/ppermute | solution.py:572
  382.7 48.0 %collective-permute-start.48 = (bf16[768,768]{1,0:T(8,128)(2,1)}, bf16[768,768]{1,0:T(8,128)(2,1)S(1)}, u32[]{:S(2)}, u32[]{:S(2)}) collective-permute-start(bf16[768,768]{1,0:T(8,128)(2,1)} %fusion.59), channel_id=1, source_target_pairs={{0,1},{1,0},{2,3},{3,2},{4,5},{5,4},{6,7},{7,6},{8,9},{9,8},{10,11... | collective-permute-start | bytes 3538952 | tf_op jit(solution)/shard_map/ppermute | solution.py:572
  383.3 47.4 %collective-permute-start.46 = (bf16[1024,128]{1,0:T(8,128)(2,1)}, bf16[1024,128]{1,0:T(8,128)(2,1)}, u32[]{:S(2)}, u32[]{:S(2)}) collective-permute-start(bf16[1024,128]{1,0:T(8,128)(2,1)} %get-tuple-element.239), channel_id=1, source_target_pairs={{0,16},{8,24},{16,0},{24,8},{1,17},{9,25},{17,1},{25,9},{2,18},{10... | collective-permute-start | bytes 786440 | tf_op jit(solution)/shard_map/ppermute | solution.py:572
  396.7 57.8 %collective-permute-start.51 = (bf16[768,768]{1,0:T(8,128)(2,1)}, bf16[768,768]{1,0:T(8,128)(2,1)}, u32[]{:S(2)}, u32[]{:S(2)}) collective-permute-start(bf16[768,768]{1,0:T(8,128)(2,1)} %convolution_convert_fusion.9), channel_id=1, source_target_pairs={{0,1},{1,0},{2,3},{3,2},{4,5},{5,4},{6,7},{7,6},{8,9},{9,8},{10,11... | collective-permute-start | bytes 3538952 | tf_op jit(solution)/shard_map/ppermute | solution.py:572
  403.4 27.2 %collective-permute-start.47 = (bf16[384,768]{1,0:T(8,128)(2,1)S(1)}, bf16[384,768]{1,0:T(8,128)(2,1)S(1)}, u32[]{:S(2)}, u32[]{:S(2)}) collective-permute-start(bf16[384,768]{1,0:T(8,128)(2,1)S(1)} %slice.1007), channel_id=1, source_target_pairs={{0,2},{1,3},{2,0},{3,1},{4,6},{5,7},{6,4},{7,5},{8,10},{9,11},{10,... | collective-permute-start | bytes 1769480 | tf_op jit(solution)/shard_map/ppermute | solution.py:572
  428.4 26.0 %collective-permute-start.52 = (bf16[1024,128]{1,0:T(8,128)(2,1)S(1)}, bf16[1024,128]{1,0:T(8,128)(2,1)S(1)}, u32[]{:S(2)}, u32[]{:S(2)}) collective-permute-start(bf16[1024,128]{1,0:T(8,128)(2,1)S(1)} %get-tuple-element.402), channel_id=1, source_target_pairs={{0,16},{8,24},{16,0},{24,8},{1,17},{9,25},{17,1},{25,9},{2,18},{10... | collective-permute-start | bytes 786440 | tf_op jit(solution)/shard_map/ppermute | solution.py:572
  445.6 36.2 %collective-permute-start.61 = (bf16[768,768]{1,0:T(8,128)(2,1)}, bf16[768,768]{1,0:T(8,128)(2,1)}, u32[]{:S(2)}, u32[]{:S(2)}) collective-permute-start(bf16[768,768]{1,0:T(8,128)(2,1)} %convolution_convert_fusion.8), channel_id=1, source_target_pairs={{0,1},{1,0},{2,3},{3,2},{4,5},{5,4},{6,7},{7,6},{8,9},{9,8},{10,11... | collective-permute-start | bytes 3538952 | tf_op jit(solution)/shard_map/ppermute | solution.py:572
  458.2 23.6 %collective-permute-start.62 = (bf16[384,768]{1,0:T(8,128)(2,1)}, bf16[384,768]{1,0:T(8,128)(2,1)}, u32[]{:S(2)}, u32[]{:S(2)}) collective-permute-start(bf16[384,768]{1,0:T(8,128)(2,1)} %slice.1005), channel_id=1, source_target_pairs={{0,2},{1,3},{2,0},{3,1},{4,6},{5,7},{6,4},{7,5},{8,10},{9,11},{10,... | collective-permute-start | bytes 1769480 | tf_op jit(solution)/shard_map/ppermute | solution.py:572
  487.1 45.2 %collective-permute-start.71 = (bf16[192,768]{1,0:T(8,128)(2,1)}, bf16[192,768]{1,0:T(8,128)(2,1)}, u32[]{:S(2)}, u32[]{:S(2)}) collective-permute-start(bf16[192,768]{1,0:T(8,128)(2,1)} %slice.1012), channel_id=1, source_target_pairs={{0,4},{1,5},{2,6},{3,7},{4,0},{5,1},{6,2},{7,3},{8,12},{9,13},{10,... | collective-permute-start | bytes 884744 | tf_op jit(solution)/shard_map/ppermute | solution.py:572
  488.6 44.9 %collective-permute-start.66 = (bf16[192,768]{1,0:T(8,128)(2,1)}, bf16[192,768]{1,0:T(8,128)(2,1)}, u32[]{:S(2)}, u32[]{:S(2)}) collective-permute-start(bf16[192,768]{1,0:T(8,128)(2,1)} %slice.1013), channel_id=1, source_target_pairs={{0,4},{1,5},{2,6},{3,7},{4,0},{5,1},{6,2},{7,3},{8,12},{9,13},{10,... | collective-permute-start | bytes 884744 | tf_op jit(solution)/shard_map/ppermute | solution.py:572
  490.1 35.4 %collective-permute-start.54 = (bf16[256,1536]{1,0:T(8,128)(2,1)}, bf16[256,1536]{1,0:T(8,128)(2,1)}, u32[]{:S(2)}, u32[]{:S(2)}) collective-permute-start(bf16[256,1536]{1,0:T(8,128)(2,1)} %convolution_convert_fusion.4), channel_id=1, source_target_pairs={{0,16},{8,24},{16,0},{24,8},{1,17},{9,25},{17,1},{25,9},{2,18},{10... | collective-permute-start | bytes 2359304 | tf_op jit(solution)/shard_map/ppermute | solution.py:572
  491.1 27.9 %collective-permute-start.64 = (bf16[384,768]{1,0:T(8,128)(2,1)}, bf16[384,768]{1,0:T(8,128)(2,1)}, u32[]{:S(2)}, u32[]{:S(2)}) collective-permute-start(bf16[384,768]{1,0:T(8,128)(2,1)} %slice.1004), channel_id=1, source_target_pairs={{0,2},{1,3},{2,0},{3,1},{4,6},{5,7},{6,4},{7,5},{8,10},{9,11},{10,... | collective-permute-start | bytes 1769480 | tf_op jit(solution)/shard_map/ppermute | solution.py:572
  495.0 40.7 %collective-permute-start.63 = (bf16[192,768]{1,0:T(8,128)(2,1)}, bf16[192,768]{1,0:T(8,128)(2,1)}, u32[]{:S(2)}, u32[]{:S(2)}) collective-permute-start(bf16[192,768]{1,0:T(8,128)(2,1)} %slice.1011), channel_id=1, source_target_pairs={{0,4},{1,5},{2,6},{3,7},{4,0},{5,1},{6,2},{7,3},{8,12},{9,13},{10,... | collective-permute-start | bytes 884744 | tf_op jit(solution)/shard_map/ppermute | solution.py:572
  519.0 23.7 %collective-permute-start.68 = (bf16[768,256]{0,1:T(8,128)(2,1)S(1)}, bf16[768,256]{0,1:T(8,128)(2,1)}, u32[]{:S(2)}, u32[]{:S(2)}) collective-permute-start(bf16[768,256]{0,1:T(8,128)(2,1)S(1)} %pad_maximum_fusion.33), channel_id=1, source_target_pairs={{0,1},{1,0},{2,3},{3,2},{4,5},{5,4},{6,7},{7,6},{8,9},{9,8},{10,11... | collective-permute-start | bytes 1179656 | tf_op jit(solution)/shard_map/ppermute | solution.py:572
  532.3 35.8 %collective-permute-start.55 = (bf16[512,1536]{1,0:T(8,128)(2,1)}, bf16[512,1536]{1,0:T(8,128)(2,1)}, u32[]{:S(2)}, u32[]{:S(2)}) collective-permute-start(bf16[512,1536]{1,0:T(8,128)(2,1)} %pad_maximum_fusion.11), channel_id=1, source_target_pairs={{0,8},{8,0},{16,24},{24,16},{1,9},{9,1},{17,25},{25,17},{2,10},{10... | collective-permute-start | bytes 4718600 | tf_op jit(solution)/shard_map/ppermute | solution.py:572
  (196 other events, 2987.3 us)
Sparse Core Ops, SparseCore 0:
  487.3 40.8 all-gather.2

commit v6 on v5

--- a/solution.py
+++ b/solution.py
@@ -14,7 +14,7 @@
 CHUNK = 128
 LANES = 128
 GROUP = 16
-TAIL = 8
+TAIL = 16
 FAR = -10000.0
 PRECISE = lax.Precision.HIGHEST
 BF16 = jnp.bfloat16
@@ -143,7 +143,7 @@
     for pair in range(width // LANES):
         at = slice(pair * LANES, (pair + 1) * LANES)
         tail_x[:TAIL, at] = tail_x[CHUNK:, at]
-        tail_x[TAIL:, at] = x_ref[:, at]
+        tail_x[TAIL:, at] = x_ref[:, at].astype(F32)
         pre = conv_pre(tail_x, at, taps_ref[:, at], bias_ref[:, at], aux)
         x_conv = pre * jax.nn.sigmoid(pre)
         inputs = x_conv * dt_wide[:, at]
@@ -359,8 +359,8 @@
     lane = iota((CHUNK, LANES), 1)
     for pair in range(width // LANES):
         at = slice(pair * LANES, (pair + 1) * LANES)
-        joined_x[:TAIL, at] = x_tail_ref[:, at]
-        joined_x[TAIL:, at] = x_ref[:, at]
+        joined_x[:TAIL, at] = x_tail_ref[:, at].astype(F32)
+        joined_x[TAIL:, at] = x_ref[:, at].astype(F32)
         pre = conv_pre(joined_x, at, taps_ref[:, at], bias_ref[:, at], aux)
         sig = jax.nn.sigmoid(pre)
         x_conv = pre * sig
@@ -821,7 +821,7 @@
     stream = hidden_low.astype(F32)
     normed0 = (stream * rms_of(stream) * gains[0]).astype(BF16)
     stream0 = hidden_low[:quarter].astype(F32)
-    x_pre0 = dot(normed0, x_rows[0])
+    x_pre0 = dot(normed0, x_rows[0]).astype(BF16)
     bcdt_pre0 = dot(after(normed0, x_pre0, z0_near, out0_far), bcdt_rows[0])
     gate_pre0 = dot(after(normed0, bcdt_pre0, out0_near, x1_far), z_rows[0]).astype(BF16)
     u0, y0, sq, kept0 = scan_fwd(me_row, x_pre0, bcdt_pre0, gate_pre0, side, weights[0])
@@ -846,12 +846,13 @@
     normed1 = jnp.concatenate([normed_half, swap(normed_half, "tensor", 1)], 0)
     scaled0 = (u0.astype(F32) * reordered(inv0, me)[:, None]).astype(BF16)
 
-    x_pre1 = dot(after(normed1, out1_near), x_rows[1])
+    x_pre1 = dot(after(normed1, out1_near), x_rows[1]).astype(BF16)
     bcdt_pre1 = dot(normed1, bcdt_rows[1])
     gate_pre1 = dot(normed1, z_rows[1]).astype(BF16)
     u1, y1, sq, kept1 = scan_fwd(me_row, x_pre1, bcdt_pre1, gate_pre1, side, weights[1])
     scaled_grad1 = dot(cotangent_low, out_rows[1])
     cross = restored(jnp.sum(scaled_grad1 * u1.astype(F32), -1), me)
+    scaled_grad1 = scaled_grad1.astype(BF16)
     both = tensor_sum(jnp.stack([sq[0], cross]))
     mixed_sent = dot_t(u1[half:], out_rows[1]).astype(BF16)
     mixed_mine = dot_t(u1[:half], out_rows[1])
@@ -933,7 +934,7 @@
     grad0 = lax.optimization_barrier(grad0)
     out_sent0 = sent_half(grad0, scaled0)
     out_got0 = swap(out_sent0, "dp", 1)
-    scaled_grad0 = dot(after(grad0, out_sent0), out_rows[0])
+    scaled_grad0 = dot(after(grad0, out_sent0), out_rows[0]).astype(BF16)
     columns = jnp.stack([inv0, inv0 * inv0 * inv0 * cross / INNER], 1)
     g_gate0, g_y, d_gain0 = gate_bwd(
         me_row, scaled_grad0, y0, gate_pre0, columns, gated_gain[0][None]

time: 592 us -> 591 us (level)
    unnamed x319 -> x313, local copies, waits for them, and re-layouts: 18.4 us -> 18 us
  transfers between devices with their start and end apart: 73 -> 73, of which waited for: 33 -> 34; matrix products, arithmetic and copies ran while one was open for 33% -> 33% of each run, Pallas kernels for 11% -> 12%
where the time goes in v6:
time: 591 us; the launch traced here: 582 us
  waiting for transfers between devices  162 us (27%)
  matrix products  135 us (23%)
  Pallas kernels  84 us (14%)
  starting transfers between devices  71.8 us (12%)
  other arithmetic  65.7 us (11%)
  local copies, waits for them, and re-layouts  46.1 us (8%)
  between operations  17.5 us (3%)
    ppermute x72, waiting for transfers between devices, swap(): return lax.ppermute(values, axis, partners(lax.axis_size(axis), step))  162 us
    ppermute x72, starting transfers between devices, swap(): return lax.ppermute(values, axis, partners(lax.axis_size(axis), step))  71.7 us
    dot_general x18, matrix products, dot_t(): lax.dot_general(lhs, rhs, (((1,), (1,)), ((), ())), preferred_element_typ...  50.9 us
    pallas_call x2, Pallas kernels, scan_bwd(): pl.pallas_call(scan_bwd_kernel, grid_spec=pltpu.PrefetchScalarGridSpec(nu...  49.8 us
    dot_general x10, matrix products, dot(): lax.dot_general(lhs, rhs, (((1,), (0,)), ((), ())), preferred_element_typ...  49.5 us
    dot_general x16, matrix products, grad_half(): return lax.dot_general(taken, grads, dims, preferred_element_type=F32)  32.5 us
    pallas_call x2, Pallas kernels, scan_fwd(): pl.pallas_call(scan_fwd_kernel, grid_spec=pltpu.PrefetchScalarGridSpec(nu...  25.1 us
    unnamed x313, local copies, waits for them, and re-layouts  18 us
  transfers between devices with their start and end apart: 73, of which 34 were waited for; matrix products, arithmetic and copies ran while one was open for 33% of the time, Pallas kernels for 12%

profile of v6, /device:TPU:0, one launch (start us, length us, event | category | flops | bytes accessed | tf_op | source)
XLA Modules:
  0.0 581.9 jit_solution(13497060685185285111)
XLA Ops:
  9.3 4.1 collective-permute-start.1
  18.8 8.1 %collective-permute-done.1 = bf16[192,256]{0,1:T(8,128)(2,1)S(1)} collective-permute-done((bf16[192,256]{0,1:T(8,128)(2,1)S(1)}, bf16[192,256]{0,1:T(8,128)(2,1)S(1)}, u32[]{:S(2)}, u32[]{:S(2)}) %collective-permute-start.1) | collective-permute-done | bytes 98336 | tf_op jit(solution)/shard_map/ppermute | solution.py:572
  27.7 4.7 collective-permute-done
  42.6 4.0 constant_dynamic-slice_fusion.20
  63.3 6.4 %convolution_convert_fusion.1 = bf16[1024,1536]{1,0:T(8,128)(2,1)} fusion(bf16[1024,1536]{1,0:T(8,128)(2,1)S(1)} %pad_maximum_fusion, bf16[1536,1536]{1,0:T(8,128)(2,1)S(1)} %fusion), kind=kOutput, calls=%fused_computation.10 | convolution fusion | flops 4833411072 | bytes 11010048 | tf_op jit(solution)/shard_map/dot_general | solution.py:676
  84.4 8.5 %convolution_convert_fusion = bf16[1024,1536]{1,0:T(8,128)(2,1)} fusion(bf16[1024,1536]{1,0:T(8,128)(2,1)} %pad_maximum_fusion.1, bf16[1536,1536]{1,0:T(8,128)(2,1)S(1)} %copy-done.33), kind=kOutput, calls=%fused_computation.9 | convolution fusion | flops 4833411072 | bytes 11010048 | tf_op jit(solution)/shard_map/dot_general | solution.py:676
  99.7 4.3 collective-permute-done.9
  108.6 5.3 convolution_convert_fusion.10.x_ref.x_tail_ref
  120.3 7.9 %collective-permute-done.19 = bf16[768,768]{1,0:T(8,128)(2,1)S(1)} collective-permute-done((bf16[768,768]{1,0:T(8,128)(2,1)S(1)}, bf16[768,768]{1,0:T(8,128)(2,1)S(1)}, u32[]{:S(2)}, u32[]{:S(2)}) %collective-permute-start.19) | collective-permute-done | bytes 1179680 | tf_op jit(solution)/shard_map/ppermute | solution.py:572
  128.3 5.3 convolution_convert_fusion.9.gate_ref
  133.7 12.6 %scan_fwd.2 = (bf16[1024,768]{1,0:T(8,128)(2,1)S(1)}, bf16[1024,768]{1,0:T(8,128)(2,1)S(1)}, f32[8,1024]{1,0:T(8,128)S(1)}, bf16[8,128,768]{2,1,0:T(8,128)(2,1)S(1)}) custom-call(s32[1]{0:T(128)} %bitcast.me_ref, bf16[1024,768]{1,0:T(8,128)(2,1)} %convolution_convert_fusion.10.x_ref.x_tail_ref, f32[1024,384]{1,0:T(8,128)} %fusion.167.bcdt_ref.bc_tail_ref, ...), custom_call_target="tpu_custom_call" | custom-call | flops 14092861440 | bytes 15728640 | tf_op jit(solution)/shard_map/scan_fwd/pallas_call | solution.py:194
  146.4 4.7 collective-permute-done.22
  164.5 19.1 %collective-permute-done.12 = bf16[384,768]{1,0:T(8,128)(2,1)S(1)} collective-permute-done((bf16[384,768]{1,0:T(8,128)(2,1)S(1)}, bf16[384,768]{1,0:T(8,128)(2,1)S(1)}, u32[]{:S(2)}, u32[]{:S(2)}) %collective-permute-start.12) | collective-permute-done | bytes 589856 | tf_op jit(solution)/shard_map/ppermute | solution.py:572
  188.8 17.2 %collective-permute-done.26 = bf16[256,1536]{1,0:T(8,128)(2,1)S(1)} collective-permute-done((bf16[256,1536]{1,0:T(8,128)(2,1)S(1)}, bf16[256,1536]{1,0:T(8,128)(2,1)S(1)}, u32[]{:S(2)}, u32[]{:S(2)}) %collective-permute-start.26) | collective-permute-done | bytes 786464 | tf_op jit(solution)/shard_map/ppermute | solution.py:572
  206.1 5.8 collective-permute-done.27
  226.0 12.4 %scan_fwd.3 = (bf16[1024,768]{1,0:T(8,128)(2,1)S(1)}, bf16[1024,768]{1,0:T(8,128)(2,1)S(1)}, f32[8,1024]{1,0:T(8,128)S(1)}, bf16[8,128,768]{2,1,0:T(8,128)(2,1)S(1)}) custom-call(s32[1]{0:T(128)} %bitcast.me_ref, bf16[1024,768]{1,0:T(8,128)(2,1)} %convolution_convert_fusion.8.x_ref.x_tail_ref, f32[1024,384]{1,0:T(8,128)} %fusion.168.bcdt_ref.bc_tail_ref, ...), custom_call_target="tpu_custom_call" | custom-call | flops 14092861440 | bytes 15728640 | tf_op jit(solution)/shard_map/scan_fwd/pallas_call | solution.py:194
  241.3 6.5 %fusion.10 = (f32[1024]{0:T(1024)S(1)}, bf16[1024,768]{1,0:T(8,128)(2,1)}) fusion(bf16[1024,768]{1,0:T(8,128)(2,1)S(1)} %get-tuple-element.201, bf16[1024,1536]{1,0:T(8,128)(2,1)} %convolution_convert_fusion, bf16[1536,768]{1,0:T(8,128)(2,1)} %copy-done.122), kind=kOutput, calls=%fused_computation.23 | convolution fusion | flops 2419063808 | bytes 8654848 | tf_op jit(solution)/shard_map/dot_general | solution.py:676
  259.4 4.6 gate_bwd.2
  267.7 24.8 %scan_bwd.2 = (bf16[1024,768]{1,0:T(8,128)(2,1)S(1)}, bf16[1024,256]{1,0:T(8,128)(2,1)S(1)}, bf16[1024,128]{1,0:T(8,128)(2,1)S(1)}, f32[8,768]{1,0:T(8,128)S(1)}, f32[8,256]{1,0:T(8,128)S(1)}) custom-call(s32[1]{0:T(128)} %bitcast.me_ref, bf16[1024,768]{1,0:T(8,128)(2,1)S(1)} %get-tuple-element.205.g_ref, ...), custom_call_target="tpu_custom_call" | custom-call | flops 28185722880 | bytes 15728640 | tf_op jit(solution)/shard_map/scan_bwd/pallas_call | solution.py:475
  300.7 5.0 fusion.13
  314.5 5.6 fusion.6
  333.2 3.9 collective-permute-done.36
  337.2 5.5 collective-permute-done.35
  350.6 13.0 %collective-permute-done.39 = f32[256]{0:T(256)S(1)} collective-permute-done((f32[256]{0:T(256)S(1)}, f32[256]{0:T(256)S(1)}, u32[]{:S(2)}, u32[]{:S(2)}) %collective-permute-start.39) | collective-permute-done | bytes 1056 | tf_op jit(solution)/shard_map/ppermute | solution.py:572
  382.5 3.9 convolution_convert_fusion.6.gs_ref
  386.4 4.6 gate_bwd.3
  395.0 5.2 collective-permute-done.44
  402.2 25.0 %scan_bwd.3 = (bf16[1024,768]{1,0:T(8,128)(2,1)S(1)}, bf16[1024,256]{1,0:T(8,128)(2,1)S(1)}, bf16[1024,128]{1,0:T(8,128)(2,1)S(1)}, f32[8,768]{1,0:T(8,128)S(1)}, f32[8,256]{1,0:T(8,128)S(1)}) custom-call(s32[1]{0:T(128)} %bitcast.me_ref, bf16[1024,768]{1,0:T(8,128)(2,1)S(1)} %get-tuple-element.236.g_ref, ...), custom_call_target="tpu_custom_call" | custom-call | flops 28185722880 | bytes 15728640 | tf_op jit(solution)/shard_map/scan_bwd/pallas_call | solution.py:475
  465.1 6.9 %collective-permute-done.50 = bf16[256,1536]{1,0:T(8,128)(2,1)} collective-permute-done((bf16[256,1536]{1,0:T(8,128)(2,1)}, bf16[256,1536]{1,0:T(8,128)(2,1)}, u32[]{:S(2)}, u32[]{:S(2)}) %collective-permute-start.50) | collective-permute-done | bytes 786464 | tf_op jit(solution)/shard_map/ppermute | solution.py:572
  474.5 6.3 %convolution_convert_fusion.4 = bf16[256,1536]{1,0:T(8,128)(2,1)} fusion(bf16[1536,1536]{1,0:T(8,128)(2,1)} %copy-done.32, f32[256,1536]{1,0:T(8,128)S(1)} %get-tuple-element.261, f32[256]{0:T(256)S(1)} %broadcast_multiply_fusion, f32[1536]{0:T(1024)S(1)} %copy-done.121, f32[256]{0:T(256)S(1)} %add_rsqrt_fusion.3, ...), kind=kOutput, calls=%fused_computation.35 | convolution fusion | flops 1214251008 | bytes 11812864 | tf_op jit(solution)/shard_map/dot_general | solution.py:680
  502.4 15.5 %collective-permute-done.64 = bf16[384,768]{1,0:T(8,128)(2,1)} collective-permute-done((bf16[384,768]{1,0:T(8,128)(2,1)}, bf16[384,768]{1,0:T(8,128)(2,1)}, u32[]{:S(2)}, u32[]{:S(2)}) %collective-permute-start.64) | collective-permute-done | bytes 589856 | tf_op jit(solution)/shard_map/ppermute | solution.py:572
  554.0 6.1 %collective-permute-done.60 = f32[30,768]{1,0:T(8,128)S(1)} collective-permute-done((f32[30,768]{1,0:T(8,128)S(1)}, f32[30,768]{1,0:T(8,128)S(1)}, u32[]{:S(2)}, u32[]{:S(2)}) %collective-permute-start.60) | collective-permute-done | bytes 92192 | tf_op jit(solution)/shard_map/ppermute | solution.py:572
  (706 shorter events, 291.8 us)
Async XLA Ops:
  7.3 558.4 %all-gather.3.cloned.1.call-start = ((), (), s32[]{:S(2)}) async-start(), calls=%async_computation | async-start | bytes 3932160 | tf_op jit(solution)/shard_map/all_gather | solution.py:948
  15.9 47.4 %collective-permute-start.4 = (bf16[192,768]{1,0:T(8,128)(2,1)S(1)}, bf16[192,768]{1,0:T(8,128)(2,1)S(1)}, u32[]{:S(2)}, u32[]{:S(2)}) collective-permute-start(bf16[192,768]{1,0:T(8,128)(2,1)S(1)} %get-tuple-element.394), channel_id=1, source_target_pairs={{0,1},{1,0},{2,3},{3,2},{4,5},{5,4},{6,7},{7,6},{8,9},{9,8},{10,11... | collective-permute-start | bytes 884744 | tf_op jit(solution)/shard_map/ppermute | solution.py:572
  58.4 22.5 %collective-permute-start.6 = (bf16[384,768]{1,0:T(8,128)(2,1)}, bf16[384,768]{1,0:T(8,128)(2,1)}, u32[]{:S(2)}, u32[]{:S(2)}) collective-permute-start(bf16[384,768]{1,0:T(8,128)(2,1)} %pad_maximum_fusion.23), channel_id=1, source_target_pairs={{0,2},{1,3},{2,0},{3,1},{4,6},{5,7},{6,4},{7,5},{8,10},{9,11},{10,... | collective-permute-start | bytes 1769480 | tf_op jit(solution)/shard_map/ppermute | solution.py:572
  74.0 34.5 %collective-permute-start.15 = (bf16[768,768]{1,0:T(8,128)(2,1)S(1)}, bf16[768,768]{1,0:T(8,128)(2,1)S(1)}, u32[]{:S(2)}, u32[]{:S(2)}) collective-permute-start(bf16[768,768]{1,0:T(8,128)(2,1)S(1)} %pad_maximum_fusion.13), channel_id=1, source_target_pairs={{0,1},{1,0},{2,3},{3,2},{4,5},{5,4},{6,7},{7,6},{8,9},{9,8},{10,11... | collective-permute-start | bytes 3538952 | tf_op jit(solution)/shard_map/ppermute | solution.py:572
  94.9 33.4 %collective-permute-start.19 = (bf16[768,768]{1,0:T(8,128)(2,1)S(1)}, bf16[768,768]{1,0:T(8,128)(2,1)S(1)}, u32[]{:S(2)}, u32[]{:S(2)}) collective-permute-start(bf16[768,768]{1,0:T(8,128)(2,1)S(1)} %pad_maximum_fusion.14), channel_id=1, source_target_pairs={{0,1},{1,0},{2,3},{3,2},{4,5},{5,4},{6,7},{7,6},{8,9},{9,8},{10,11... | collective-permute-start | bytes 3538952 | tf_op jit(solution)/shard_map/ppermute | solution.py:572
  103.9 42.4 %collective-permute-start.10 = (bf16[384,768]{1,0:T(8,128)(2,1)}, bf16[384,768]{1,0:T(8,128)(2,1)S(1)}, u32[]{:S(2)}, u32[]{:S(2)}) collective-permute-start(bf16[384,768]{1,0:T(8,128)(2,1)} %pad_maximum_fusion.25), channel_id=1, source_target_pairs={{0,2},{1,3},{2,0},{3,1},{4,6},{5,7},{6,4},{7,5},{8,10},{9,11},{10,... | collective-permute-start | bytes 1769480 | tf_op jit(solution)/shard_map/ppermute | solution.py:572
  105.1 41.2 %collective-permute-start.11 = (bf16[192,768]{1,0:T(8,128)(2,1)S(1)}, bf16[192,768]{1,0:T(8,128)(2,1)S(1)}, u32[]{:S(2)}, u32[]{:S(2)}) collective-permute-start(bf16[192,768]{1,0:T(8,128)(2,1)S(1)} %get-tuple-element.164), channel_id=1, source_target_pairs={{0,4},{1,5},{2,6},{3,7},{4,0},{5,1},{6,2},{7,3},{8,12},{9,13},{10,... | collective-permute-start | bytes 884744 | tf_op jit(solution)/shard_map/ppermute | solution.py:572
  118.9 32.2 %collective-permute-start.22 = (bf16[768,768]{1,0:T(8,128)(2,1)}, bf16[768,768]{1,0:T(8,128)(2,1)}, u32[]{:S(2)}, u32[]{:S(2)}) collective-permute-start(bf16[768,768]{1,0:T(8,128)(2,1)} %pad_maximum_fusion.15), channel_id=1, source_target_pairs={{0,1},{1,0},{2,3},{3,2},{4,5},{5,4},{6,7},{7,6},{8,9},{9,8},{10,11... | collective-permute-start | bytes 3538952 | tf_op jit(solution)/shard_map/ppermute | solution.py:572
  154.7 28.9 %collective-permute-start.12 = (bf16[384,768]{1,0:T(8,128)(2,1)S(1)}, bf16[384,768]{1,0:T(8,128)(2,1)S(1)}, u32[]{:S(2)}, u32[]{:S(2)}) collective-permute-start(bf16[384,768]{1,0:T(8,128)(2,1)S(1)} %pad_maximum_fusion.24), channel_id=1, source_target_pairs={{0,4},{1,5},{2,6},{3,7},{4,0},{5,1},{6,2},{7,3},{8,12},{9,13},{10,... | collective-permute-start | bytes 1769480 | tf_op jit(solution)/shard_map/ppermute | solution.py:572
  155.1 28.6 %collective-permute-start.13 = (bf16[384,768]{1,0:T(8,128)(2,1)S(1)}, bf16[384,768]{1,0:T(8,128)(2,1)S(1)}, u32[]{:S(2)}, u32[]{:S(2)}) collective-permute-start(bf16[384,768]{1,0:T(8,128)(2,1)S(1)} %pad_maximum_fusion.27), channel_id=1, source_target_pairs={{0,2},{1,3},{2,0},{3,1},{4,6},{5,7},{6,4},{7,5},{8,10},{9,11},{10,... | collective-permute-start | bytes 1769480 | tf_op jit(solution)/shard_map/ppermute | solution.py:572
  157.9 27.8 %collective-permute-start.25 = (bf16[768,768]{1,0:T(8,128)(2,1)S(1)}, bf16[768,768]{1,0:T(8,128)(2,1)S(1)}, u32[]{:S(2)}, u32[]{:S(2)}) collective-permute-start(bf16[768,768]{1,0:T(8,128)(2,1)S(1)} %pad_maximum_fusion.16), channel_id=1, source_target_pairs={{0,1},{1,0},{2,3},{3,2},{4,5},{5,4},{6,7},{7,6},{8,9},{9,8},{10,11... | collective-permute-start | bytes 3538952 | tf_op jit(solution)/shard_map/ppermute | solution.py:572
  163.8 21.9 %collective-permute-start.24 = (bf16[256,1536]{1,0:T(8,128)(2,1)S(1)}, bf16[256,1536]{1,0:T(8,128)(2,1)S(1)}, u32[]{:S(2)}, u32[]{:S(2)}) collective-permute-start(bf16[256,1536]{1,0:T(8,128)(2,1)S(1)} %slice.1003), channel_id=1, source_target_pairs={{0,16},{8,24},{16,0},{24,8},{1,17},{9,25},{17,1},{25,9},{2,18},{10... | collective-permute-start | bytes 2359304 | tf_op jit(solution)/shard_map/ppermute | solution.py:572
  183.7 28.1 %collective-permute-start.14 = (bf16[768,768]{1,0:T(8,128)(2,1)S(1)}, bf16[768,768]{1,0:T(8,128)(2,1)S(1)}, u32[]{:S(2)}, u32[]{:S(2)}) collective-permute-start(bf16[768,768]{1,0:T(8,128)(2,1)S(1)} %pad_maximum_fusion.12), channel_id=1, source_target_pairs={{0,2},{1,3},{2,0},{3,1},{4,6},{5,7},{6,4},{7,5},{8,10},{9,11},{10,... | collective-permute-start | bytes 3538952 | tf_op jit(solution)/shard_map/ppermute | solution.py:572
  183.9 27.9 %collective-permute-start.27 = (bf16[768,768]{1,0:T(8,128)(2,1)S(1)}, bf16[768,768]{1,0:T(8,128)(2,1)S(1)}, u32[]{:S(2)}, u32[]{:S(2)}) collective-permute-start(bf16[768,768]{1,0:T(8,128)(2,1)S(1)} %pad_maximum_fusion.17), channel_id=1, source_target_pairs={{0,1},{1,0},{2,3},{3,2},{4,5},{5,4},{6,7},{7,6},{8,9},{9,8},{10,11... | collective-permute-start | bytes 3538952 | tf_op jit(solution)/shard_map/ppermute | solution.py:572
  265.4 32.6 %collective-permute-start.32 = (bf16[768,768]{1,0:T(8,128)(2,1)S(1)}, bf16[768,768]{1,0:T(8,128)(2,1)S(1)}, u32[]{:S(2)}, u32[]{:S(2)}) collective-permute-start(bf16[768,768]{1,0:T(8,128)(2,1)S(1)} %convolution_convert_fusion.13), channel_id=1, source_target_pairs={{0,1},{1,0},{2,3},{3,2},{4,5},{5,4},{6,7},{7,6},{8,9},{9,8},{10,11... | collective-permute-start | bytes 3538952 | tf_op jit(solution)/shard_map/ppermute | solution.py:572
  267.0 31.0 %collective-permute-start.33 = (bf16[256,1536]{1,0:T(8,128)(2,1)S(1)}, bf16[256,1536]{1,0:T(8,128)(2,1)S(1)}, u32[]{:S(2)}, u32[]{:S(2)}) collective-permute-start(bf16[256,1536]{1,0:T(8,128)(2,1)S(1)} %copy-done.98), channel_id=1, source_target_pairs={{0,16},{8,24},{16,0},{24,8},{1,17},{9,25},{17,1},{25,9},{2,18},{10... | collective-permute-start | bytes 2359304 | tf_op jit(solution)/shard_map/ppermute | solution.py:572
  308.4 28.7 %collective-permute-start.36 = (bf16[768,768]{1,0:T(8,128)(2,1)}, bf16[768,768]{1,0:T(8,128)(2,1)}, u32[]{:S(2)}, u32[]{:S(2)}) collective-permute-start(bf16[768,768]{1,0:T(8,128)(2,1)} %fusion.53), channel_id=1, source_target_pairs={{0,1},{1,0},{2,3},{3,2},{4,5},{5,4},{6,7},{7,6},{8,9},{9,8},{10,11... | collective-permute-start | bytes 3538952 | tf_op jit(solution)/shard_map/ppermute | solution.py:572
  371.2 29.1 %collective-permute-start.44 = (bf16[768,768]{1,0:T(8,128)(2,1)}, bf16[768,768]{1,0:T(8,128)(2,1)}, u32[]{:S(2)}, u32[]{:S(2)}) collective-permute-start(bf16[768,768]{1,0:T(8,128)(2,1)} %fusion.56), channel_id=1, source_target_pairs={{0,1},{1,0},{2,3},{3,2},{4,5},{5,4},{6,7},{7,6},{8,9},{9,8},{10,11... | collective-permute-start | bytes 3538952 | tf_op jit(solution)/shard_map/ppermute | solution.py:572
  381.4 48.1 %collective-permute-start.48 = (bf16[768,768]{1,0:T(8,128)(2,1)}, bf16[768,768]{1,0:T(8,128)(2,1)S(1)}, u32[]{:S(2)}, u32[]{:S(2)}) collective-permute-start(bf16[768,768]{1,0:T(8,128)(2,1)} %fusion.59), channel_id=1, source_target_pairs={{0,1},{1,0},{2,3},{3,2},{4,5},{5,4},{6,7},{7,6},{8,9},{9,8},{10,11... | collective-permute-start | bytes 3538952 | tf_op jit(solution)/shard_map/ppermute | solution.py:572
  382.0 47.5 %collective-permute-start.46 = (bf16[1024,128]{1,0:T(8,128)(2,1)}, bf16[1024,128]{1,0:T(8,128)(2,1)}, u32[]{:S(2)}, u32[]{:S(2)}) collective-permute-start(bf16[1024,128]{1,0:T(8,128)(2,1)} %get-tuple-element.239), channel_id=1, source_target_pairs={{0,16},{8,24},{16,0},{24,8},{1,17},{9,25},{17,1},{25,9},{2,18},{10... | collective-permute-start | bytes 786440 | tf_op jit(solution)/shard_map/ppermute | solution.py:572
  393.5 59.9 %collective-permute-start.51 = (bf16[768,768]{1,0:T(8,128)(2,1)}, bf16[768,768]{1,0:T(8,128)(2,1)}, u32[]{:S(2)}, u32[]{:S(2)}) collective-permute-start(bf16[768,768]{1,0:T(8,128)(2,1)} %convolution_convert_fusion.12), channel_id=1, source_target_pairs={{0,1},{1,0},{2,3},{3,2},{4,5},{5,4},{6,7},{7,6},{8,9},{9,8},{10,11... | collective-permute-start | bytes 3538952 | tf_op jit(solution)/shard_map/ppermute | solution.py:572
  402.1 27.4 %collective-permute-start.47 = (bf16[384,768]{1,0:T(8,128)(2,1)S(1)}, bf16[384,768]{1,0:T(8,128)(2,1)S(1)}, u32[]{:S(2)}, u32[]{:S(2)}) collective-permute-start(bf16[384,768]{1,0:T(8,128)(2,1)S(1)} %slice.1007), channel_id=1, source_target_pairs={{0,2},{1,3},{2,0},{3,1},{4,6},{5,7},{6,4},{7,5},{8,10},{9,11},{10,... | collective-permute-start | bytes 1769480 | tf_op jit(solution)/shard_map/ppermute | solution.py:572
  427.3 26.1 %collective-permute-start.52 = (bf16[1024,128]{1,0:T(8,128)(2,1)S(1)}, bf16[1024,128]{1,0:T(8,128)(2,1)S(1)}, u32[]{:S(2)}, u32[]{:S(2)}) collective-permute-start(bf16[1024,128]{1,0:T(8,128)(2,1)S(1)} %get-tuple-element.404), channel_id=1, source_target_pairs={{0,16},{8,24},{16,0},{24,8},{1,17},{9,25},{17,1},{25,9},{2,18},{10... | collective-permute-start | bytes 786440 | tf_op jit(solution)/shard_map/ppermute | solution.py:572
  444.5 36.2 %collective-permute-start.61 = (bf16[768,768]{1,0:T(8,128)(2,1)}, bf16[768,768]{1,0:T(8,128)(2,1)}, u32[]{:S(2)}, u32[]{:S(2)}) collective-permute-start(bf16[768,768]{1,0:T(8,128)(2,1)} %convolution_convert_fusion.11), channel_id=1, source_target_pairs={{0,1},{1,0},{2,3},{3,2},{4,5},{5,4},{6,7},{7,6},{8,9},{9,8},{10,11... | collective-permute-start | bytes 3538952 | tf_op jit(solution)/shard_map/ppermute | solution.py:572
  457.1 23.6 %collective-permute-start.62 = (bf16[384,768]{1,0:T(8,128)(2,1)}, bf16[384,768]{1,0:T(8,128)(2,1)}, u32[]{:S(2)}, u32[]{:S(2)}) collective-permute-start(bf16[384,768]{1,0:T(8,128)(2,1)} %slice.1005), channel_id=1, source_target_pairs={{0,2},{1,3},{2,0},{3,1},{4,6},{5,7},{6,4},{7,5},{8,10},{9,11},{10,... | collective-permute-start | bytes 1769480 | tf_op jit(solution)/shard_map/ppermute | solution.py:572
  486.1 45.1 %collective-permute-start.71 = (bf16[192,768]{1,0:T(8,128)(2,1)}, bf16[192,768]{1,0:T(8,128)(2,1)}, u32[]{:S(2)}, u32[]{:S(2)}) collective-permute-start(bf16[192,768]{1,0:T(8,128)(2,1)} %slice.1012), channel_id=1, source_target_pairs={{0,4},{1,5},{2,6},{3,7},{4,0},{5,1},{6,2},{7,3},{8,12},{9,13},{10,... | collective-permute-start | bytes 884744 | tf_op jit(solution)/shard_map/ppermute | solution.py:572
  487.5 44.9 %collective-permute-start.66 = (bf16[192,768]{1,0:T(8,128)(2,1)}, bf16[192,768]{1,0:T(8,128)(2,1)}, u32[]{:S(2)}, u32[]{:S(2)}) collective-permute-start(bf16[192,768]{1,0:T(8,128)(2,1)} %slice.1013), channel_id=1, source_target_pairs={{0,4},{1,5},{2,6},{3,7},{4,0},{5,1},{6,2},{7,3},{8,12},{9,13},{10,... | collective-permute-start | bytes 884744 | tf_op jit(solution)/shard_map/ppermute | solution.py:572
  489.0 35.3 %collective-permute-start.54 = (bf16[256,1536]{1,0:T(8,128)(2,1)}, bf16[256,1536]{1,0:T(8,128)(2,1)}, u32[]{:S(2)}, u32[]{:S(2)}) collective-permute-start(bf16[256,1536]{1,0:T(8,128)(2,1)} %convolution_convert_fusion.4), channel_id=1, source_target_pairs={{0,16},{8,24},{16,0},{24,8},{1,17},{9,25},{17,1},{25,9},{2,18},{10... | collective-permute-start | bytes 2359304 | tf_op jit(solution)/shard_map/ppermute | solution.py:572
  490.1 27.9 %collective-permute-start.64 = (bf16[384,768]{1,0:T(8,128)(2,1)}, bf16[384,768]{1,0:T(8,128)(2,1)}, u32[]{:S(2)}, u32[]{:S(2)}) collective-permute-start(bf16[384,768]{1,0:T(8,128)(2,1)} %slice.1004), channel_id=1, source_target_pairs={{0,2},{1,3},{2,0},{3,1},{4,6},{5,7},{6,4},{7,5},{8,10},{9,11},{10,... | collective-permute-start | bytes 1769480 | tf_op jit(solution)/shard_map/ppermute | solution.py:572
  493.9 40.7 %collective-permute-start.63 = (bf16[192,768]{1,0:T(8,128)(2,1)}, bf16[192,768]{1,0:T(8,128)(2,1)}, u32[]{:S(2)}, u32[]{:S(2)}) collective-permute-start(bf16[192,768]{1,0:T(8,128)(2,1)} %slice.1011), channel_id=1, source_target_pairs={{0,4},{1,5},{2,6},{3,7},{4,0},{5,1},{6,2},{7,3},{8,12},{9,13},{10,... | collective-permute-start | bytes 884744 | tf_op jit(solution)/shard_map/ppermute | solution.py:572
  517.9 23.7 %collective-permute-start.68 = (bf16[768,256]{0,1:T(8,128)(2,1)}, bf16[768,256]{0,1:T(8,128)(2,1)}, u32[]{:S(2)}, u32[]{:S(2)}) collective-permute-start(bf16[768,256]{0,1:T(8,128)(2,1)} %pad_maximum_fusion.33), channel_id=1, source_target_pairs={{0,1},{1,0},{2,3},{3,2},{4,5},{5,4},{6,7},{7,6},{8,9},{9,8},{10,11... | collective-permute-start | bytes 1179656 | tf_op jit(solution)/shard_map/ppermute | solution.py:572
  531.2 35.8 %collective-permute-start.55 = (bf16[512,1536]{1,0:T(8,128)(2,1)}, bf16[512,1536]{1,0:T(8,128)(2,1)}, u32[]{:S(2)}, u32[]{:S(2)}) collective-permute-start(bf16[512,1536]{1,0:T(8,128)(2,1)} %pad_maximum_fusion.11), channel_id=1, source_target_pairs={{0,8},{8,0},{16,24},{24,16},{1,9},{9,1},{17,25},{25,17},{2,10},{10... | collective-permute-start | bytes 4718600 | tf_op jit(solution)/shard_map/ppermute | solution.py:572
  (193 other events, 3178.5 us)
Sparse Core Ops, SparseCore 0:
  486.2 40.9 all-gather.2
